TPU v7x, 32 devices: a whole 2x2x4 slice. The times are simulated.
32 devices in a mesh: parts: 1, head: 32 (over z, y, x, core).
Axes of the slice: x: 2, y: 2, z: 4, core: 2. Of those that a mesh axis runs over, the one named last changes fastest.
Arguments:
- queries: bfloat16 [8, 2048, 2048], P('parts', 'head'), may hold values from -6 to 6
- keys: bfloat16 [8, 2048, 2048], P('parts', 'head'), may hold values from -6 to 6
- values: bfloat16 [8, 2048, 2048], P('parts', 'head'), may hold values from -6 to 6
- slot_positions: int32 [8, 2048], P('parts', 'head'), may hold values from 0 to 2047, each once within a row
- counts: int32 [8], P('parts'), may hold values from 16 to 2048, as said below
- timesteps: int32 [8], P('parts'), may hold values from 0 to 999
- labels: int32 [8], P('parts'), may hold values from 0 to 127
- time_weight: bfloat16 [256, 4096], replicated, may hold values from -0.375 to 0.375
- norm_gain: float32 [2048], replicated, may hold values from 0.25 to 1.75
- gate_weight: bfloat16 [2048, 8192], P(None, 'head'), may hold values from -0.125 to 0.125
- up_weight: bfloat16 [2048, 8192], P(None, 'head'), may hold values from -0.125 to 0.125
- down_weight: bfloat16 [8192, 2048], P('head'), may hold values from -0.0625 to 0.0625
- class_weight: bfloat16 [2048, 128], replicated, may hold values from -3 to 3
- class_bias: float32 [128], replicated, may hold values from -5 to 112
Outputs:
- attention: bfloat16 [256, 2048, 64], P(('parts', 'head'))
- guidance: float32 [8, 128, 2048], P('parts', 'head')
Inputs may be any that keep to these rules, and one draw needn't show every extreme that they name: `counts`: multiples of 16; in every part one shower has exactly 2048. `slot_positions`: each shower's row is a permutation of 0 to 2047.
All inputs are finite; a program needn't handle non-finite values.
Results may differ from a plain program's by a relative error of at most 0.01.
The roundings to bfloat16 on the way count: a program that leaves them out, or rounds other values in their place, can miss the bound.
Values may be sent and summed in bfloat16 or wider, within the bound.
No kernel may reach another device: no remote copies, remote signals or barrier semaphores. Data moves between devices by JAX's collectives and lax.ppermute only.
A program may use at most 192 MiB of HBM per device.

v0:
```python
import math

import jax
import jax.numpy as jnp
from jax import lax
from jax.sharding import PartitionSpec as P

HEADS = 32
POOL = 16


epsilon = 1e-06


def sinusoid(steps, embed_width):
    half_width = embed_width // 2
    frequency = jnp.exp(-math.log(10000.0) * jnp.arange(half_width, dtype=jnp.float32) / half_width)
    angles = steps.astype(jnp.float32)[:, None] * frequency[None, :]
    return jnp.concatenate([jnp.cos(angles), jnp.sin(angles)], axis=1)


def attend_pair(pair_data):
    query_rows, key_rows, value_rows, key_valid = pair_data
    head_dim = query_rows.shape[1]
    scores = jnp.dot(query_rows, key_rows.T, preferred_element_type=jnp.float32) * head_dim ** (
        -0.5
    )
    scores = jnp.where(key_valid[None, :], scores, -jnp.inf)
    peak = jnp.max(scores, axis=1, keepdims=True)
    exponent = jnp.exp(scores - peak)
    weights = (exponent / jnp.sum(exponent, axis=1, keepdims=True)).astype(jnp.bfloat16)
    mixed = jnp.dot(weights, value_rows, preferred_element_type=jnp.float32)
    return (mixed * key_valid[:, None].astype(jnp.float32)).astype(jnp.bfloat16)


def body(
    queries,
    keys,
    values,
    slot_positions,
    counts,
    timesteps,
    labels,
    time_weight,
    norm_gain,
    gate_weight,
    up_weight,
    down_weight,
    class_weight,
    class_bias,
):
    devices = lax.axis_size("head")
    device_index = lax.axis_index("head")
    showers, local_length, model_width = queries.shape
    head_dim = model_width // HEADS
    pairs_here = showers * HEADS // devices
    windows = local_length * devices // POOL
    per_device = windows // devices
    row_total = showers * windows

    def to_pairs(block):
        return (
            block.reshape(showers, local_length, HEADS, head_dim)
            .transpose(0, 2, 1, 3)
            .reshape(devices, pairs_here, local_length, head_dim)
        )

    valid_slots = slot_positions < counts[:, None]
    slot_flags = jnp.broadcast_to(
        valid_slots.astype(jnp.bfloat16)[:, None, :], (showers, HEADS, local_length)
    ).reshape(devices, pairs_here, local_length)
    query_rows = lax.all_to_all(to_pairs(queries), "head", split_axis=0, concat_axis=2, tiled=True)
    key_rows = lax.all_to_all(to_pairs(keys), "head", split_axis=0, concat_axis=2, tiled=True)
    value_rows = lax.all_to_all(to_pairs(values), "head", split_axis=0, concat_axis=2, tiled=True)
    flag_rows = lax.all_to_all(slot_flags, "head", split_axis=0, concat_axis=2, tiled=True)
    pair_count = query_rows.shape[1]
    flag_rows = flag_rows[0]
    attention_part = lax.map(
        attend_pair, (query_rows[0], key_rows[0], value_rows[0], flag_rows > 0.5)
    )
    flag_values = flag_rows.astype(jnp.float32)
    window_count = jnp.sum(flag_values.reshape(pair_count, windows, POOL), axis=2)
    window_sum = jnp.sum(
        attention_part.astype(jnp.float32).reshape(pair_count, windows, POOL, head_dim), axis=2
    )
    pooled_part = (window_sum / jnp.maximum(window_count, 1.0)[:, :, None]).astype(jnp.bfloat16)
    attention, pooled, window_count = (
        attention_part,
        pooled_part,
        window_count.astype(jnp.bfloat16),
    )
    pooled_all, count_all = (
        lax.all_gather(pooled, "head", axis=0, tiled=True),
        lax.all_gather(window_count, "head", axis=0, tiled=True),
    )
    pooled_rows = (
        pooled_all.reshape(showers, HEADS, devices, per_device, head_dim)
        .transpose(2, 0, 3, 1, 4)
        .reshape(devices, showers, per_device, model_width)
        .astype(jnp.float32)
    )
    row_count = (
        count_all.reshape(showers, HEADS, devices, per_device)[:, 0]
        .transpose(1, 0, 2)
        .astype(jnp.float32)
    )
    embedding = sinusoid(timesteps, time_weight.shape[0]).astype(jnp.bfloat16)
    modulation = jnp.dot(embedding, time_weight, preferred_element_type=jnp.float32)
    shifts = modulation[:, None, :model_width]
    scales = 1.0 + modulation[:, None, model_width:]
    inverse_rms = lax.rsqrt(jnp.mean(pooled_rows * pooled_rows, axis=3, keepdims=True) + epsilon)
    unit_rows = pooled_rows * inverse_rms
    normed = (
        (unit_rows * norm_gain * scales[None] + shifts[None])
        .astype(jnp.bfloat16)
        .reshape(row_total, model_width)
    )
    own_pooled = lax.dynamic_slice_in_dim(pooled_rows, device_index, 1, 0)[0]
    own_count = lax.dynamic_slice_in_dim(row_count, device_index, 1, 0)[0]
    own_units = lax.dynamic_slice_in_dim(unit_rows, device_index, 1, 0)[0]
    own_inverse = lax.dynamic_slice_in_dim(inverse_rms, device_index, 1, 0)[0]
    shower_counts = counts.astype(jnp.float32)
    class_matrix = class_weight.astype(jnp.float32)
    target = (
        labels[:, None] == jnp.arange(class_matrix.shape[1], dtype=jnp.int32)[None, :]
    ).astype(jnp.float32)
    gate_out = jnp.dot(normed, gate_weight, preferred_element_type=jnp.float32)
    up_out = jnp.dot(normed, up_weight, preferred_element_type=jnp.float32)
    activated = jax.nn.silu(gate_out)
    hidden = (activated * up_out).astype(jnp.bfloat16)
    own_mlp = lax.psum_scatter(
        jnp.dot(hidden, down_weight, preferred_element_type=jnp.float32),
        "head",
        scatter_dimension=0,
        tiled=True,
    ).reshape(showers, per_device, model_width)
    partial_value = jnp.sum(own_count[:, :, None] * (own_pooled + own_mlp), axis=1)
    features = lax.psum(partial_value, "head") / shower_counts[:, None]
    logits = jnp.dot(features, class_matrix, precision=lax.Precision.HIGHEST) + class_bias
    exponent = jnp.exp(logits - jnp.max(logits, axis=1, keepdims=True))
    probability = exponent / jnp.sum(exponent, axis=1, keepdims=True)
    feature_grad = jnp.dot(target - probability, class_matrix.T, precision=lax.Precision.HIGHEST)
    row_grads = (
        row_count[:, :, :, None]
        / shower_counts[None, :, None, None]
        * feature_grad[None, :, None, :]
    )
    hidden_grad = jnp.dot(
        row_grads.astype(jnp.bfloat16).reshape(row_total, model_width),
        down_weight.T,
        preferred_element_type=jnp.float32,
    )
    sigmoid_gate = jax.nn.sigmoid(gate_out)
    gate_grad = (
        hidden_grad * up_out * sigmoid_gate * (1.0 + gate_out * (1.0 - sigmoid_gate))
    ).astype(jnp.bfloat16)
    up_grad = (hidden_grad * activated).astype(jnp.bfloat16)
    normed_grad = lax.psum_scatter(
        jnp.dot(gate_grad, gate_weight.T, preferred_element_type=jnp.float32)
        + jnp.dot(up_grad, up_weight.T, preferred_element_type=jnp.float32),
        "head",
        scatter_dimension=0,
        tiled=True,
    ).reshape(showers, per_device, model_width)
    own_row_grads = lax.dynamic_slice_in_dim(row_grads, device_index, 1, 0)[0]
    unit_grad = normed_grad * norm_gain * scales
    pooled_grad = own_inverse * (
        unit_grad - own_units * jnp.mean(unit_grad * own_units, axis=2, keepdims=True)
    )
    guidance = windows * (own_row_grads + pooled_grad)
    return (attention, guidance)


def solution(mesh):
    in_specs = (
        P("parts", "head", None),
        P("parts", "head", None),
        P("parts", "head", None),
        P("parts", "head"),
        P("parts"),
        P("parts"),
        P("parts"),
        P(),
        P(),
        P(None, "head"),
        P(None, "head"),
        P("head", None),
        P(),
        P(),
    )
    out_specs = (P(("parts", "head"), None, None), P("parts", "head", None))
    return jax.shard_map(body, mesh=mesh, in_specs=in_specs, out_specs=out_specs, check_vma=False)
```

profile of v0, /device:TPU:0, one launch (start us, length us, event | category | flops | bytes accessed | tf_op | source)
XLA Modules:
  0.0 924.3 jit_solution(15136962674087946436)
XLA Ops:
  8.8 7.3 all-to-all-start
  16.1 7.1 reshape.154
  29.0 7.9 reshape.178
  42.9 7.1 reshape.156
  55.7 7.9 reshape.180
  63.6 28.2 %all-to-all-done.1 = bf16[32,2,16384]{2,1,0:T(2,128)(2,1)} async-done(((bf16[32,2,16384]{2,1,0:T(2,128)(2,1)}), bf16[32,2,16384]{2,1,0:T(2,128)(2,1)}, u32[]{:S(2)}, u32[]{:S(2)}) %all-to-all-start.1) | async-done | bytes 2097184 | tf_op jit(solution)/shard_map/all_to_all | solution.py:72
  96.4 7.1 reshape.158
  109.2 7.9 reshape.182
  117.1 28.2 %all-to-all-done.2 = bf16[32,2,16384]{2,1,0:T(2,128)(2,1)} async-done(((bf16[32,2,16384]{2,1,0:T(2,128)(2,1)}), bf16[32,2,16384]{2,1,0:T(2,128)(2,1)}, u32[]{:S(2)}, u32[]{:S(2)}) %all-to-all-start.2) | async-done | bytes 2097184 | tf_op jit(solution)/shard_map/all_to_all | solution.py:73
  150.8 7.9 reshape.179
  164.2 7.9 reshape.181
  177.7 20.6 %all-to-all-done.3 = bf16[32,2,16384]{2,1,0:T(2,128)(2,1)} async-done(((bf16[32,2,16384]{2,1,0:T(2,128)(2,1)}), bf16[32,2,16384]{2,1,0:T(2,128)(2,1)}, u32[]{:S(2)}, u32[]{:S(2)}) %all-to-all-start.3) | async-done | bytes 2097184 | tf_op jit(solution)/shard_map/all_to_all | solution.py:74
  198.3 7.9 reshape.183
  211.7 119.1 %while.10 = (s32[]{:T(128)}, bf16[8,2048,64]{1,2,0:T(8,128)(2,1)}, pred[8,2048]{1,0:T(8,128)(4,1)S(1)}, bf16[8,2048,64]{2,1,0:T(8,128)(2,1)}, bf16[8,2048,64]{2,...) while((s32[]{:T(128)}, bf16[8,2048,64]{1,2,0:T(8,128)(2,1)}, pred[8,2048]{1,0:T(8,128)(4,1)S(1)}, ...), condition=%wide.region_3.4_spmd, body=%wide.region_0.3_spmd.sunk | while | flops 1124333568 | bytes 52238416 | solution.py:78
  250.5 6.0 fusion.77
  265.4 6.0 fusion.77
  280.2 6.0 fusion.77
  295.1 6.0 fusion.77
  310.0 6.0 fusion.77
  349.0 10.2 %mul.175 = f32[1024,2048]{1,0:T(8,128)} reshape(f32[32,8,4,2048]{3,2,1,0:T(4,128)} %mul.174) | data formatting | bytes 16777216 | tf_op jit(solution)/shard_map/mul | solution.py:114
  364.6 10.0 %add.83 = f32[1024,2048]{1,0:T(8,128)} reshape(f32[32,8,4,2048]{3,2,1,0:T(4,128)} %add.82) | data formatting | bytes 16777216 | tf_op jit(solution)/shard_map/add | solution.py:114
  374.6 30.1 %all-gather.2.cloned.1.call-done = bf16[256,128,64]{1,2,0:T(8,128)(2,1)} async-done(((bf16[8,128,64]{1,2,0:T(8,128)(2,1)}), bf16[256,128,64]{1,2,0:T(8,128)(2,1)}) %all-gather.2.cloned.1.call-update) | async-done | bytes 4194320 | tf_op jit(solution)/shard_map/all_gather | solution.py:93
  410.3 12.7 %copy.135 = f32[256,128,64]{2,0,1:T(8,128)} copy(bf16[256,128,64]{1,2,0:T(8,128)(2,1)} %all-gather.2.cloned.1.call-done) | data formatting | bytes 12582912 | tf_op jit(solution)/shard_map/convert_element_type | solution.py:100
  423.0 11.9 %copy.137 = f32[32,8,4,32,64]{4,3,2,1,0:T(8,128)} copy(f32[32,8,4,32,64]{4,3,1,2,0:T(8,128)} %bitcast.115) | data formatting | bytes 16777216 | tf_op jit(solution)/shard_map/convert_element_type | solution.py:100
  434.9 14.8 %reshape.169 = f32[1024,2048]{1,0:T(8,128)} reshape(f32[32,8,4,32,64]{4,3,2,1,0:T(8,128)} %copy.137) | data formatting | bytes 16777216 | tf_op jit(solution)/shard_map/convert_element_type | solution.py:100
  449.7 10.5 %add_convert_fusion = bf16[1024,2048]{1,0:T(8,128)(2,1)S(1)} fusion(f32[1024,2048]{1,0:T(8,128)} %add.83, f32[1024,2048]{1,0:T(8,128)} %mul.175, f32[1024,2048]{1,0:T(8,128)} %reshape.169, f32[2048]{0:T(1024)S(1)} %copy-done.8, f32[1024]{0:T(1024)S(1)} %rsqrt.18), kind=kLoop, calls=%fused_computation.24 | loop fusion | flops 10485760 | bytes 29372416 | tf_op jit(solution)/shard_map/convert_element_type | solution.py:115
  468.4 39.5 %all_gather.6 = bf16[256,128]{1,0:T(8,128)(2,1)S(1)} all-gather(bf16[8,128]{1,0:T(8,128)(2,1)S(1)} %copy-done.10), channel_id=1, replica_groups=mesh['parts'=1,'head'=32] {'head'}, dimensions={0}, use_global_device_ids=true | all-gather | bytes 67584 | tf_op jit(solution)/shard_map/all_gather | solution.py:94
  513.4 14.9 %reshape.168 = f32[32,8,4,2048]{3,1,2,0:T(8,128)} reshape(f32[32,8,4,32,64]{4,3,1,2,0:T(8,128)} %bitcast.116) | data formatting | bytes 16777216 | tf_op jit(solution)/shard_map/convert_element_type | solution.py:100
  529.9 85.8 %reduce-scatter.3.cloned.1.call-done = f32[32,2048]{1,0:T(8,128)} async-done(((f32[1024,2048]{1,0:T(8,128)}), f32[32,2048]{1,0:T(8,128)}) %reduce-scatter.3.cloned.1.call-update) | async-done | bytes 262160 | tf_op jit(solution)/shard_map/reduce_scatter | solution.py:131
  622.1 112.7 %all-reduce.2.cloned.1.call-done = f32[8,2048]{1,0:T(8,128)} async-done(((f32[8,2048]{1,0:T(8,128)}), f32[8,2048]{1,0:T(8,128)}) %all-reduce.2.cloned.1.call-update) | async-done | bytes 65552 | tf_op jit(solution)/shard_map/psum | solution.py:138
  743.5 10.3 %mul.186 = f32[1024,2048]{1,0:T(8,128)} reshape(f32[32,8,4,2048]{3,2,1,0:T(4,128)} %mul.180) | data formatting | bytes 16777216 | tf_op jit(solution)/shard_map/mul | solution.py:144
  766.5 148.4 %reduce-scatter.5.cloned.1.call-done = f32[32,2048]{1,0:T(8,128)} async-done(((f32[1024,2048]{1,0:T(8,128)}), f32[32,2048]{1,0:T(8,128)}) %reduce-scatter.5.cloned.1.call-update) | async-done | bytes 262160 | tf_op jit(solution)/shard_map/reduce_scatter | solution.py:158
  (142 shorter events, 214.5 us)
Async XLA Ops:
  7.2 336.1 %copy-start = (bf16[256,4096]{1,0:T(8,128)(2,1)S(1)}, bf16[256,4096]{1,0:T(8,128)(2,1)}, u32[]{:S(2)}) copy-start(bf16[256,4096]{1,0:T(8,128)(2,1)} %param.23) | copy-start | bytes 6291460
  8.8 28.0 %all-to-all-start = ((bf16[32,2,256]{2,1,0:T(2,128)(2,1)}), bf16[32,2,256]{2,1,0:T(2,128)(2,1)S(1)}, u32[]{:S(2)}, u32[]{:S(2)}) async-start(bf16[32,2,256]{2,1,0:T(2,128)(2,1)} %reshape.176), calls=%async_computation | async-start | bytes 65536 | tf_op jit(solution)/shard_map/all_to_all | solution.py:75
  36.9 54.8 %all-to-all-start.1 = ((bf16[32,2,16384]{2,1,0:T(2,128)(2,1)}), bf16[32,2,16384]{2,1,0:T(2,128)(2,1)}, u32[]{:S(2)}, u32[]{:S(2)}) async-start(bf16[32,2,16384]{2,1,0:T(2,128)(2,1)} %reshape.178), calls=%async_computation.1 | async-start | bytes 4194304 | tf_op jit(solution)/shard_map/all_to_all | solution.py:72
  91.7 53.5 %all-to-all-start.2 = ((bf16[32,2,16384]{2,1,0:T(2,128)(2,1)}), bf16[32,2,16384]{2,1,0:T(2,128)(2,1)}, u32[]{:S(2)}, u32[]{:S(2)}) async-start(bf16[32,2,16384]{2,1,0:T(2,128)(2,1)} %reshape.180), calls=%async_computation.2 | async-start | bytes 4194304 | tf_op jit(solution)/shard_map/all_to_all | solution.py:73
  145.3 53.0 %all-to-all-start.3 = ((bf16[32,2,16384]{2,1,0:T(2,128)(2,1)}), bf16[32,2,16384]{2,1,0:T(2,128)(2,1)}, u32[]{:S(2)}, u32[]{:S(2)}) async-start(bf16[32,2,16384]{2,1,0:T(2,128)(2,1)} %reshape.182), calls=%async_computation.3 | async-start | bytes 4194304 | tf_op jit(solution)/shard_map/all_to_all | solution.py:74
  149.4 255.3 %all-gather.2.cloned.1.call-start = ((), (), s32[]{:S(2)}) async-start(), calls=%async_computation.6 | async-start | bytes 4325376 | tf_op jit(solution)/shard_map/all_gather | solution.py:93
  330.9 11.2 %copy-start.9 = (f32[8,128]{1,0:T(8,128)S(1)}, f32[8,128]{1,0:T(8,128)}, u32[]{:S(2)}) copy-start(f32[8,128]{1,0:T(8,128)} %get-tuple-element.86) | copy-start | bytes 12292
  330.9 12.3 %copy-start.12 = (s32[8]{0:T(128)S(1)}, s32[8]{0:T(128)}, u32[]{:S(2)}) copy-start(s32[8]{0:T(128)} %param.21) | copy-start | bytes 100
  343.1 272.7 %reduce-scatter.3.cloned.1.call-start = ((), (), s32[]{:S(2)}) async-start(), calls=%async_computation.7 | async-start | bytes 8650752 | tf_op jit(solution)/shard_map/reduce_scatter | solution.py:131
  434.9 14.8 %copy-start.8 = (f32[2048]{0:T(1024)S(1)}, f32[2048]{0:T(1024)}, u32[]{:S(2)}) copy-start(f32[2048]{0:T(1024)} %param.24) | copy-start | bytes 24580
  449.7 10.5 %copy-start.4 = (bf16[2048,256]{1,0:T(8,128)(2,1)S(1)}, bf16[2048,256]{1,0:T(8,128)(2,1)}, u32[]{:S(2)}) copy-start(bf16[2048,256]{1,0:T(8,128)(2,1)} %param.25) | copy-start | bytes 3145732
  449.7 11.8 %copy-start.6 = (bf16[2048,256]{1,0:T(8,128)(2,1)S(1)}, bf16[2048,256]{1,0:T(8,128)(2,1)}, u32[]{:S(2)}) copy-start(bf16[2048,256]{1,0:T(8,128)(2,1)} %param.26) | copy-start | bytes 3145732
  460.2 3.5 copy-start.3
  462.7 1.0 copy-start.1
  463.7 4.6 copy-start.11
  463.7 4.6 copy-start.10
  468.3 266.6 %all-reduce.2.cloned.1.call-start = ((), (), s32[]{:S(2)}) async-start(), calls=%async_computation.8 | async-start | bytes 131072 | tf_op jit(solution)/shard_map/psum | solution.py:138
  619.5 295.4 %reduce-scatter.5.cloned.1.call-start = ((), (), s32[]{:S(2)}) async-start(), calls=%async_computation.9 | async-start | bytes 8650752 | tf_op jit(solution)/shard_map/reduce_scatter | solution.py:158
  753.8 5.1 copy-start.2
  753.8 5.1 copy-start.5
  758.9 1.5 copy-start.7
Sparse Core Ops, SparseCore 0:
  343.2 61.4 all-gather.1
  468.4 147.3 reduce-scatter.2
  621.4 113.4 all-reduce.1
  765.2 149.6 reduce-scatter.4
where the time goes:
time: 935 us; the launch traced here: 924 us
  waiting for transfers between devices  454 us (49%)
  local copies, waits for them, and re-layouts  224 us (24%)
  matrix products  99.8 us (11%)
  other arithmetic  70.2 us (8%)
  blocking collectives  39.5 us (4%)
  starting transfers between devices  22.2 us (2%)
  between operations  14.6 us (2%)
    reduce_scatter x1, waiting for transfers between devices, body(): lax.psum_scatter(jnp.dot(gate_grad, gate_weight.T, preferred_element_type...  148 us
    psum x1, waiting for transfers between devices, body(): features = lax.psum(partial_value, 'head') / shower_counts[:, None]  113 us
    reduce_scatter x1, waiting for transfers between devices, body(): lax.psum_scatter(jnp.dot(hidden, down_weight, preferred_element_type=jnp....  85.8 us
    convert_element_type x4, local copies, waits for them, and re-layouts, body(): pooled_rows = pooled_all.reshape(showers, HEADS, devices, per_device, hea...  54.3 us
    unnamed x34, local copies, waits for them, and re-layouts  49.3 us
    dot_general x8, matrix products, attend_pair(): mixed = jnp.dot(weights, value_rows, preferred_element_type=jnp.float32)  48.2 us
    reduce_sum x8, other arithmetic, attend_pair(): jnp.sum(exponent, axis=1, keepdims=True)  40.4 us
    all_gather x1, blocking collectives, body(): lax.all_gather(window_count, 'head', axis=0, tiled=True)  39.5 us
  transfers between devices with their start and end apart: 8, of which 7 were waited for; matrix products, arithmetic and copies ran while one was open for 16% of the time, Pallas kernels for 0%

commit v1 on v0

v1 whole, which is shorter than its diff:
```python
import functools
import math

import jax
import jax.numpy as jnp
import numpy as np
from jax import lax
from jax.experimental import pallas as pl
from jax.experimental.pallas import tpu as pltpu
from jax.sharding import PartitionSpec as P

HEADS = 32
POOL = 16
LANES = 128
MASKED = -1e30
epsilon = 1e-06
HIGH = lax.Precision.HIGHEST
NT = (((1,), (1,)), ((), ()))
NN = (((1,), (0,)), ((), ()))
MIB = 1 << 20


def mm(a, b, dims=NN, precision=None):
    return lax.dot_general(a, b, dims, precision=precision, preferred_element_type=jnp.float32)


def sinusoid(steps, embed_width):
    half_width = embed_width // 2
    frequency = jnp.exp(-math.log(10000.0) * jnp.arange(half_width, dtype=jnp.float32) / half_width)
    angles = steps.astype(jnp.float32)[:, None] * frequency[None, :]
    return jnp.concatenate([jnp.cos(angles), jnp.sin(angles)], axis=1)


def attend_kernel(block, q_ref, k_ref, v_ref, valid_ref, pool_ref, cnt_ref, *rest):
    att_ref, pooled_ref = rest[-2:]
    length = q_ref.shape[0]
    half = LANES // 2
    lane = lax.broadcasted_iota(jnp.int32, (1, LANES), 1)
    low = lane < half
    valid = valid_ref[...]
    bias = jnp.where(valid > 0.5, 0.0, MASKED)
    keys = k_ref[...]
    rows = v_ref[...]
    one = jnp.ones_like(rows)
    values = (jnp.where(low, rows, one), jnp.where(low, one, rows))

    def step(i, carry):
        at = pl.ds(pl.multiple_of(i * block, block), block)
        query = q_ref[at, :] * jnp.asarray(0.125, jnp.bfloat16)
        zero = jnp.zeros_like(query)
        outs = []
        for h in range(2):
            own = jnp.where(low, query, zero) if h == 0 else jnp.where(low, zero, query)
            scores = mm(own, keys, NT) + bias
            peak = jnp.max(scores, axis=1, keepdims=True)
            weights = jnp.exp(scores - peak).astype(jnp.bfloat16)
            outs.append(mm(weights, values[h]))
        top = jnp.where(low, outs[0], outs[1])
        total = jnp.where(low, pltpu.roll(outs[0], half, 1), pltpu.roll(outs[1], half, 1))
        mixed = ((top / total).T * valid_ref[:, at]).astype(jnp.bfloat16)
        att_ref[0, :, at] = mixed[:half]
        att_ref[1, :, at] = mixed[half:]
        return carry

    lax.fori_loop(0, length // block, step, 0)
    both = jnp.concatenate([att_ref[0], att_ref[1]], axis=0)
    pooled_ref[...] = (mm(pool_ref[...], both, NT) / cnt_ref[...]).astype(jnp.bfloat16)


def attend(qkv, valid, pool, cnt, first, count, pairs, before):
    length = qkv.shape[0]
    windows = pool.shape[0]
    head_dim = LANES // 2

    def part(which):
        return pl.BlockSpec((length, LANES), lambda j: (0, which * count + j))

    def whole(shape):
        return pl.BlockSpec(shape, lambda j: (0, 0))

    in_specs = [
        part(0),
        part(1),
        part(2),
        whole((1, length)),
        whole((windows, length)),
        whole((windows, LANES)),
    ]
    operands = [qkv, qkv, qkv, valid, pool, cnt]
    aliases = {}
    if before is not None:
        in_specs.append(pl.BlockSpec(memory_space=pl.ANY))
        operands.append(before)
        aliases = {6: 0}
    return pl.pallas_call(
        functools.partial(attend_kernel, min(512, length)),
        grid=(count,),
        out_shape=(
            jax.ShapeDtypeStruct((pairs, head_dim, length), jnp.bfloat16),
            jax.ShapeDtypeStruct((windows, count * LANES), jnp.bfloat16),
        ),
        in_specs=in_specs,
        out_specs=(
            pl.BlockSpec((2, head_dim, length), lambda j: (first + j, 0, 0)),
            pl.BlockSpec((windows, LANES), lambda j: (0, j)),
        ),
        input_output_aliases=aliases,
        compiler_params=pltpu.CompilerParams(vmem_limit_bytes=40 * MIB),
        cost_estimate=pl.CostEstimate(
            flops=count * 2 * 4 * length * length * head_dim,
            bytes_accessed=count * length * LANES * 8,
            transcendentals=count * 2 * length * length,
        ),
        name="attend",
    )(*operands)


def forward_kernel(
    lanes, own_ref, *refs
):
    n = len(lanes)
    x_refs, refs = refs[:n], refs[n:]
    (
        perm_ref, gain_ref, scale_ref, shift_ref, gate_ref, up_ref, dc_ref, cnt_ref, own_cnt_ref,
        coef_ref, class_ref, logits_ref, ga_ref, aa_ref, own_x_ref, gathered, normed,
    ) = refs
    step = pl.program_id(0)
    showers = logits_ref.shape[0]
    group = x_refs[0].shape[0] // showers
    rows = x_refs[0].shape[1]
    width = gain_ref.shape[1]
    block = own_x_ref.shape[0]
    total = rows * showers

    @pl.when(step == 0)
    def _():
        for s in range(showers):
            for m in range(group):
                at = m * (width // group)
                for ref, size in zip(x_refs, lanes):
                    gathered[s * rows : (s + 1) * rows, at : at + size] = ref[s * group + m].astype(
                        jnp.float32
                    )
                    at += size
        packed = gathered[...].astype(jnp.bfloat16)
        gathered[...] = mm(perm_ref[...], packed)
        for b in range(total // block):
            at = slice(b * block, (b + 1) * block)
            x = gathered[at]
            inverse = lax.rsqrt(jnp.mean(x * x, axis=1, keepdims=True) + epsilon)
            normed[at] = (x * inverse * gain_ref[...] * scale_ref[...] + shift_ref[...]).astype(
                jnp.bfloat16
            )
        own_x_ref[...] = gathered[pl.ds(pl.multiple_of(own_ref[0] * block, block), block), :]
        sums = mm(own_cnt_ref[...], gathered[...].astype(jnp.bfloat16))
        logits_ref[...] = mm(sums, class_ref[...].astype(jnp.float32), precision=HIGH)

    gate = mm(normed[...], gate_ref[0])
    up = mm(normed[...], up_ref[0])
    sigma = jax.nn.sigmoid(gate)
    activated = gate * sigma
    hidden = (activated * up).astype(jnp.bfloat16)
    logits_ref[...] += mm(mm(cnt_ref[...], hidden), dc_ref[0], precision=HIGH)
    coef = coef_ref[...][:, :1]
    ga_ref[0] = coef * (up * sigma * (1.0 + gate * (1.0 - sigma)))
    aa_ref[0] = coef * activated


def backward_kernel(
    parts_ref, counts_ref, bias_ref, target_ref, spread_ref, gate_ref, up_ref, dc_ref, ga_ref, aa_ref,
    dn_ref, miss_ref, total,
):
    step = pl.program_id(0)
    blocks, block, _ = dn_ref.shape

    @pl.when(step == 0)
    def _():
        logits = jnp.sum(parts_ref[...], axis=0) / counts_ref[...] + bias_ref[...]
        exponent = jnp.exp(logits - jnp.max(logits, axis=1, keepdims=True))
        miss_ref[...] = target_ref[...] - exponent / jnp.sum(exponent, axis=1, keepdims=True)

    wide = mm(mm(spread_ref[...], miss_ref[...], precision=HIGH), dc_ref[0], NT, HIGH)
    wide = jnp.concatenate([wide] * blocks, axis=0)
    gate_grad = (wide * ga_ref[0]).astype(jnp.bfloat16)
    up_grad = (wide * aa_ref[0]).astype(jnp.bfloat16)
    term = mm(gate_grad, gate_ref[0], NT) + mm(up_grad, up_ref[0], NT)

    @pl.when(step == 0)
    def _():
        total[...] = term

    @pl.when(step > 0)
    def _():
        total[...] += term

    @pl.when(step == pl.num_programs(0) - 1)
    def _():
        for b in range(blocks):
            dn_ref[b] = total[b * block : (b + 1) * block].astype(jnp.bfloat16)


def final_kernel(windows, dn_ref, x_ref, gain_ref, scale_ref, dy_ref, out_ref):
    total = dn_ref[0].astype(jnp.float32)
    for b in range(1, dn_ref.shape[0]):
        total = total + dn_ref[b].astype(jnp.float32)
    x = x_ref[...]
    inverse = lax.rsqrt(jnp.mean(x * x, axis=1, keepdims=True) + epsilon)
    unit = x * inverse
    grad = total * gain_ref[...] * scale_ref[...]
    back = inverse * (grad - unit * jnp.mean(grad * unit, axis=1, keepdims=True))
    value = windows * (dy_ref[...] + back)
    each = out_ref.shape[1]
    for s in range(out_ref.shape[0]):
        out_ref[s] = value[s * each : (s + 1) * each]


def body(
    queries,
    keys,
    values,
    slot_positions,
    counts,
    timesteps,
    labels,
    time_weight,
    norm_gain,
    gate_weight,
    up_weight,
    down_weight,
    class_weight,
    class_bias,
):
    devices = lax.axis_size("head")
    me = lax.axis_index("head")
    showers, local, width = queries.shape
    length = local * devices
    group = devices // showers
    outer = devices // group
    features = width // group
    slabs = features // LANES
    each = local // POOL
    windows = length // POOL
    classes = class_weight.shape[1]
    owned = me // group
    rows = outer * each
    block = showers * each
    total = showers * rows

    def swap(x, bit):
        return lax.ppermute(x, "head", [(d, d ^ bit) for d in range(devices)])

    chunks = [(0, slabs - 1), (slabs - 1, 1)] if slabs > 1 else [(0, 1)]

    def outgoing(x, first, count):
        x = x.reshape(showers, local, group, features)[
            ..., first * LANES : (first + count) * LANES
        ]
        return x.transpose(0, 2, 1, 3).reshape(devices, local, count * LANES)

    received = []
    for first, count in chunks:
        sent = jnp.concatenate([outgoing(x, first, count) for x in (queries, keys, values)], axis=2)
        got = lax.all_to_all(sent, "head", 0, 0, tiled=True)
        received.append(got.reshape(length, 3 * count * LANES))

    flags = (slot_positions < counts[:, None]).astype(jnp.bfloat16)
    flags = jnp.where(
        jnp.arange(devices)[:, None, None] == me, flags[None], jnp.zeros((), jnp.bfloat16)
    )
    bit = 1
    while bit < devices:
        flags = flags + swap(flags, bit)
        bit *= 2
    flags = flags.astype(jnp.float32)
    cnt = jnp.sum(flags.reshape(devices, showers, each, POOL), axis=3)
    own_flags = lax.dynamic_index_in_dim(flags, owned, 1, False).reshape(1, length)

    order = np.arange(windows).reshape(outer, group, each).transpose(1, 0, 2).reshape(windows)
    pool = jnp.asarray(order, jnp.int32)[:, None] == jnp.arange(length, dtype=jnp.int32)[None] // POOL
    pool = pool.astype(jnp.bfloat16)
    own_cnt = lax.dynamic_index_in_dim(cnt, owned, 1, False)
    own_cnt = own_cnt.reshape(outer, group, each).transpose(1, 0, 2).reshape(windows, 1)
    own_cnt = jnp.broadcast_to(jnp.maximum(own_cnt, 1.0), (windows, LANES))

    def gather(x):
        x = x[None]
        bit = 1
        while bit < group:
            x = jnp.concatenate([x, swap(x, bit)], axis=0)
            bit *= 2
        return x

    gates = gather(gate_weight)
    ups = gather(up_weight)
    class_map = gather(jnp.dot(down_weight, class_weight, preferred_element_type=jnp.float32))

    shower_counts = counts.astype(jnp.float32)
    mine = lax.dynamic_index_in_dim(
        cnt.reshape(outer, group, showers, each), me % group, 1, False
    )
    coef = (mine / shower_counts[None, :, None]).reshape(total, 1)
    coef = jnp.broadcast_to(coef, (total, LANES))
    row_shower = np.tile(np.repeat(np.arange(showers), each), outer)
    row_outer = np.repeat(np.arange(outer), block)
    cnt_rows = jnp.where(
        jnp.arange(showers)[:, None] == jnp.asarray(row_shower)[None], mine.reshape(1, total), 0.0
    )
    own_cnt_rows = jnp.where(jnp.asarray(row_outer)[None] == owned, cnt_rows, 0.0)
    source = np.arange(total).reshape(showers, outer, each).transpose(1, 0, 2).reshape(total)
    perm = jnp.asarray(source, jnp.int32)[:, None] == jnp.arange(total, dtype=jnp.int32)[None]
    perm = perm.astype(jnp.bfloat16)
    embedding = sinusoid(timesteps, time_weight.shape[0]).astype(jnp.bfloat16)
    modulation = jnp.dot(embedding, time_weight, preferred_element_type=jnp.float32)
    shifts = jnp.repeat(modulation[:, :width], each, axis=0)
    scales = jnp.repeat(1.0 + modulation[:, width:], each, axis=0)
    gain = norm_gain.reshape(1, width)

    attention = None
    pooled = []
    for qkv, (first, count) in zip(received, chunks):
        attention, part = attend(
            qkv, own_flags, pool, own_cnt, first, count, 2 * slabs, attention
        )
        part = part.reshape(1, group, rows, count * LANES)
        part = jnp.broadcast_to(part, (outer,) + part.shape[1:])
        part = part.reshape(devices, rows, count * LANES)
        pooled.append(lax.all_to_all(part, "head", 0, 0, tiled=True))

    units = gate_weight.shape[1]

    def whole(x):
        return pl.BlockSpec(x.shape, lambda i: (0,) * x.ndim)

    def member(x):
        return pl.BlockSpec((1,) + x.shape[1:], lambda i: (i, 0, 0))

    side = jax.ShapeDtypeStruct((group, total, units), jnp.float32)
    side_spec = pl.BlockSpec((1, total, units), lambda i: (i, 0, 0))
    fixed = (perm, gain, scales, shifts)
    streamed = (gates, ups, class_map)
    late = (cnt_rows.astype(jnp.bfloat16), own_cnt_rows.astype(jnp.bfloat16), coef, class_weight)
    partial, gate_side, up_side, own_x = pl.pallas_call(
        functools.partial(forward_kernel, [count * LANES for _, count in chunks]),
        grid=(group,),
        out_shape=(
            jax.ShapeDtypeStruct((showers, classes), jnp.float32),
            side,
            side,
            jax.ShapeDtypeStruct((block, width), jnp.float32),
        ),
        in_specs=[pl.BlockSpec(memory_space=pltpu.SMEM)]
        + [whole(x) for x in pooled]
        + [whole(x) for x in fixed]
        + [member(x) for x in streamed]
        + [whole(x) for x in late],
        out_specs=(
            pl.BlockSpec((showers, classes), lambda i: (0, 0)),
            side_spec,
            side_spec,
            pl.BlockSpec((block, width), lambda i: (0, 0)),
        ),
        scratch_shapes=[
            pltpu.VMEM((total, width), jnp.float32),
            pltpu.VMEM((total, width), jnp.bfloat16),
        ],
        compiler_params=pltpu.CompilerParams(vmem_limit_bytes=40 * MIB),
        name="classifier_forward",
    )(owned.reshape(1).astype(jnp.int32), *pooled, *fixed, *streamed, *late)

    parts = lax.all_to_all(
        jnp.broadcast_to(partial[None], (devices,) + partial.shape), "head", 0, 0, tiled=True
    )
    target = (labels[:, None] == jnp.arange(classes, dtype=jnp.int32)[None]).astype(jnp.float32)
    spread = jnp.asarray(
        np.repeat(np.eye(showers), each, axis=0).astype(np.float32)
    )
    heads_in = (
        parts,
        jnp.broadcast_to(shower_counts[:, None], (showers, classes)),
        class_bias.reshape(1, classes),
        target,
        spread,
    )
    grads, miss = pl.pallas_call(
        backward_kernel,
        grid=(group,),
        out_shape=(
            jax.ShapeDtypeStruct((outer, block, width), jnp.bfloat16),
            jax.ShapeDtypeStruct((showers, classes), jnp.float32),
        ),
        in_specs=[whole(x) for x in heads_in]
        + [member(x) for x in streamed + (gate_side, up_side)],
        out_specs=(
            pl.BlockSpec((outer, block, width), lambda i: (0, 0, 0)),
            pl.BlockSpec((showers, classes), lambda i: (0, 0)),
        ),
        scratch_shapes=[pltpu.VMEM((total, width), jnp.float32)],
        compiler_params=pltpu.CompilerParams(vmem_limit_bytes=40 * MIB),
        name="classifier_backward",
    )(*heads_in, *streamed, gate_side, up_side)

    lines = [[o * group + m for o in range(outer)] for m in range(group)]
    grads = lax.all_to_all(grads, "head", 0, 0, axis_index_groups=lines, tiled=True)
    feature_grad = mm(miss, class_weight.astype(jnp.float32), NT, HIGH)
    here = lax.dynamic_index_in_dim(cnt, me, 0, False)
    own_row_grads = (here / shower_counts[:, None])[:, :, None] * feature_grad[:, None, :]
    own_row_grads = own_row_grads.reshape(block, width)
    guidance = pl.pallas_call(
        functools.partial(final_kernel, float(windows)),
        out_shape=jax.ShapeDtypeStruct((showers, each, width), jnp.float32),
        compiler_params=pltpu.CompilerParams(vmem_limit_bytes=40 * MIB),
        name="norm_backward",
    )(grads, own_x, gain, scales, own_row_grads)
    return (attention.transpose(0, 2, 1), guidance)


def solution(mesh):
    in_specs = (
        P("parts", "head", None),
        P("parts", "head", None),
        P("parts", "head", None),
        P("parts", "head"),
        P("parts"),
        P("parts"),
        P("parts"),
        P(),
        P(),
        P(None, "head"),
        P(None, "head"),
        P("head", None),
        P(),
        P(),
    )
    out_specs = (P(("parts", "head"), None, None), P("parts", "head", None))
    return jax.shard_map(body, mesh=mesh, in_specs=in_specs, out_specs=out_specs, check_vma=False)
```

time: 935 us -> 393 us (0.42)
  waiting for transfers between devices: 454 us -> 187 us
  local copies, waits for them, and re-layouts: 224 us -> 50.2 us
  matrix products: 99.8 us -> 3.2 us
  Pallas kernels: 0 us -> 84.5 us
  other arithmetic: 70.2 us -> 24.3 us
  blocking collectives: 39.5 us -> 0 us
  starting transfers between devices: 22.2 us -> 40.9 us
  between operations: 14.6 us -> 1.22 us
    reduce_scatter x2 -> x0, waiting for transfers between devices: 234 us -> none  [the longest x1 148 us: body(): lax.psum_scatter(jnp.dot(gate_grad, gate_weight.T, preferred_element_type...]
    psum x1 -> x0, waiting for transfers between devices: 113 us -> none  [body(): features = lax.psum(partial_value, 'head') / shower_counts[:, None]]
    dot_general x24 -> x2, matrix products: 99.4 us -> 2.81 us  [the longest x1 2.3 us: body(): jnp.dot(down_weight, class_weight, preferred_element_type=jnp.float32)]
    pallas_call x0 -> x5, Pallas kernels: none -> 84.5 us  [the longest x2 69.8 us: attend(): pl.pallas_call(functools.partial(attend_kernel, min(512, length)), grid=(...]
    all_to_all x4 -> x6, waiting for transfers between devices: 76.9 us -> 144 us  [the longest x2 96.2 us: body(): got = lax.all_to_all(sent, 'head', 0, 0, tiled=True)]
    convert_element_type x8 -> x0, local copies, waits for them, and re-layouts: 57.2 us -> none  [the longest x4 54.3 us: body(): pooled_rows = pooled_all.reshape(showers, HEADS, devices, per_device, hea...]
    reduce_sum x15 -> x1, other arithmetic: 52.7 us -> 0.09 us  [body(): cnt = jnp.sum(flags.reshape(devices, showers, each, POOL), axis=3)]
    ppermute x0 -> x11, waiting for transfers between devices: none -> 42.5 us  [swap(): return lax.ppermute(x, 'head', [(d, d ^ bit) for d in range(devices)])]
  transfers between devices with their start and end apart: 8 -> 17, of which waited for: 7 -> 9; matrix products, arithmetic and copies ran while one was open for 16% -> 9% of each run, Pallas kernels for 0% -> 18%
where the time goes in v1:
time: 393 us; the launch traced here: 391 us
  waiting for transfers between devices  187 us (48%)
  Pallas kernels  84.5 us (22%)
  local copies, waits for them, and re-layouts  50.2 us (13%)
  starting transfers between devices  40.9 us (10%)
  other arithmetic  24.3 us (6%)
    all_to_all x2, waiting for transfers between devices, body(): got = lax.all_to_all(sent, 'head', 0, 0, tiled=True)  96.2 us
    pallas_call x2, Pallas kernels, attend(): pl.pallas_call(functools.partial(attend_kernel, min(512, length)), grid=(...  69.8 us
    ppermute x11, waiting for transfers between devices, swap(): return lax.ppermute(x, 'head', [(d, d ^ bit) for d in range(devices)])  42.5 us
    all_to_all x1, waiting for transfers between devices, body(): lax.all_to_all(grads, 'head', 0, 0, axis_index_groups=lines, tiled=True)  25.2 us
    unnamed x64, local copies, waits for them, and re-layouts  20.6 us
    all_to_all x2, waiting for transfers between devices, body(): pooled.append(lax.all_to_all(part, 'head', 0, 0, tiled=True))  15.5 us
    concatenate x6, other arithmetic, gather(): x = jnp.concatenate([x, swap(x, bit)], axis=0)  15.4 us
    reshape x3, local copies, waits for them, and re-layouts, outgoing(): x.reshape(showers, local, group, features)  13.7 us
  transfers between devices with their start and end apart: 17, of which 9 were waited for; matrix products, arithmetic and copies ran while one was open for 9% of the time, Pallas kernels for 18%

profile of v1, /device:TPU:0, one launch (start us, length us, event | category | flops | bytes accessed | tf_op | source)
XLA Modules:
  0.0 391.4 jit_solution(8031089377755055155)
XLA Ops:
  0.6 4.6 %reshape.187 = bf16[8,64,4,512]{3,2,1,0:T(4,128)(2,1)} reshape(bf16[8,64,2048]{2,1,0:T(8,128)(2,1)} %param.21) | data formatting | bytes 4194304 | tf_op jit(solution)/shard_map/reshape | solution.py:255
  5.3 4.5 %reshape.185 = bf16[8,64,4,512]{3,2,1,0:T(4,128)(2,1)} reshape(bf16[8,64,2048]{2,1,0:T(8,128)(2,1)} %param.20) | data formatting | bytes 4194304 | tf_op jit(solution)/shard_map/reshape | solution.py:255
  9.8 4.5 %reshape.183 = bf16[8,64,4,512]{3,2,1,0:T(4,128)(2,1)} reshape(bf16[8,64,2048]{2,1,0:T(8,128)(2,1)} %param.19) | data formatting | bytes 4194304 | tf_op jit(solution)/shard_map/reshape | solution.py:255
  20.9 2.5 pad_maximum_fusion
  23.4 7.4 %all-to-all-start.1 = ((bf16[32,64,1152]{2,1,0:T(8,128)(2,1)}), bf16[32,64,1152]{2,1,0:T(8,128)(2,1)}, u32[]{:S(2)}, u32[]{:S(2)}) async-start(bf16[32,64,1152]{2,1,0:T(8,128)(2,1)} %pad_maximum_fusion), calls=%async_computation.1 | async-start | bytes 9437184 | tf_op jit(solution)/shard_map/all_to_all | solution.py:263
  31.8 2.3 convolution_bitcast_fusion
  39.9 96.2 %all-to-all-done.1 = bf16[32,64,1152]{2,1,0:T(8,128)(2,1)} async-done(((bf16[32,64,1152]{2,1,0:T(8,128)(2,1)}), bf16[32,64,1152]{2,1,0:T(8,128)(2,1)}, u32[]{:S(2)}, u32[]{:S(2)}) %all-to-all-start.1) | async-done | bytes 4718624 | tf_op jit(solution)/shard_map/all_to_all | solution.py:263
  136.1 4.1 %all-to-all-start = ((bf16[32,64,384]{2,1,0:T(8,128)(2,1)}), bf16[32,64,384]{2,1,0:T(8,128)(2,1)}, u32[]{:S(2)}, u32[]{:S(2)}) async-start(bf16[32,64,384]{2,1,0:T(8,128)(2,1)} %pad_maximum_fusion.5), calls=%async_computation | async-start | bytes 3145728 | tf_op jit(solution)/shard_map/all_to_all | solution.py:263
  141.9 13.6 %collective-permute-done.1 = bf16[32,8,64]{0,2,1:T(8,128)(2,1)S(1)} collective-permute-done((bf16[32,8,64]{0,2,1:T(8,128)(2,1)S(1)}, bf16[32,8,64]{0,2,1:T(8,128)(2,1)S(1)}, u32[]{:S(2)}, u32[]{:S(2)}) %collective-permute-start.1) | collective-permute-done | bytes 32800 | tf_op jit(solution)/shard_map/ppermute | solution.py:250
  155.7 3.3 collective-permute-start.2
  159.1 4.0 %collective-permute-done.2 = bf16[32,8,64]{0,2,1:T(8,128)(2,1)S(1)} collective-permute-done((bf16[32,8,64]{0,2,1:T(8,128)(2,1)S(1)}, bf16[32,8,64]{0,2,1:T(8,128)(2,1)S(1)}, u32[]{:S(2)}, u32[]{:S(2)}) %collective-permute-start.2) | collective-permute-done | bytes 32800 | tf_op jit(solution)/shard_map/ppermute | solution.py:250
  163.3 7.0 %collective-permute-done.3 = bf16[32,8,64]{0,2,1:T(8,128)(2,1)S(1)} collective-permute-done((bf16[32,8,64]{0,2,1:T(8,128)(2,1)S(1)}, bf16[32,8,64]{0,2,1:T(8,128)(2,1)S(1)}, u32[]{:S(2)}, u32[]{:S(2)}) %collective-permute-start.3) | collective-permute-done | bytes 32800 | tf_op jit(solution)/shard_map/ppermute | solution.py:250
  170.3 3.2 collective-permute-start.4
  173.7 9.6 %collective-permute-done.4 = bf16[32,8,64]{0,2,1:T(8,128)(2,1)S(1)} collective-permute-done((bf16[32,8,64]{0,2,1:T(8,128)(2,1)S(1)}, bf16[32,8,64]{0,2,1:T(8,128)(2,1)S(1)}, u32[]{:S(2)}, u32[]{:S(2)}) %collective-permute-start.4) | collective-permute-done | bytes 32800 | tf_op jit(solution)/shard_map/ppermute | solution.py:250
  183.9 3.1 pad_maximum_fusion.3
  188.2 2.8 pad_maximum_fusion.4
  192.0 51.3 %attend.2 = (bf16[8,64,2048]{2,1,0:T(8,128)(2,1)}, bf16[128,384]{1,0:T(8,128)(2,1)S(1)}) custom-call(bf16[2048,1152]{1,0:T(8,128)(2,1)} %bitcast.15.q_ref.k_ref.v_ref, bf16[2048,1152]{1,0:T(8,128)(2,1)} %bitcast.15.q_ref.k_ref.v_ref, bf16[2048,1152]{1,0:T(8,128)(2,1)} %bitcast.15.q_ref.k_ref.v_ref, f32[1,2048]{1,0:T(1,128)S(1)} %reshape.190.valid_ref, ...), custom_call_target="tpu_custom_call" | custom-call | flops 6442450944 | bytes 6291456 | tf_op jit(solution)/shard_map/attend/pallas_call | solution.py:95
  243.3 18.4 %attend.3 = (bf16[8,64,2048]{2,1,0:T(8,128)(2,1)}, bf16[128,128]{1,0:T(8,128)(2,1)S(1)}) custom-call(bf16[2048,384]{1,0:T(8,128)(2,1)} %bitcast.6.q_ref.k_ref.v_ref, bf16[2048,384]{1,0:T(8,128)(2,1)} %bitcast.6.q_ref.k_ref.v_ref, bf16[2048,384]{1,0:T(8,128)(2,1)} %bitcast.6.q_ref.k_ref.v_ref, ...), custom_call_target="tpu_custom_call", output_to_operand_aliasing={{0}: (6, {})} | custom-call | flops 2147483648 | bytes 2097152 | tf_op jit(solution)/shard_map/attend/pallas_call | solution.py:95
  262.5 3.7 all-to-all-start.3
  267.3 15.5 %all-to-all-done.3.refs_1_ = bf16[32,32,128]{2,1,0:T(8,128)(2,1)S(1)} async-done(((bf16[32,32,128]{2,1,0:T(8,128)(2,1)}), bf16[32,32,128]{2,1,0:T(8,128)(2,1)S(1)}, u32[]{:S(2)}, u32[]{:S(2)}) %all-to-all-start.3) | async-done | bytes 262176 | tf_op jit(solution)/shard_map/all_to_all | solution.py:327
  283.8 3.7 all-to-all-start.2
  295.7 8.3 %collective-permute-done.10 = f32[2,256,128]{2,1,0:T(8,128)} collective-permute-done((f32[2,256,128]{2,1,0:T(8,128)S(1)}, f32[2,256,128]{2,1,0:T(8,128)}, u32[]{:S(2)}, u32[]{:S(2)}) %collective-permute-start.10) | collective-permute-done | bytes 262176 | tf_op jit(solution)/shard_map/ppermute | solution.py:250
  305.1 3.8 pad_maximum_fusion.1.refs_6_.gate_ref
  308.9 3.5 pad_maximum_fusion.2.refs_7_.up_ref
  315.4 2.2 copy-done.3
  319.5 6.6 %classifier_forward.1 = (f32[8,128]{1,0:T(8,128)S(1)}, f32[4,256,256]{2,1,0:T(8,128)S(1)}, f32[4,256,256]{2,1,0:T(8,128)S(1)}, f32[32,2048]{1,0:T(8,128)S(1)}) custom-call(s32[1]{0:T(128)} %bitcast.17.own_ref, bf16[32,32,384]{2,1,0:T(8,128)(2,1)} %all-to-all-done.2.refs_0_, bf16[32,32,128]{2,1,0:T(8,128)(2,1)S(1)} %copy-done.11, ...), custom_call_target="tpu_custom_call" | custom-call | tf_op jit(solution)/shard_map/classifier_forward/pallas_call | solution.py:342
  329.4 4.8 %all-to-all-start.4 = ((f32[32,8,128]{2,1,0:T(8,128)}), f32[32,8,128]{2,1,0:T(8,128)S(1)}, u32[]{:S(2)}, u32[]{:S(2)}) async-start(f32[32,8,128]{2,1,0:T(8,128)} %broadcast_in_dim.131), calls=%async_computation.4 | async-start | bytes 262144 | tf_op jit(solution)/shard_map/all_to_all | solution.py:370
  335.0 7.5 %all-to-all-done.4.parts_ref = f32[32,8,128]{2,1,0:T(8,128)S(1)} async-done(((f32[32,8,128]{2,1,0:T(8,128)}), f32[32,8,128]{2,1,0:T(8,128)S(1)}, u32[]{:S(2)}, u32[]{:S(2)}) %all-to-all-start.4) | async-done | bytes 131104 | tf_op jit(solution)/shard_map/all_to_all | solution.py:370
  351.4 6.0 %classifier_backward.1 = (bf16[8,32,2048]{2,1,0:T(8,128)(2,1)S(1)}, f32[8,128]{1,0:T(8,128)S(1)}) custom-call(f32[32,8,128]{2,1,0:T(8,128)S(1)} %all-to-all-done.4.parts_ref, f32[8,128]{1,0:T(8,128)S(1)} %broadcast_in_dim.132.counts_ref, f32[1,128]{1,0:T(1,128)S(1)} %bitcast.53, f32[8,128]{1,0:T(8,128)S(1)} %fusion.12.target_ref, f32[32,8]{1,0:T(8,128)S(1)} %copy-done.17, ...), custom_call_target="tpu_custom_call" | custom-call | tf_op jit(solution)/shard_map/classifier_backward/pallas_call | solution.py:384
  358.3 4.4 %all-to-all-start.5 = ((bf16[8,32,2048]{2,1,0:T(8,128)(2,1)}), bf16[8,32,2048]{2,1,0:T(8,128)(2,1)}, u32[]{:S(2)}, u32[]{:S(2)}) async-start(bf16[8,32,2048]{2,1,0:T(8,128)(2,1)} %copy-done.13), calls=%async_computation.5 | async-start | bytes 2097152 | tf_op jit(solution)/shard_map/all_to_all | solution.py:403
  363.9 25.2 %all-to-all-done.5.dn_ref = bf16[8,32,2048]{2,1,0:T(8,128)(2,1)} async-done(((bf16[8,32,2048]{2,1,0:T(8,128)(2,1)}), bf16[8,32,2048]{2,1,0:T(8,128)(2,1)}, u32[]{:S(2)}, u32[]{:S(2)}) %all-to-all-start.5) | async-done | bytes 1048608 | tf_op jit(solution)/shard_map/all_to_all | solution.py:403
  389.1 2.2 norm_backward.1
  (149 shorter events, 50.1 us)
Async XLA Ops:
  0.6 265.6 %copy-start = (bf16[256,4096]{1,0:T(8,128)(2,1)S(1)}, bf16[256,4096]{1,0:T(8,128)(2,1)}, u32[]{:S(2)}) copy-start(bf16[256,4096]{1,0:T(8,128)(2,1)} %param.26) | copy-start | bytes 6291460
  23.4 7.4 %copy-start.26 = (s32[8,64]{1,0:T(8,128)S(1)}, s32[8,64]{1,0:T(8,128)}, u32[]{:S(2)}) copy-start(s32[8,64]{1,0:T(8,128)} %param.22) | copy-start | bytes 6148
  23.4 7.5 %copy-start.29 = (s32[8]{0:T(128)S(1)}, s32[8]{0:T(128)}, u32[]{:S(2)}) copy-start(s32[8]{0:T(128)} %param.23) | copy-start | bytes 100
  23.4 8.4 %copy-start.5 = (bf16[2048,128]{1,0:T(8,128)(2,1)S(1)}, bf16[2048,128]{1,0:T(8,128)(2,1)}, u32[]{:S(2)}) copy-start(bf16[2048,128]{1,0:T(8,128)(2,1)} %refs_12_.1) | copy-start | bytes 1572868
  23.4 112.7 %all-to-all-start.1 = ((bf16[32,64,1152]{2,1,0:T(8,128)(2,1)}), bf16[32,64,1152]{2,1,0:T(8,128)(2,1)}, u32[]{:S(2)}, u32[]{:S(2)}) async-start(bf16[32,64,1152]{2,1,0:T(8,128)(2,1)} %pad_maximum_fusion), calls=%async_computation.1 | async-start | bytes 9437184 | tf_op jit(solution)/shard_map/all_to_all | solution.py:263
  31.1 109.1 %collective-permute-start = (bf16[32,8,64]{0,2,1:T(8,128)(2,1)S(1)}, bf16[32,8,64]{0,2,1:T(8,128)(2,1)S(1)}, u32[]{:S(2)}, u32[]{:S(2)}) collective-permute-start(bf16[32,8,64]{0,2,1:T(8,128)(2,1)S(1)} %broadcast_select_fusion), channel_id=1, source_target_pairs={{0,1},{1,0},{2,3},{3,2},{4,5},{5,4},{6,7},{7,6},{8,9},{9,8},{10,11... | collective-permute-start | bytes 98312 | tf_op jit(solution)/shard_map/ppermute | solution.py:250
  31.3 152.6 %collective-permute-start.5 = (bf16[1,2048,256]{2,1,0:T(8,128)(2,1)}, bf16[1,2048,256]{2,1,0:T(8,128)(2,1)}, u32[]{:S(2)}, u32[]{:S(2)}) collective-permute-start(bf16[1,2048,256]{2,1,0:T(8,128)(2,1)} %bitcast.57), channel_id=1, source_target_pairs={{0,1},{1,0},{2,3},{3,2},{4,5},{5,4},{6,7},{7,6},{8,9},{9,8},{10,11... | collective-permute-start | bytes 3145736 | tf_op jit(solution)/shard_map/ppermute | solution.py:250
  31.6 156.6 %collective-permute-start.7 = (bf16[1,2048,256]{2,1,0:T(8,128)(2,1)}, bf16[1,2048,256]{2,1,0:T(8,128)(2,1)}, u32[]{:S(2)}, u32[]{:S(2)}) collective-permute-start(bf16[1,2048,256]{2,1,0:T(8,128)(2,1)} %bitcast.60), channel_id=1, source_target_pairs={{0,1},{1,0},{2,3},{3,2},{4,5},{5,4},{6,7},{7,6},{8,9},{9,8},{10,11... | collective-permute-start | bytes 3145736 | tf_op jit(solution)/shard_map/ppermute | solution.py:250
  34.1 257.4 %collective-permute-start.9 = (f32[1,256,128]{2,1,0:T(8,128)}, f32[1,256,128]{2,1,0:T(8,128)}, u32[]{:S(2)}, u32[]{:S(2)}) collective-permute-start(f32[1,256,128]{2,1,0:T(8,128)} %convolution_bitcast_fusion), channel_id=1, source_target_pairs={{0,1},{1,0},{2,3},{3,2},{4,5},{5,4},{6,7},{7,6},{8,9},{9,8},{10,11... | collective-permute-start | bytes 393224 | tf_op jit(solution)/shard_map/ppermute | solution.py:250
  39.9 119.1 %copy-start.28 = (s32[128]{0:T(128)S(1)}, s32[128]{0:T(128)}, u32[]{:S(2)}) copy-start(s32[128]{0:T(128)} %constant.84.clone) | copy-start | bytes 1540
  39.9 123.4 %copy-start.31 = (s32[8]{0:T(128)S(1)}, s32[8]{0:T(128)}, u32[]{:S(2)}) copy-start(s32[8]{0:T(128)} %param.24) | copy-start | bytes 100
  136.1 107.2 %all-to-all-start = ((bf16[32,64,384]{2,1,0:T(8,128)(2,1)}), bf16[32,64,384]{2,1,0:T(8,128)(2,1)}, u32[]{:S(2)}, u32[]{:S(2)}) async-start(bf16[32,64,384]{2,1,0:T(8,128)(2,1)} %pad_maximum_fusion.5), calls=%async_computation | async-start | bytes 3145728 | tf_op jit(solution)/shard_map/all_to_all | solution.py:263
  140.3 15.2 %collective-permute-start.1 = (bf16[32,8,64]{0,2,1:T(8,128)(2,1)S(1)}, bf16[32,8,64]{0,2,1:T(8,128)(2,1)S(1)}, u32[]{:S(2)}, u32[]{:S(2)}) collective-permute-start(bf16[32,8,64]{0,2,1:T(8,128)(2,1)S(1)} %fusion.1), channel_id=1, source_target_pairs={{0,2},{1,3},{2,0},{3,1},{4,6},{5,7},{6,4},{7,5},{8,10},{9,11},{10,... | collective-permute-start | bytes 98312 | tf_op jit(solution)/shard_map/ppermute | solution.py:250
  155.7 7.5 %collective-permute-start.2 = (bf16[32,8,64]{0,2,1:T(8,128)(2,1)S(1)}, bf16[32,8,64]{0,2,1:T(8,128)(2,1)S(1)}, u32[]{:S(2)}, u32[]{:S(2)}) collective-permute-start(bf16[32,8,64]{0,2,1:T(8,128)(2,1)S(1)} %fusion.21), channel_id=1, source_target_pairs={{0,4},{1,5},{2,6},{3,7},{4,0},{5,1},{6,2},{7,3},{8,12},{9,13},{10,... | collective-permute-start | bytes 98312 | tf_op jit(solution)/shard_map/ppermute | solution.py:250
  163.2 7.1 %collective-permute-start.3 = (bf16[32,8,64]{0,2,1:T(8,128)(2,1)S(1)}, bf16[32,8,64]{0,2,1:T(8,128)(2,1)S(1)}, u32[]{:S(2)}, u32[]{:S(2)}) collective-permute-start(bf16[32,8,64]{0,2,1:T(8,128)(2,1)S(1)} %add.48), channel_id=1, source_target_pairs={{0,8},{1,9},{2,10},{3,11},{4,12},{5,13},{6,14},{7,15},{8,0},{9,1},... | collective-permute-start | bytes 98312 | tf_op jit(solution)/shard_map/ppermute | solution.py:250
  170.3 12.9 %collective-permute-start.4 = (bf16[32,8,64]{0,2,1:T(8,128)(2,1)S(1)}, bf16[32,8,64]{0,2,1:T(8,128)(2,1)S(1)}, u32[]{:S(2)}, u32[]{:S(2)}) collective-permute-start(bf16[32,8,64]{0,2,1:T(8,128)(2,1)S(1)} %add.49), channel_id=1, source_target_pairs={{0,16},{1,17},{2,18},{3,19},{4,20},{5,21},{6,22},{7,23},{8,24},{9,... | collective-permute-start | bytes 98312 | tf_op jit(solution)/shard_map/ppermute | solution.py:250
  183.6 110.5 %copy-start.23 = (f32[32,8,4]{0,2,1:T(4,128)}, f32[32,8,4]{0,2,1:T(4,128)S(1)}, u32[]{:S(2)}) copy-start(f32[32,8,4]{0,2,1:T(4,128)S(1)} %bitcast_reduce_fusion) | copy-start | bytes 12292
  183.9 4.3 %copy-start.21 = (bf16[2048,256]{1,0:T(8,128)(2,1)S(1)}, bf16[2048,256]{1,0:T(8,128)(2,1)}, u32[]{:S(2)}) copy-start(bf16[2048,256]{1,0:T(8,128)(2,1)} %param.29) | copy-start | bytes 3145732
  187.0 118.0 %collective-permute-start.6 = (bf16[2,2048,256]{2,1,0:T(8,128)(2,1)}, bf16[2,2048,256]{2,1,0:T(8,128)(2,1)}, u32[]{:S(2)}, u32[]{:S(2)}) collective-permute-start(bf16[2,2048,256]{2,1,0:T(8,128)(2,1)} %pad_maximum_fusion.3), channel_id=1, source_target_pairs={{0,2},{1,3},{2,0},{3,1},{4,6},{5,7},{6,4},{7,5},{8,10},{9,11},{10,... | collective-permute-start | bytes 6291464 | tf_op jit(solution)/shard_map/ppermute | solution.py:250
  191.1 117.8 %collective-permute-start.8 = (bf16[2,2048,256]{2,1,0:T(8,128)(2,1)}, bf16[2,2048,256]{2,1,0:T(8,128)(2,1)}, u32[]{:S(2)}, u32[]{:S(2)}) collective-permute-start(bf16[2,2048,256]{2,1,0:T(8,128)(2,1)} %pad_maximum_fusion.4), channel_id=1, source_target_pairs={{0,2},{1,3},{2,0},{3,1},{4,6},{5,7},{6,4},{7,5},{8,10},{9,11},{10,... | collective-permute-start | bytes 6291464 | tf_op jit(solution)/shard_map/ppermute | solution.py:250
  262.5 20.3 %all-to-all-start.3 = ((bf16[32,32,128]{2,1,0:T(8,128)(2,1)}), bf16[32,32,128]{2,1,0:T(8,128)(2,1)S(1)}, u32[]{:S(2)}, u32[]{:S(2)}) async-start(bf16[32,32,128]{2,1,0:T(8,128)(2,1)} %bitcast.21), calls=%async_computation.3 | async-start | bytes 524288 | tf_op jit(solution)/shard_map/all_to_all | solution.py:327
  266.3 21.3 %copy-start.27 = (s32[256]{0:T(256)S(1)}, s32[256]{0:T(256)}, u32[]{:S(2)}) copy-start(s32[256]{0:T(256)} %constant.87.clone) | copy-start | bytes 3076
  266.3 21.4 %copy-start.30 = (s32[8]{0:T(128)S(1)}, s32[8]{0:T(128)}, u32[]{:S(2)}) copy-start(s32[8]{0:T(128)} %param.23) | copy-start | bytes 100
  282.8 7.2 %copy-start.10 = (bf16[32,32,128]{2,1,0:T(8,128)(2,1)}, bf16[32,32,128]{2,1,0:T(8,128)(2,1)S(1)}, u32[]{:S(2)}) copy-start(bf16[32,32,128]{2,1,0:T(8,128)(2,1)S(1)} %all-to-all-done.3.refs_1_) | copy-start | bytes 786436
  283.8 28.6 %all-to-all-start.2 = ((bf16[32,32,384]{2,1,0:T(8,128)(2,1)}), bf16[32,32,384]{2,1,0:T(8,128)(2,1)}, u32[]{:S(2)}, u32[]{:S(2)}) async-start(bf16[32,32,384]{2,1,0:T(8,128)(2,1)} %bitcast.63), calls=%async_computation.2 | async-start | bytes 1572864 | tf_op jit(solution)/shard_map/all_to_all | solution.py:327
  292.5 11.5 %collective-permute-start.10 = (f32[2,256,128]{2,1,0:T(8,128)S(1)}, f32[2,256,128]{2,1,0:T(8,128)}, u32[]{:S(2)}, u32[]{:S(2)}) collective-permute-start(f32[2,256,128]{2,1,0:T(8,128)S(1)} %pad_maximum_fusion.7), channel_id=1, source_target_pairs={{0,2},{1,3},{2,0},{3,1},{4,6},{5,7},{6,4},{7,5},{8,10},{9,11},{10,... | collective-permute-start | bytes 786440 | tf_op jit(solution)/shard_map/ppermute | solution.py:250
  308.9 4.3 %copy-start.16 = (f32[2048]{0:T(1024)S(1)}, f32[2048]{0:T(1024)}, u32[]{:S(2)}) copy-start(f32[2048]{0:T(1024)} %param.27) | copy-start | bytes 24580
  329.4 13.1 %all-to-all-start.4 = ((f32[32,8,128]{2,1,0:T(8,128)}), f32[32,8,128]{2,1,0:T(8,128)S(1)}, u32[]{:S(2)}, u32[]{:S(2)}) async-start(f32[32,8,128]{2,1,0:T(8,128)} %broadcast_in_dim.131), calls=%async_computation.4 | async-start | bytes 262144 | tf_op jit(solution)/shard_map/all_to_all | solution.py:370
  358.3 4.4 %copy-start.25 = (f32[8]{0:T(128)S(1)}, f32[8]{0:T(128)}, u32[]{:S(2)}) copy-start(f32[8]{0:T(128)} %convert_element_type.36) | copy-start | bytes 100
  358.3 4.6 %copy-start.24 = (f32[32,8,4]{0,2,1:T(4,128)S(1)}, f32[32,8,4]{0,2,1:T(4,128)}, u32[]{:S(2)}) copy-start(f32[32,8,4]{0,2,1:T(4,128)} %copy-done.23) | copy-start | bytes 12292
  358.3 30.8 %copy-start.15 = (f32[32,2048]{1,0:T(8,128)S(1)}, f32[32,2048]{1,0:T(8,128)}, u32[]{:S(2)}) copy-start(f32[32,2048]{1,0:T(8,128)} %copy-done.14) | copy-start | bytes 786436
  358.3 30.8 %all-to-all-start.5 = ((bf16[8,32,2048]{2,1,0:T(8,128)(2,1)}), bf16[8,32,2048]{2,1,0:T(8,128)(2,1)}, u32[]{:S(2)}, u32[]{:S(2)}) async-start(bf16[8,32,2048]{2,1,0:T(8,128)(2,1)} %copy-done.13), calls=%async_computation.5 | async-start | bytes 2097152 | tf_op jit(solution)/shard_map/all_to_all | solution.py:403
  (17 other events, 25.1 us)

commit v2 on v1

--- a/solution.py
+++ b/solution.py
@@ -13,6 +13,7 @@
 POOL = 16
 LANES = 128
 MASKED = -1e30
+ABSENT = 64.0
 epsilon = 1e-06
 HIGH = lax.Precision.HIGHEST
 NT = (((1,), (1,)), ((), ()))
@@ -31,21 +32,45 @@
     return jnp.concatenate([jnp.cos(angles), jnp.sin(angles)], axis=1)
 
 
-def attend_kernel(block, q_ref, k_ref, v_ref, valid_ref, pool_ref, cnt_ref, *rest):
+def pack_kernel(chunks, slot_ref, count_ref, q_ref, k_ref, v_ref, *outs):
+    shower = pl.program_id(0)
+    group = outs[0].shape[0]
+    local = q_ref.shape[1]
+    features = q_ref.shape[2] // group
+    valid = (slot_ref[pl.ds(shower, 1), :] < count_ref[shower]).astype(jnp.float32)
+    square = (local, local)
+    diagonal = lax.broadcasted_iota(jnp.int32, square, 0) == lax.broadcasted_iota(
+        jnp.int32, square, 1
+    )
+    column = jnp.sum(jnp.where(diagonal, valid, 0.0), axis=1, keepdims=True) > 0.5
+    for (first, count), out in zip(chunks, outs):
+        size = count * LANES
+        for m in range(group):
+            at = m * features + first * LANES
+            for t, ref in enumerate((q_ref, k_ref, v_ref)):
+                part = ref[0, :, at : at + size]
+                if t == 1:
+                    part = jnp.where(column, part, jnp.asarray(ABSENT, part.dtype))
+                out[m, :, t * size : (t + 1) * size] = part
+
+
+def attend_kernel(block, q_ref, k_ref, v_ref, pool_ref, *rest):
     att_ref, pooled_ref = rest[-2:]
     length = q_ref.shape[0]
     half = LANES // 2
     lane = lax.broadcasted_iota(jnp.int32, (1, LANES), 1)
     low = lane < half
-    valid = valid_ref[...]
-    bias = jnp.where(valid > 0.5, 0.0, MASKED)
     keys = k_ref[...]
     rows = v_ref[...]
     one = jnp.ones_like(rows)
+    present = jnp.where(keys.astype(jnp.float32) < 0.5 * ABSENT, 1.0, 0.0).astype(jnp.bfloat16)
+    pick = jnp.broadcast_to(jnp.where(lane == 0, 1.0, 0.0).astype(jnp.bfloat16), (8, LANES))
+    valid = mm(pick, present, NT)[:1]
+    bias = jnp.where(valid > 0.5, 0.0, MASKED)
     values = (jnp.where(low, rows, one), jnp.where(low, one, rows))
 
-    def step(i, carry):
-        at = pl.ds(pl.multiple_of(i * block, block), block)
+    for i in range(length // block):
+        at = slice(i * block, (i + 1) * block)
         query = q_ref[at, :] * jnp.asarray(0.125, jnp.bfloat16)
         zero = jnp.zeros_like(query)
         outs = []
@@ -57,17 +82,20 @@
             outs.append(mm(weights, values[h]))
         top = jnp.where(low, outs[0], outs[1])
         total = jnp.where(low, pltpu.roll(outs[0], half, 1), pltpu.roll(outs[1], half, 1))
-        mixed = ((top / total).T * valid_ref[:, at]).astype(jnp.bfloat16)
+        mixed = ((top / total).T * valid[:, at]).astype(jnp.bfloat16)
         att_ref[0, :, at] = mixed[:half]
         att_ref[1, :, at] = mixed[half:]
-        return carry
-
-    lax.fori_loop(0, length // block, step, 0)
     both = jnp.concatenate([att_ref[0], att_ref[1]], axis=0)
-    pooled_ref[...] = (mm(pool_ref[...], both, NT) / cnt_ref[...]).astype(jnp.bfloat16)
-
-
-def attend(qkv, valid, pool, cnt, first, count, pairs, before):
+    cnt = mm(pool_ref[...], jnp.broadcast_to(valid, (LANES, length)).astype(jnp.bfloat16), NT)
+    pooled = (mm(pool_ref[...], both, NT) / jnp.maximum(cnt, 1.0)).astype(jnp.bfloat16)
+    rows = pooled_ref.shape[1]
+    group = pooled.shape[0] // rows
+    for d in range(pooled_ref.shape[0]):
+        m = d % group
+        pooled_ref[d] = pooled[m * rows : (m + 1) * rows]
+
+
+def attend(qkv, pool, first, count, pairs, devices, rows, before):
     length = qkv.shape[0]
     windows = pool.shape[0]
     head_dim = LANES // 2
@@ -82,27 +110,25 @@
         part(0),
         part(1),
         part(2),
-        whole((1, length)),
         whole((windows, length)),
-        whole((windows, LANES)),
     ]
-    operands = [qkv, qkv, qkv, valid, pool, cnt]
+    operands = [qkv, qkv, qkv, pool]
     aliases = {}
     if before is not None:
         in_specs.append(pl.BlockSpec(memory_space=pl.ANY))
         operands.append(before)
-        aliases = {6: 0}
+        aliases = {4: 0}
     return pl.pallas_call(
         functools.partial(attend_kernel, min(512, length)),
         grid=(count,),
         out_shape=(
             jax.ShapeDtypeStruct((pairs, head_dim, length), jnp.bfloat16),
-            jax.ShapeDtypeStruct((windows, count * LANES), jnp.bfloat16),
+            jax.ShapeDtypeStruct((devices, rows, count * LANES), jnp.bfloat16),
         ),
         in_specs=in_specs,
         out_specs=(
             pl.BlockSpec((2, head_dim, length), lambda j: (first + j, 0, 0)),
-            pl.BlockSpec((windows, LANES), lambda j: (0, j)),
+            pl.BlockSpec((devices, rows, LANES), lambda j: (0, 0, j)),
         ),
         input_output_aliases=aliases,
         compiler_params=pltpu.CompilerParams(vmem_limit_bytes=40 * MIB),
@@ -122,7 +148,7 @@
     x_refs, refs = refs[:n], refs[n:]
     (
         perm_ref, gain_ref, scale_ref, shift_ref, gate_ref, up_ref, dc_ref, cnt_ref, own_cnt_ref,
-        coef_ref, class_ref, logits_ref, ga_ref, aa_ref, own_x_ref, gathered, normed,
+        coef_ref, class_ref, copies_ref, ga_ref, aa_ref, own_x_ref, gathered, normed, logits_ref,
     ) = refs
     step = pl.program_id(0)
     showers = logits_ref.shape[0]
@@ -164,6 +190,11 @@
     coef = coef_ref[...][:, :1]
     ga_ref[0] = coef * (up * sigma * (1.0 + gate * (1.0 - sigma)))
     aa_ref[0] = coef * activated
+
+    @pl.when(step == pl.num_programs(0) - 1)
+    def _():
+        for d in range(copies_ref.shape[0]):
+            copies_ref[d] = logits_ref[...]
 
 
 def backward_kernel(
@@ -251,53 +282,66 @@
 
     chunks = [(0, slabs - 1), (slabs - 1, 1)] if slabs > 1 else [(0, 1)]
 
-    def outgoing(x, first, count):
-        x = x.reshape(showers, local, group, features)[
-            ..., first * LANES : (first + count) * LANES
+    sent = pl.pallas_call(
+        functools.partial(pack_kernel, chunks),
+        grid=(showers,),
+        out_shape=[
+            jax.ShapeDtypeStruct((devices, local, 3 * count * LANES), jnp.bfloat16)
+            for _, count in chunks
+        ],
+        in_specs=[
+            pl.BlockSpec((showers, local), lambda s: (0, 0)),
+            pl.BlockSpec(memory_space=pltpu.SMEM),
         ]
-        return x.transpose(0, 2, 1, 3).reshape(devices, local, count * LANES)
-
-    received = []
-    for first, count in chunks:
-        sent = jnp.concatenate([outgoing(x, first, count) for x in (queries, keys, values)], axis=2)
-        got = lax.all_to_all(sent, "head", 0, 0, tiled=True)
-        received.append(got.reshape(length, 3 * count * LANES))
-
-    flags = (slot_positions < counts[:, None]).astype(jnp.bfloat16)
-    flags = jnp.where(
-        jnp.arange(devices)[:, None, None] == me, flags[None], jnp.zeros((), jnp.bfloat16)
-    )
-    bit = 1
-    while bit < devices:
-        flags = flags + swap(flags, bit)
-        bit *= 2
-    flags = flags.astype(jnp.float32)
-    cnt = jnp.sum(flags.reshape(devices, showers, each, POOL), axis=3)
-    own_flags = lax.dynamic_index_in_dim(flags, owned, 1, False).reshape(1, length)
+        + [pl.BlockSpec((1, local, width), lambda s: (s, 0, 0))] * 3,
+        out_specs=[
+            pl.BlockSpec((group, local, 3 * count * LANES), lambda s: (s, 0, 0))
+            for _, count in chunks
+        ],
+        compiler_params=pltpu.CompilerParams(vmem_limit_bytes=60 * MIB),
+        name="pack",
+    )(slot_positions, counts, queries, keys, values)
+    sent, slot_positions, gate_weight, up_weight, down_weight = lax.optimization_barrier(
+        (sent, slot_positions, gate_weight, up_weight, down_weight)
+    )
+
+    def exchange(x):
+        got = lax.all_to_all(x, "head", 0, 0, tiled=True)
+        return got.reshape(length, x.shape[2])
+
+    received = [exchange(sent[0])]
+
+    valid = (slot_positions < counts[:, None]).astype(jnp.float32)
+    here = jnp.sum(valid.reshape(showers, each, POOL), axis=2)
+    mine = jnp.where(jnp.arange(outer)[:, None, None] == owned, here[None], 0.0)
+    bit = devices // 2
+    while bit >= group:
+        mine = mine + swap(mine, bit)
+        bit //= 2
 
     order = np.arange(windows).reshape(outer, group, each).transpose(1, 0, 2).reshape(windows)
     pool = jnp.asarray(order, jnp.int32)[:, None] == jnp.arange(length, dtype=jnp.int32)[None] // POOL
     pool = pool.astype(jnp.bfloat16)
-    own_cnt = lax.dynamic_index_in_dim(cnt, owned, 1, False)
-    own_cnt = own_cnt.reshape(outer, group, each).transpose(1, 0, 2).reshape(windows, 1)
-    own_cnt = jnp.broadcast_to(jnp.maximum(own_cnt, 1.0), (windows, LANES))
 
     def gather(x):
-        x = x[None]
-        bit = 1
-        while bit < group:
-            x = jnp.concatenate([x, swap(x, bit)], axis=0)
-            bit *= 2
+        x = [x[None]]
+        bit = group // 2
+        while bit:
+            x = [jnp.concatenate(x, axis=0)]
+            x.append(swap(x[0], bit))
+            bit //= 2
         return x
 
     gates = gather(gate_weight)
     ups = gather(up_weight)
     class_map = gather(jnp.dot(down_weight, class_weight, preferred_element_type=jnp.float32))
 
+    sent, gates, ups, class_map, mine = lax.optimization_barrier(
+        (sent[1:], gates, ups, class_map, mine)
+    )
+    received += [exchange(x) for x in sent]
+
     shower_counts = counts.astype(jnp.float32)
-    mine = lax.dynamic_index_in_dim(
-        cnt.reshape(outer, group, showers, each), me % group, 1, False
-    )
     coef = (mine / shower_counts[None, :, None]).reshape(total, 1)
     coef = jnp.broadcast_to(coef, (total, LANES))
     row_shower = np.tile(np.repeat(np.arange(showers), each), outer)
@@ -315,15 +359,28 @@
     scales = jnp.repeat(1.0 + modulation[:, width:], each, axis=0)
     gain = norm_gain.reshape(1, width)
 
+    target = (labels[:, None] == jnp.arange(classes, dtype=jnp.int32)[None]).astype(jnp.float32)
+    spread = jnp.asarray(
+        np.repeat(np.eye(showers), each, axis=0).astype(np.float32)
+    )
+    spread_counts = jnp.broadcast_to(shower_counts[:, None], (showers, classes))
+    heads_in = (spread_counts, class_bias.reshape(1, classes), target, spread)
+    fixed = (perm, gain, scales, shifts)
+    streamed = tuple(jnp.concatenate(x, axis=0) for x in (gates, ups, class_map))
+    late = (cnt_rows.astype(jnp.bfloat16), own_cnt_rows.astype(jnp.bfloat16), coef, class_weight)
+
     attention = None
     pooled = []
     for qkv, (first, count) in zip(received, chunks):
         attention, part = attend(
-            qkv, own_flags, pool, own_cnt, first, count, 2 * slabs, attention
+            qkv, pool, first, count, 2 * slabs, devices, rows, attention
         )
-        part = part.reshape(1, group, rows, count * LANES)
-        part = jnp.broadcast_to(part, (outer,) + part.shape[1:])
-        part = part.reshape(devices, rows, count * LANES)
+        if pooled:
+            part, pooled[-1] = lax.optimization_barrier((part, pooled[-1]))
+        else:
+            part, fixed, streamed, late, heads_in = lax.optimization_barrier(
+                (part, fixed, streamed, late, heads_in)
+            )
         pooled.append(lax.all_to_all(part, "head", 0, 0, tiled=True))
 
     units = gate_weight.shape[1]
@@ -336,14 +393,11 @@
 
     side = jax.ShapeDtypeStruct((group, total, units), jnp.float32)
     side_spec = pl.BlockSpec((1, total, units), lambda i: (i, 0, 0))
-    fixed = (perm, gain, scales, shifts)
-    streamed = (gates, ups, class_map)
-    late = (cnt_rows.astype(jnp.bfloat16), own_cnt_rows.astype(jnp.bfloat16), coef, class_weight)
     partial, gate_side, up_side, own_x = pl.pallas_call(
         functools.partial(forward_kernel, [count * LANES for _, count in chunks]),
         grid=(group,),
         out_shape=(
-            jax.ShapeDtypeStruct((showers, classes), jnp.float32),
+            jax.ShapeDtypeStruct((devices, showers, classes), jnp.float32),
             side,
             side,
             jax.ShapeDtypeStruct((block, width), jnp.float32),
@@ -354,7 +408,7 @@
         + [member(x) for x in streamed]
         + [whole(x) for x in late],
         out_specs=(
-            pl.BlockSpec((showers, classes), lambda i: (0, 0)),
+            pl.BlockSpec((devices, showers, classes), lambda i: (0, 0, 0)),
             side_spec,
             side_spec,
             pl.BlockSpec((block, width), lambda i: (0, 0)),
@@ -362,25 +416,13 @@
         scratch_shapes=[
             pltpu.VMEM((total, width), jnp.float32),
             pltpu.VMEM((total, width), jnp.bfloat16),
+            pltpu.VMEM((showers, classes), jnp.float32),
         ],
-        compiler_params=pltpu.CompilerParams(vmem_limit_bytes=40 * MIB),
+        compiler_params=pltpu.CompilerParams(vmem_limit_bytes=56 * MIB),
         name="classifier_forward",
     )(owned.reshape(1).astype(jnp.int32), *pooled, *fixed, *streamed, *late)
 
-    parts = lax.all_to_all(
-        jnp.broadcast_to(partial[None], (devices,) + partial.shape), "head", 0, 0, tiled=True
-    )
-    target = (labels[:, None] == jnp.arange(classes, dtype=jnp.int32)[None]).astype(jnp.float32)
-    spread = jnp.asarray(
-        np.repeat(np.eye(showers), each, axis=0).astype(np.float32)
-    )
-    heads_in = (
-        parts,
-        jnp.broadcast_to(shower_counts[:, None], (showers, classes)),
-        class_bias.reshape(1, classes),
-        target,
-        spread,
-    )
+    parts = lax.all_to_all(partial, "head", 0, 0, tiled=True)
     grads, miss = pl.pallas_call(
         backward_kernel,
         grid=(group,),
@@ -388,21 +430,20 @@
             jax.ShapeDtypeStruct((outer, block, width), jnp.bfloat16),
             jax.ShapeDtypeStruct((showers, classes), jnp.float32),
         ),
-        in_specs=[whole(x) for x in heads_in]
+        in_specs=[whole(x) for x in (parts,) + heads_in]
         + [member(x) for x in streamed + (gate_side, up_side)],
         out_specs=(
             pl.BlockSpec((outer, block, width), lambda i: (0, 0, 0)),
             pl.BlockSpec((showers, classes), lambda i: (0, 0)),
         ),
         scratch_shapes=[pltpu.VMEM((total, width), jnp.float32)],
-        compiler_params=pltpu.CompilerParams(vmem_limit_bytes=40 * MIB),
+        compiler_params=pltpu.CompilerParams(vmem_limit_bytes=56 * MIB),
         name="classifier_backward",
-    )(*heads_in, *streamed, gate_side, up_side)
+    )(parts, *heads_in, *streamed, gate_side, up_side)
 
     lines = [[o * group + m for o in range(outer)] for m in range(group)]
     grads = lax.all_to_all(grads, "head", 0, 0, axis_index_groups=lines, tiled=True)
     feature_grad = mm(miss, class_weight.astype(jnp.float32), NT, HIGH)
-    here = lax.dynamic_index_in_dim(cnt, me, 0, False)
     own_row_grads = (here / shower_counts[:, None])[:, :, None] * feature_grad[:, None, :]
     own_row_grads = own_row_grads.reshape(block, width)
     guidance = pl.pallas_call(

time: 393 us -> 291 us (0.74)
  waiting for transfers between devices: 187 us -> 127 us
  local copies, waits for them, and re-layouts: 50.2 us -> 7.94 us
  blocking collectives: 0 us -> 25.6 us
  other arithmetic: 24.3 us -> 14.2 us
  starting transfers between devices: 40.9 us -> 33.4 us
  Pallas kernels: 84.5 us -> 78.7 us
    all_to_all x3 -> x2, waiting for transfers between devices: 104 us -> 0.01 us  [exchange(): got = lax.all_to_all(x, 'head', 0, 0, tiled=True)]
    ppermute x11 -> x9, waiting for transfers between devices: 42.5 us -> 99.9 us  [swap(): return lax.ppermute(x, 'head', [(d, d ^ bit) for d in range(devices)])]
    all_to_all x0 -> x2, blocking collectives: none -> 25.6 us  [the longest x1 14.1 us: body(): pooled.append(lax.all_to_all(part, 'head', 0, 0, tiled=True))]
    pallas_call x2, Pallas kernels: 69.8 us -> 50.1 us  [attend(): pl.pallas_call(functools.partial(attend_kernel, min(512, length)), grid=(...]
    unnamed x64 -> x36, local copies, waits for them, and re-layouts: 20.6 us -> 1.99 us
    reshape x4 -> x1, local copies, waits for them, and re-layouts: 13.7 us -> 0.08 us  [body(): here = jnp.sum(valid.reshape(showers, each, POOL), axis=2)]
    concatenate x8 -> x5, other arithmetic: 19.3 us -> 9.62 us  [the longest x2 6.63 us: body(): jnp.concatenate(x, axis=0)]
    all_to_all x2 -> x1, waiting for transfers between devices: 15.5 us -> 6.97 us  [body(): pooled.append(lax.all_to_all(part, 'head', 0, 0, tiled=True))]
  transfers between devices with their start and end apart: 17 -> 13, of which waited for: 9 -> 7; matrix products, arithmetic and copies ran while one was open for 9% -> 8% of each run, Pallas kernels for 18% -> 17%
where the time goes in v2:
time: 291 us; the launch traced here: 290 us
  waiting for transfers between devices  127 us (44%)
  Pallas kernels  78.7 us (27%)
  starting transfers between devices  33.4 us (11%)
  blocking collectives  25.6 us (9%)
  other arithmetic  14.2 us (5%)
  local copies, waits for them, and re-layouts  7.94 us (3%)
    ppermute x9, waiting for transfers between devices, swap(): return lax.ppermute(x, 'head', [(d, d ^ bit) for d in range(devices)])  99.9 us
    pallas_call x2, Pallas kernels, attend(): pl.pallas_call(functools.partial(attend_kernel, min(512, length)), grid=(...  50.1 us
    all_to_all x1, waiting for transfers between devices, body(): lax.all_to_all(grads, 'head', 0, 0, axis_index_groups=lines, tiled=True)  20.4 us
    all_to_all x1, blocking collectives, body(): pooled.append(lax.all_to_all(part, 'head', 0, 0, tiled=True))  14.1 us
    all_to_all x2, starting transfers between devices, exchange(): got = lax.all_to_all(x, 'head', 0, 0, tiled=True)  12.8 us
    all_to_all x1, blocking collectives, body(): parts = lax.all_to_all(partial, 'head', 0, 0, tiled=True)  11.5 us
    ppermute x9, starting transfers between devices, swap(): return lax.ppermute(x, 'head', [(d, d ^ bit) for d in range(devices)])  10.8 us
    pallas_call x1, Pallas kernels, body(): pl.pallas_call(functools.partial(forward_kernel, [count * LANES for _, co...  10 us
  transfers between devices with their start and end apart: 13, of which 7 were waited for; matrix products, arithmetic and copies ran while one was open for 8% of the time, Pallas kernels for 17%

profile of v2, /device:TPU:0, one launch (start us, length us, event | category | flops | bytes accessed | tf_op | source)
XLA Modules:
  0.0 290.5 jit_solution(2715304303320517597)
XLA Ops:
  0.6 8.2 %pack.1 = (bf16[32,64,1152]{2,1,0:T(8,128)(2,1)}, bf16[32,64,384]{2,1,0:T(8,128)(2,1)}) custom-call(s32[8,64]{1,0:T(8,128)} %slot_ref.1, s32[8]{0:T(128)} %count_ref.1, bf16[8,64,2048]{2,1,0:T(8,128)(2,1)} %q_ref.1, bf16[8,64,2048]{2,1,0:T(8,128)(2,1)} %k_ref.1, bf16[8,64,2048]{2,1,0:T(8,128)(2,1)} %v_ref.1), custom_call_target="tpu_custom_call" | custom-call | tf_op jit(solution)/shard_map/pack/pallas_call | solution.py:285
  8.8 7.4 %all-to-all-start.1 = ((bf16[32,64,1152]{2,1,0:T(8,128)(2,1)}), bf16[32,64,1152]{2,1,0:T(8,128)(2,1)}, u32[]{:S(2)}, u32[]{:S(2)}) async-start(bf16[32,64,1152]{2,1,0:T(8,128)(2,1)} %get-tuple-element.54), calls=%async_computation.1 | async-start | bytes 9437184 | tf_op jit(solution)/shard_map/all_to_all | solution.py:309
  16.3 1.8 collective-permute-start
  18.3 68.0 %collective-permute-done = bf16[1,2048,256]{2,1,0:T(8,128)(2,1)S(1)} collective-permute-done((bf16[1,2048,256]{2,1,0:T(8,128)(2,1)S(1)}, bf16[1,2048,256]{2,1,0:T(8,128)(2,1)S(1)}, u32[]{:S(2)}, u32[]{:S(2)}) %collective-permute-start) | collective-permute-done | bytes 1048608 | tf_op jit(solution)/shard_map/ppermute | solution.py:281
  86.3 1.5 pad_maximum_fusion.2
  87.9 26.7 %collective-permute-done.2 = bf16[1,2048,256]{2,1,0:T(8,128)(2,1)S(1)} collective-permute-done((bf16[1,2048,256]{2,1,0:T(8,128)(2,1)}, bf16[1,2048,256]{2,1,0:T(8,128)(2,1)S(1)}, u32[]{:S(2)}, u32[]{:S(2)}) %collective-permute-start.2) | collective-permute-done | bytes 1048608 | tf_op jit(solution)/shard_map/ppermute | solution.py:281
  114.7 1.5 pad_maximum_fusion.3
  117.1 4.2 %collective-permute-start.6 = (f32[8,8,4]{2,1,0:T(8,128)S(1)}, f32[8,8,4]{2,1,0:T(8,128)S(1)}, u32[]{:S(2)}, u32[]{:S(2)}) collective-permute-start(f32[8,8,4]{2,1,0:T(8,128)S(1)} %broadcast_select_fusion), channel_id=1, source_target_pairs={{0,16},{1,17},{2,18},{3,19},{4,20},{5,21},{6,22},{7,23},{8,24},{9,... | collective-permute-start | bytes 3080 | tf_op jit(solution)/shard_map/ppermute | solution.py:281
  121.3 1.9 collective-permute-done.6
  123.2 1.9 collective-permute-start.7
  125.3 1.9 collective-permute-done.7
  127.3 2.3 collective-permute-start.8
  130.0 1.4 collective-permute-done.8
  131.5 5.4 %all-to-all-start = ((bf16[32,64,384]{2,1,0:T(8,128)(2,1)}), bf16[32,64,384]{2,1,0:T(8,128)(2,1)}, u32[]{:S(2)}, u32[]{:S(2)}) async-start(bf16[32,64,384]{2,1,0:T(8,128)(2,1)} %get-tuple-element.53), calls=%async_computation | async-start | bytes 3145728 | tf_op jit(solution)/shard_map/all_to_all | solution.py:309
  140.5 0.9 pad_maximum_fusion.4.refs_8_.dc_ref
  142.0 5.8 %pad_maximum_fusion = (bf16[4,2048,256]{2,1,0:T(8,128)(2,1)}, bf16[4,2048,256]{2,1,0:T(8,128)(2,1)}) fusion(bf16[2,2048,256]{2,1,0:T(8,128)(2,1)} %collective-permute-done.1, bf16[2,2048,256]{2,1,0:T(8,128)(2,1)} %pad_maximum_fusion.2, bf16[2,2048,256]{2,1,0:T(8,128)(2,1)} %collective-permute-done.3, bf16[2,2048,256]{2,1,0:T(8,128)(2,1)} %pad_maximum_fusion.3), kind=kLoop, calls=%fused_computation | loop fusion | flops 4194304 | bytes 16777216 | tf_op jit(solution)/shard_map/concatenate | solution.py:369
  147.8 36.7 %attend.2 = (bf16[8,64,2048]{2,1,0:T(8,128)(2,1)}, bf16[32,32,384]{2,1,0:T(8,128)(2,1)}) custom-call(bf16[2048,1152]{1,0:T(8,128)(2,1)} %bitcast.4.q_ref.k_ref.v_ref, bf16[2048,1152]{1,0:T(8,128)(2,1)} %bitcast.4.q_ref.k_ref.v_ref, bf16[2048,1152]{1,0:T(8,128)(2,1)} %bitcast.4.q_ref.k_ref.v_ref, bf16[128,2048]{1,0:T(8,128)(2,1)S(1)} %compare_convert_fusion.pool_ref), custom_call_target="tpu_custom_call" | custom-call | flops 6442450944 | bytes 6291456 | tf_op jit(solution)/shard_map/attend/pallas_call | solution.py:121
  185.9 6.1 %all-to-all-start.2 = ((bf16[32,32,384]{2,1,0:T(8,128)(2,1)}), bf16[32,32,384]{2,1,0:T(8,128)(2,1)}, u32[]{:S(2)}, u32[]{:S(2)}) async-start(bf16[32,32,384]{2,1,0:T(8,128)(2,1)} %get-tuple-element.66), calls=%async_computation.2 | async-start | bytes 1572864 | tf_op jit(solution)/shard_map/all_to_all | solution.py:384
  192.0 13.4 %attend.3 = (bf16[8,64,2048]{2,1,0:T(8,128)(2,1)}, bf16[32,32,128]{2,1,0:T(8,128)(2,1)S(1)}) custom-call(bf16[2048,384]{1,0:T(8,128)(2,1)} %bitcast.3.q_ref.k_ref.v_ref, bf16[2048,384]{1,0:T(8,128)(2,1)} %bitcast.3.q_ref.k_ref.v_ref, bf16[2048,384]{1,0:T(8,128)(2,1)} %bitcast.3.q_ref.k_ref.v_ref, ...), custom_call_target="tpu_custom_call", output_to_operand_aliasing={{0}: (4, {})} | custom-call | flops 2147483648 | bytes 2097152 | tf_op jit(solution)/shard_map/attend/pallas_call | solution.py:121
  205.4 7.0 %all-to-all-done.2.refs_0_ = bf16[32,32,384]{2,1,0:T(8,128)(2,1)} async-done(((bf16[32,32,384]{2,1,0:T(8,128)(2,1)}), bf16[32,32,384]{2,1,0:T(8,128)(2,1)}, u32[]{:S(2)}, u32[]{:S(2)}) %all-to-all-start.2) | async-done | bytes 786464 | tf_op jit(solution)/shard_map/all_to_all | solution.py:384
  212.4 14.1 %all_to_all.30.refs_1_ = bf16[32,32,128]{2,1,0:T(8,128)(2,1)} all-to-all(bf16[32,32,128]{2,1,0:T(8,128)(2,1)S(1)} %get-tuple-element.68), channel_id=1, replica_groups=mesh['parts'=1,'head'=32] {'head'}, dimensions={0} | all-to-all | bytes 524288 | tf_op jit(solution)/shard_map/all_to_all | solution.py:384
  226.5 10.0 %classifier_forward.1 = (f32[32,8,128]{2,1,0:T(8,128)}, f32[4,256,256]{2,1,0:T(8,128)}, f32[4,256,256]{2,1,0:T(8,128)}, f32[32,2048]{1,0:T(8,128)}) custom-call(s32[1]{0:T(128)} %bitcast.6.own_ref, bf16[32,32,384]{2,1,0:T(8,128)(2,1)} %all-to-all-done.2.refs_0_, bf16[32,32,128]{2,1,0:T(8,128)(2,1)} %all_to_all.30.refs_1_, bf16[256,256]{1,0:T(8,128)(2,1)} %fusion.refs_2_, ...), custom_call_target="tpu_custom_call" | custom-call | tf_op jit(solution)/shard_map/classifier_forward/pallas_call | solution.py:396
  236.5 11.5 %all_to_all.31.parts_ref = f32[32,8,128]{2,1,0:T(8,128)} all-to-all(f32[32,8,128]{2,1,0:T(8,128)} %get-tuple-element.80), channel_id=1, replica_groups=mesh['parts'=1,'head'=32] {'head'}, dimensions={0} | all-to-all | bytes 262144 | tf_op jit(solution)/shard_map/all_to_all | solution.py:425
  248.0 9.5 %classifier_backward.1 = (bf16[8,32,2048]{2,1,0:T(8,128)(2,1)}, f32[8,128]{1,0:T(8,128)}) custom-call(f32[32,8,128]{2,1,0:T(8,128)} %all_to_all.31.parts_ref, f32[8,128]{1,0:T(8,128)} %broadcast_in_dim.104.counts_ref, f32[1,128]{1,0:T(1,128)} %bitcast.21, f32[8,128]{1,0:T(8,128)} %fusion.12.target_ref, f32[32,8]{1,0:T(8,128)} %constant.58.clone.spread_ref, ...), custom_call_target="tpu_custom_call" | custom-call | tf_op jit(solution)/shard_map/classifier_backward/pallas_call | solution.py:426
  257.5 3.7 %all-to-all-start.5 = ((bf16[8,32,2048]{2,1,0:T(8,128)(2,1)}), bf16[8,32,2048]{2,1,0:T(8,128)(2,1)S(1)}, u32[]{:S(2)}, u32[]{:S(2)}) async-start(bf16[8,32,2048]{2,1,0:T(8,128)(2,1)} %get-tuple-element.87), calls=%async_computation.5 | async-start | bytes 2097152 | tf_op jit(solution)/shard_map/all_to_all | solution.py:445
  261.3 1.6 fusion.15
  263.7 1.7 mul.37
  265.4 1.7 broadcast_multiply_fusion.dy_ref
  267.1 20.4 %all-to-all-done.5.dn_ref = bf16[8,32,2048]{2,1,0:T(8,128)(2,1)S(1)} async-done(((bf16[8,32,2048]{2,1,0:T(8,128)(2,1)}), bf16[8,32,2048]{2,1,0:T(8,128)(2,1)S(1)}, u32[]{:S(2)}, u32[]{:S(2)}) %all-to-all-start.5) | async-done | bytes 1048608 | tf_op jit(solution)/shard_map/all_to_all | solution.py:445
  287.5 0.9 copy-done.2
  288.5 0.9 copy-done.3
  289.4 1.0 norm_backward.1
  (79 shorter events, 8.7 us)
Async XLA Ops:
  0.6 129.0 %copy-start = (bf16[256,4096]{1,0:T(8,128)(2,1)S(1)}, bf16[256,4096]{1,0:T(8,128)(2,1)}, u32[]{:S(2)}) copy-start(bf16[256,4096]{1,0:T(8,128)(2,1)} %param.26) | copy-start | bytes 6291460
  8.8 7.4 %copy-start.7 = (bf16[2048,256]{1,0:T(8,128)(2,1)S(1)}, bf16[2048,256]{1,0:T(8,128)(2,1)}, u32[]{:S(2)}) copy-start(bf16[2048,256]{1,0:T(8,128)(2,1)} %param.28) | copy-start | bytes 3145732
  8.8 122.7 %all-to-all-start.1 = ((bf16[32,64,1152]{2,1,0:T(8,128)(2,1)}), bf16[32,64,1152]{2,1,0:T(8,128)(2,1)}, u32[]{:S(2)}, u32[]{:S(2)}) async-start(bf16[32,64,1152]{2,1,0:T(8,128)(2,1)} %get-tuple-element.54), calls=%async_computation.1 | async-start | bytes 9437184 | tf_op jit(solution)/shard_map/all_to_all | solution.py:309
  16.3 70.1 %collective-permute-start = (bf16[1,2048,256]{2,1,0:T(8,128)(2,1)S(1)}, bf16[1,2048,256]{2,1,0:T(8,128)(2,1)S(1)}, u32[]{:S(2)}, u32[]{:S(2)}) collective-permute-start(bf16[1,2048,256]{2,1,0:T(8,128)(2,1)S(1)} %bitcast.17), channel_id=1, source_target_pairs={{0,2},{1,3},{2,0},{3,1},{4,6},{5,7},{6,4},{7,5},{8,10},{9,11},{10,... | collective-permute-start | bytes 3145736 | tf_op jit(solution)/shard_map/ppermute | solution.py:281
  18.0 96.6 %copy-start.8 = (bf16[2048,256]{1,0:T(8,128)(2,1)S(1)}, bf16[2048,256]{1,0:T(8,128)(2,1)}, u32[]{:S(2)}) copy-start(bf16[2048,256]{1,0:T(8,128)(2,1)} %param.29) | copy-start | bytes 3145732
  18.0 96.6 %collective-permute-start.2 = (bf16[1,2048,256]{2,1,0:T(8,128)(2,1)}, bf16[1,2048,256]{2,1,0:T(8,128)(2,1)S(1)}, u32[]{:S(2)}, u32[]{:S(2)}) collective-permute-start(bf16[1,2048,256]{2,1,0:T(8,128)(2,1)} %bitcast.19), channel_id=1, source_target_pairs={{0,2},{1,3},{2,0},{3,1},{4,6},{5,7},{6,4},{7,5},{8,10},{9,11},{10,... | collective-permute-start | bytes 3145736 | tf_op jit(solution)/shard_map/ppermute | solution.py:281
  87.8 28.3 %copy-start.5 = (bf16[2048,128]{1,0:T(8,128)(2,1)S(1)}, bf16[2048,128]{1,0:T(8,128)(2,1)}, u32[]{:S(2)}) copy-start(bf16[2048,128]{1,0:T(8,128)(2,1)} %refs_12_) | copy-start | bytes 1572868
  87.8 28.3 %copy-start.6 = (bf16[256,2048]{1,0:T(8,128)(2,1)S(1)}, bf16[256,2048]{1,0:T(8,128)(2,1)}, u32[]{:S(2)}) copy-start(bf16[256,2048]{1,0:T(8,128)(2,1)} %param.30) | copy-start | bytes 3145732
  87.8 28.9 %copy-start.9 = (s32[8,64]{1,0:T(8,128)S(1)}, s32[8,64]{1,0:T(8,128)}, u32[]{:S(2)}) copy-start(s32[8,64]{1,0:T(8,128)} %slot_ref.1) | copy-start | bytes 6148
  87.8 28.9 %copy-start.11 = (s32[8]{0:T(128)S(1)}, s32[8]{0:T(128)}, u32[]{:S(2)}) copy-start(s32[8]{0:T(128)} %count_ref.1) | copy-start | bytes 100
  87.9 33.4 %copy-start.17 = (s32[8]{0:T(128)S(1)}, s32[8]{0:T(128)}, u32[]{:S(2)}) copy-start(s32[8]{0:T(128)} %param.24) | copy-start | bytes 100
  87.9 43.6 %collective-permute-start.1 = (bf16[2,2048,256]{2,1,0:T(8,128)(2,1)}, bf16[2,2048,256]{2,1,0:T(8,128)(2,1)}, u32[]{:S(2)}, u32[]{:S(2)}) collective-permute-start(bf16[2,2048,256]{2,1,0:T(8,128)(2,1)} %pad_maximum_fusion.2), channel_id=1, source_target_pairs={{0,1},{1,0},{2,3},{3,2},{4,5},{5,4},{6,7},{7,6},{8,9},{9,8},{10,11... | collective-permute-start | bytes 6291464 | tf_op jit(solution)/shard_map/ppermute | solution.py:281
  116.1 15.4 %collective-permute-start.3 = (bf16[2,2048,256]{2,1,0:T(8,128)(2,1)}, bf16[2,2048,256]{2,1,0:T(8,128)(2,1)}, u32[]{:S(2)}, u32[]{:S(2)}) collective-permute-start(bf16[2,2048,256]{2,1,0:T(8,128)(2,1)} %pad_maximum_fusion.3), channel_id=1, source_target_pairs={{0,1},{1,0},{2,3},{3,2},{4,5},{5,4},{6,7},{7,6},{8,9},{9,8},{10,11... | collective-permute-start | bytes 6291464 | tf_op jit(solution)/shard_map/ppermute | solution.py:281
  116.6 13.0 %collective-permute-start.4 = (f32[1,256,128]{2,1,0:T(8,128)S(1)}, f32[1,256,128]{2,1,0:T(8,128)S(1)}, u32[]{:S(2)}, u32[]{:S(2)}) collective-permute-start(f32[1,256,128]{2,1,0:T(8,128)S(1)} %convolution_bitcast_fusion), channel_id=1, source_target_pairs={{0,2},{1,3},{2,0},{3,1},{4,6},{5,7},{6,4},{7,5},{8,10},{9,11},{10,... | collective-permute-start | bytes 393224 | tf_op jit(solution)/shard_map/ppermute | solution.py:281
  117.1 6.1 %collective-permute-start.6 = (f32[8,8,4]{2,1,0:T(8,128)S(1)}, f32[8,8,4]{2,1,0:T(8,128)S(1)}, u32[]{:S(2)}, u32[]{:S(2)}) collective-permute-start(f32[8,8,4]{2,1,0:T(8,128)S(1)} %broadcast_select_fusion), channel_id=1, source_target_pairs={{0,16},{1,17},{2,18},{3,19},{4,20},{5,21},{6,22},{7,23},{8,24},{9,... | collective-permute-start | bytes 3080 | tf_op jit(solution)/shard_map/ppermute | solution.py:281
  123.2 4.0 %collective-permute-start.7 = (f32[8,8,4]{2,1,0:T(8,128)S(1)}, f32[8,8,4]{2,1,0:T(8,128)S(1)}, u32[]{:S(2)}, u32[]{:S(2)}) collective-permute-start(f32[8,8,4]{2,1,0:T(8,128)S(1)} %fusion.1), channel_id=1, source_target_pairs={{0,8},{1,9},{2,10},{3,11},{4,12},{5,13},{6,14},{7,15},{8,0},{9,1},... | collective-permute-start | bytes 3080 | tf_op jit(solution)/shard_map/ppermute | solution.py:281
  127.3 4.2 %collective-permute-start.8 = (f32[8,8,4]{2,1,0:T(8,128)S(1)}, f32[8,8,4]{2,1,0:T(8,128)S(1)}, u32[]{:S(2)}, u32[]{:S(2)}) collective-permute-start(f32[8,8,4]{2,1,0:T(8,128)S(1)} %fusion.21), channel_id=1, source_target_pairs={{0,4},{1,5},{2,6},{3,7},{4,0},{5,1},{6,2},{7,3},{8,12},{9,13},{10,... | collective-permute-start | bytes 3080 | tf_op jit(solution)/shard_map/ppermute | solution.py:281
  129.6 1.9 collective-permute-start.5
  131.4 7.2 %copy-start.14 = (s32[256]{0:T(256)S(1)}, s32[256]{0:T(256)}, u32[]{:S(2)}) copy-start(s32[256]{0:T(256)} %constant.56.clone) | copy-start | bytes 3076
  131.4 7.2 %copy-start.16 = (s32[8]{0:T(128)S(1)}, s32[8]{0:T(128)}, u32[]{:S(2)}) copy-start(s32[8]{0:T(128)} %param.25) | copy-start | bytes 100
  131.4 7.9 %copy-start.12 = (s32[256]{0:T(256)S(1)}, s32[256]{0:T(256)}, u32[]{:S(2)}) copy-start(s32[256]{0:T(256)} %constant.57.clone) | copy-start | bytes 3076
  131.5 8.6 %copy-start.15 = (s32[128]{0:T(128)S(1)}, s32[128]{0:T(128)}, u32[]{:S(2)}) copy-start(s32[128]{0:T(128)} %constant.54.clone) | copy-start | bytes 1540
  131.5 54.3 %all-to-all-start = ((bf16[32,64,384]{2,1,0:T(8,128)(2,1)}), bf16[32,64,384]{2,1,0:T(8,128)(2,1)}, u32[]{:S(2)}, u32[]{:S(2)}) async-start(bf16[32,64,384]{2,1,0:T(8,128)(2,1)} %get-tuple-element.53), calls=%async_computation | async-start | bytes 3145728 | tf_op jit(solution)/shard_map/all_to_all | solution.py:309
  136.9 4.5 %copy-start.13 = (s32[256]{0:T(256)S(1)}, s32[256]{0:T(256)}, u32[]{:S(2)}) copy-start(s32[256]{0:T(256)} %constant.55.clone) | copy-start | bytes 3076
  185.9 26.5 %all-to-all-start.2 = ((bf16[32,32,384]{2,1,0:T(8,128)(2,1)}), bf16[32,32,384]{2,1,0:T(8,128)(2,1)}, u32[]{:S(2)}, u32[]{:S(2)}) async-start(bf16[32,32,384]{2,1,0:T(8,128)(2,1)} %get-tuple-element.66), calls=%async_computation.2 | async-start | bytes 1572864 | tf_op jit(solution)/shard_map/all_to_all | solution.py:384
  257.5 3.9 %copy-start.10 = (f32[8,128]{1,0:T(8,128)S(1)}, f32[8,128]{1,0:T(8,128)}, u32[]{:S(2)}) copy-start(f32[8,128]{1,0:T(8,128)} %get-tuple-element.89) | copy-start | bytes 12292
  257.5 30.1 %copy-start.1 = (f32[32,2048]{1,0:T(8,128)S(1)}, f32[32,2048]{1,0:T(8,128)}, u32[]{:S(2)}) copy-start(f32[32,2048]{1,0:T(8,128)} %reshape.119.refs_4_.scale_ref) | copy-start | bytes 786436
  257.5 30.1 %copy-start.4 = (f32[2048]{0:T(1024)S(1)}, f32[2048]{0:T(1024)}, u32[]{:S(2)}) copy-start(f32[2048]{0:T(1024)} %param.27) | copy-start | bytes 24580
  257.5 30.1 %all-to-all-start.5 = ((bf16[8,32,2048]{2,1,0:T(8,128)(2,1)}), bf16[8,32,2048]{2,1,0:T(8,128)(2,1)S(1)}, u32[]{:S(2)}, u32[]{:S(2)}) async-start(bf16[8,32,2048]{2,1,0:T(8,128)(2,1)} %get-tuple-element.87), calls=%async_computation.5 | async-start | bytes 2097152 | tf_op jit(solution)/shard_map/all_to_all | solution.py:445
  287.5 1.0 copy-start.2
  288.5 0.9 copy-start.3

commit v3 on v2

v3 whole, which is shorter than its diff:
```python
import functools
import math

import jax
import jax.numpy as jnp
import numpy as np
from jax import lax
from jax.experimental import pallas as pl
from jax.experimental.pallas import tpu as pltpu
from jax.sharding import PartitionSpec as P

HEADS = 32
POOL = 16
LANES = 128
MASKED = -1e30
HEAD = 16
TEAMS = 8
ABSENT = 64.0
epsilon = 1e-06
HIGH = lax.Precision.HIGHEST
NT = (((1,), (1,)), ((), ()))
TN = (((0,), (0,)), ((), ()))
NN = (((1,), (0,)), ((), ()))
MIB = 1 << 20


def mm(a, b, dims=NN, precision=None):
    return lax.dot_general(a, b, dims, precision=precision, preferred_element_type=jnp.float32)


def sinusoid(steps, embed_width):
    half_width = embed_width // 2
    frequency = jnp.exp(-math.log(10000.0) * jnp.arange(half_width, dtype=jnp.float32) / half_width)
    angles = steps.astype(jnp.float32)[:, None] * frequency[None, :]
    return jnp.concatenate([jnp.cos(angles), jnp.sin(angles)], axis=1)


def pack_kernel(first, count, slot_ref, count_ref, q_ref, k_ref, v_ref, out):
    shower = pl.program_id(0)
    group = out.shape[0]
    local = q_ref.shape[1]
    features = q_ref.shape[2] // group
    size = count * LANES
    valid = (slot_ref[pl.ds(shower, 1), :] < count_ref[shower]).astype(jnp.float32)
    square = (local, local)
    diagonal = lax.broadcasted_iota(jnp.int32, square, 0) == lax.broadcasted_iota(
        jnp.int32, square, 1
    )
    column = jnp.sum(jnp.where(diagonal, valid, 0.0), axis=1, keepdims=True) > 0.5
    for m in range(group):
        at = m * features + first * LANES
        for t, ref in enumerate((q_ref, k_ref, v_ref)):
            part = ref[0, :, at : at + size]
            if t == 1:
                part = jnp.where(column, part, jnp.asarray(ABSENT, part.dtype))
            out[m, :, t * size : (t + 1) * size] = part


def pack(slot_positions, counts, queries, keys, values, first, count, devices):
    showers, local, width = queries.shape
    group = devices // showers
    return pl.pallas_call(
        functools.partial(pack_kernel, first, count),
        grid=(showers,),
        out_shape=jax.ShapeDtypeStruct((devices, local, 3 * count * LANES), jnp.bfloat16),
        in_specs=[
            pl.BlockSpec((showers, local), lambda s: (0, 0)),
            pl.BlockSpec(memory_space=pltpu.SMEM),
        ]
        + [pl.BlockSpec((1, local, width), lambda s: (s, 0, 0))] * 3,
        out_specs=pl.BlockSpec((group, local, 3 * count * LANES), lambda s: (s, 0, 0)),
        compiler_params=pltpu.CompilerParams(vmem_limit_bytes=58 * MIB),
        name="pack",
    )(slot_positions, counts, queries, keys, values)


def attend_kernel(block, head, q_ref, k_ref, v_ref, pool_ref, *rest):
    att_ref, pooled_ref = rest[-2:]
    length = q_ref.shape[0]
    half = LANES // 2
    lane = lax.broadcasted_iota(jnp.int32, (1, LANES), 1)
    low = lane < half
    keys = k_ref[...]
    rows = v_ref[...]
    one = jnp.ones_like(rows)
    present = jnp.where(keys.astype(jnp.float32) < 0.5 * ABSENT, 1.0, 0.0).astype(jnp.bfloat16)
    pick = jnp.broadcast_to(jnp.where(lane == 0, 1.0, 0.0).astype(jnp.bfloat16), (8, LANES))
    valid = mm(pick, present, NT)[:1]
    bias = jnp.where(valid > 0.5, 0.0, MASKED)
    values = (jnp.where(low, rows, one), jnp.where(low, one, rows))

    for i in range(length // block):
        at = slice(i * block, (i + 1) * block)
        query = q_ref[at, :] * jnp.asarray(0.125, jnp.bfloat16)
        zero = jnp.zeros_like(query)
        outs = []
        for h in range(2):
            own = jnp.where(low, query, zero) if h == 0 else jnp.where(low, zero, query)
            scores = mm(own, keys, NT) + bias
            peak = jnp.max(scores, axis=1, keepdims=True)
            weights = jnp.exp(scores - peak).astype(jnp.bfloat16)
            outs.append(mm(weights, values[h]))
        top = jnp.where(low, outs[0], outs[1])
        total = jnp.where(low, pltpu.roll(outs[0], half, 1), pltpu.roll(outs[1], half, 1))
        mixed = ((top / total).T * valid[:, at]).astype(jnp.bfloat16)
        att_ref[0, :, at] = mixed[:half]
        att_ref[1, :, at] = mixed[half:]
    both = jnp.concatenate([att_ref[0], att_ref[1]], axis=0)
    cnt = mm(pool_ref[...], jnp.broadcast_to(valid, (LANES, length)).astype(jnp.bfloat16), NT)
    pooled = (mm(pool_ref[...], both, NT) / jnp.maximum(cnt, 1.0)).astype(jnp.bfloat16)
    rows = pooled_ref.shape[1] - head
    team = pooled.shape[0] // rows
    if head:
        ones = jnp.broadcast_to(valid, (head, length)).astype(jnp.bfloat16)
        counted = mm(ones, pool_ref[...], NT).astype(jnp.bfloat16)
    for d in range(pooled_ref.shape[0]):
        m = d % team
        pooled_ref[d, head:] = pooled[m * rows : (m + 1) * rows]
        if head:
            pooled_ref[d, :head] = counted


def attend(qkv, pool, first, count, pairs, devices, rows, head, before):
    length = qkv.shape[0]
    windows = pool.shape[0]
    head_dim = LANES // 2

    def part(which):
        return pl.BlockSpec((length, LANES), lambda j: (0, which * count + j))

    def whole(shape):
        return pl.BlockSpec(shape, lambda j: (0, 0))

    in_specs = [
        part(0),
        part(1),
        part(2),
        whole((windows, length)),
    ]
    operands = [qkv, qkv, qkv, pool]
    aliases = {}
    if before is not None:
        in_specs.append(pl.BlockSpec(memory_space=pl.ANY))
        operands.append(before)
        aliases = {4: 0}
    return pl.pallas_call(
        functools.partial(attend_kernel, min(512, length), head),
        grid=(count,),
        out_shape=(
            jax.ShapeDtypeStruct((pairs, head_dim, length), jnp.bfloat16),
            jax.ShapeDtypeStruct((devices, head + rows, count * LANES), jnp.bfloat16),
        ),
        in_specs=in_specs,
        out_specs=(
            pl.BlockSpec((2, head_dim, length), lambda j: (first + j, 0, 0)),
            pl.BlockSpec((devices, head + rows, LANES), lambda j: (0, 0, j)),
        ),
        input_output_aliases=aliases,
        compiler_params=pltpu.CompilerParams(vmem_limit_bytes=40 * MIB),
        cost_estimate=pl.CostEstimate(
            flops=count * 2 * 4 * length * length * head_dim,
            bytes_accessed=count * length * LANES * 8,
            transcendentals=count * 2 * length * length,
        ),
        name="attend",
    )(*operands)


def forward_kernel(lanes, team, rows, place_ref, *refs):
    n = len(lanes)
    inputs = n + 6 + 3 * team
    sources, (copies_ref, ga_out, aa_out, own_x_ref) = refs[:inputs], refs[inputs : inputs + 4]
    buffers = refs[inputs + 4 : 2 * inputs + 4]
    gathered, normed, counted, ga_ref, aa_ref, sems, out_sems = refs[2 * inputs + 4 :]
    arriving = [
        pltpu.make_async_copy(source, buffer, sems.at[i])
        for i, (source, buffer) in enumerate(zip(sources, buffers))
    ]
    for copy in arriving:
        copy.start()

    def get(i):
        arriving[i].wait()
        return buffers[i]

    showers = copies_ref.shape[1]
    group = buffers[0].shape[0] // showers
    width = gathered.shape[1]
    block = own_x_ref.shape[0]
    total = rows * showers
    x_refs = [get(i) for i in range(n)]
    for s in range(showers):
        for m in range(group):
            at = m * (width // group)
            for ref, size in zip(x_refs, lanes):
                part = ref[s * group + m, ref.shape[1] - rows :]
                gathered[s * rows : (s + 1) * rows, at : at + size] = part.astype(jnp.float32)
                at += size
    packed = gathered[...].astype(jnp.bfloat16)
    perm_ref, gain_ref, scale_ref, shift_ref = [get(n + i) for i in range(4)]
    gathered[...] = mm(perm_ref[...], packed)
    for b in range(total // block):
        at = slice(b * block, (b + 1) * block)
        x = gathered[at]
        inverse = lax.rsqrt(jnp.mean(x * x, axis=1, keepdims=True) + epsilon)
        normed[at] = (x * inverse * gain_ref[...] * scale_ref[...] + shift_ref[...]).astype(
            jnp.bfloat16
        )
    own_x_ref[...] = gathered[pl.ds(pl.multiple_of(place_ref[0] * block, block), block), :]
    counts_ref, class_ref = [get(n + 4 + i) for i in range(2)]
    counted[...] = jnp.zeros(counted.shape, jnp.float32)
    for s in range(showers):
        counted[s : s + 1] = x_refs[-1][s * group, :HEAD].astype(jnp.float32)[:1]
    shape = (total, LANES)
    row = lax.broadcasted_iota(jnp.int32, shape, 0)
    lane = lax.broadcasted_iota(jnp.int32, shape, 1)
    each = block // showers
    from_lane = place_ref[1] * rows + row // block * each + row % each
    pick = jnp.where(lane == from_lane, 1.0, 0.0).astype(jnp.bfloat16)
    cnt_of = mm(pick, counted[...].astype(jnp.bfloat16), NT)
    cnt_of = jnp.where(lane == row % block // each, cnt_of, 0.0)
    cnt = jnp.sum(cnt_of, axis=1, keepdims=True)
    own_cnt_of = jnp.where(row // block == place_ref[0], cnt_of, 0.0).astype(jnp.bfloat16)
    cnt_of = cnt_of.astype(jnp.bfloat16)
    sums = mm(own_cnt_of, gathered[...].astype(jnp.bfloat16), TN)[:showers]
    logits = mm(sums, class_ref[...].astype(jnp.float32), precision=HIGH)
    coef = cnt / counts_ref[...][:, :1]
    leaving = []
    for i in range(team):
        gate_ref, up_ref, map_ref = [get(n + 6 + 3 * i + j) for j in range(3)]
        gate = mm(normed[...], gate_ref[...])
        up = mm(normed[...], up_ref[...])
        sigma = jax.nn.sigmoid(gate)
        activated = gate * sigma
        hidden = (activated * up).astype(jnp.bfloat16)
        logits = logits + mm(mm(cnt_of, hidden, TN)[:showers], map_ref[...], precision=HIGH)
        ga_ref[i] = coef * (up * sigma * (1.0 + gate * (1.0 - sigma)))
        aa_ref[i] = coef * activated
        for j, (kept, out) in enumerate(((ga_ref, ga_out), (aa_ref, aa_out))):
            copy = pltpu.make_async_copy(kept.at[i], out.at[i], out_sems.at[2 * i + j])
            copy.start()
            leaving.append(copy)
    for d in range(copies_ref.shape[0]):
        copies_ref[d] = logits
    for copy in leaving:
        copy.wait()


def backward_kernel(team, parts_ref, counts_ref, bias_ref, target_ref, spread_ref, *refs):
    sources = refs[: 3 * team]
    ga_in, aa_in, dn_ref, miss_ref = refs[3 * team : 3 * team + 4]
    buffers = refs[3 * team + 4 : 6 * team + 4]
    ga_ref, aa_ref, total, sems = refs[6 * team + 4 :]
    arriving = []
    for i in range(team):
        pairs = [(sources[3 * i + 2], buffers[3 * i + 2]), (ga_in.at[i], ga_ref.at[i])]
        pairs += [(aa_in.at[i], aa_ref.at[i])]
        pairs += [(sources[3 * i + j], buffers[3 * i + j]) for j in range(2)]
        arriving.append(
            [
                pltpu.make_async_copy(source, buffer, sems.at[5 * i + j])
                for j, (source, buffer) in enumerate(pairs)
            ]
        )
        for copy in arriving[-1]:
            copy.start()
    blocks, block, _ = dn_ref.shape
    logits = jnp.sum(parts_ref[...], axis=0) / counts_ref[...] + bias_ref[...]
    exponent = jnp.exp(logits - jnp.max(logits, axis=1, keepdims=True))
    miss = target_ref[...] - exponent / jnp.sum(exponent, axis=1, keepdims=True)
    miss_ref[...] = miss
    spread = mm(spread_ref[...], miss, precision=HIGH)
    for i in range(team):
        gate_ref, up_ref, map_ref = buffers[3 * i : 3 * i + 3]
        for copy in arriving[i]:
            copy.wait()
        wide = mm(spread, map_ref[...], NT, HIGH)
        wide = jnp.concatenate([wide] * blocks, axis=0)
        gate_grad = (wide * ga_ref[i]).astype(jnp.bfloat16)
        up_grad = (wide * aa_ref[i]).astype(jnp.bfloat16)
        term = mm(gate_grad, gate_ref[...], NT) + mm(up_grad, up_ref[...], NT)
        if i == 0:
            total[...] = term
        elif i < team - 1:
            total[...] += term
        else:
            term = (total[...] + term).astype(jnp.bfloat16)
            for b in range(blocks):
                dn_ref[b] = term[b * block : (b + 1) * block]


def final_kernel(windows, dn_ref, x_ref, gain_ref, scale_ref, dy_ref, out_ref):
    total = dn_ref[0].astype(jnp.float32)
    for b in range(1, dn_ref.shape[0]):
        total = total + dn_ref[b].astype(jnp.float32)
    x = x_ref[...]
    inverse = lax.rsqrt(jnp.mean(x * x, axis=1, keepdims=True) + epsilon)
    unit = x * inverse
    grad = total * gain_ref[...] * scale_ref[...]
    back = inverse * (grad - unit * jnp.mean(grad * unit, axis=1, keepdims=True))
    value = windows * (dy_ref[...] + back)
    each = out_ref.shape[1]
    for s in range(out_ref.shape[0]):
        out_ref[s] = value[s * each : (s + 1) * each]


def body(
    queries,
    keys,
    values,
    slot_positions,
    counts,
    timesteps,
    labels,
    time_weight,
    norm_gain,
    gate_weight,
    up_weight,
    down_weight,
    class_weight,
    class_bias,
):
    devices = lax.axis_size("head")
    me = lax.axis_index("head")
    showers, local, width = queries.shape
    length = local * devices
    group = devices // showers
    team = devices // TEAMS
    outer = TEAMS
    features = width // group
    slabs = features // LANES
    each = local // POOL
    windows = length // POOL
    classes = class_weight.shape[1]
    placed = me // team
    rows = outer * each
    block = showers * each
    total = showers * rows

    def swap(x, bit):
        return lax.ppermute(x, "head", [(d, d ^ bit) for d in range(devices)])

    chunks = [(0, slabs - 1), (slabs - 1, 1)] if slabs > 1 else [(0, 1)]

    valid = (slot_positions < counts[:, None]).astype(jnp.float32)
    here = jnp.sum(valid.reshape(block, POOL), axis=1, keepdims=True)
    here = jnp.broadcast_to(here, (block, LANES))

    tokens = (slot_positions, counts, queries, keys, values)
    sent = pack(*tokens, *chunks[0], devices)

    def exchange(x):
        got = lax.all_to_all(x, "head", 0, 0, tiled=True)
        return got.reshape(length, x.shape[2])

    received = [exchange(sent)]

    order = np.arange(windows).reshape(outer, team, each).transpose(1, 0, 2).reshape(windows)
    pool = jnp.asarray(order, jnp.int32)[:, None] == jnp.arange(length, dtype=jnp.int32)[None] // POOL
    pool = pool.astype(jnp.bfloat16)

    shower_counts = counts.astype(jnp.float32)
    row_counts = jnp.tile(jnp.repeat(shower_counts, each), outer)
    row_counts = jnp.broadcast_to(row_counts[:, None], (total, LANES))
    source = np.arange(total).reshape(showers, outer, each).transpose(1, 0, 2).reshape(total)
    perm = jnp.asarray(source, jnp.int32)[:, None] == jnp.arange(total, dtype=jnp.int32)[None]
    perm = perm.astype(jnp.bfloat16)
    embedding = sinusoid(timesteps, time_weight.shape[0]).astype(jnp.bfloat16)
    modulation = jnp.dot(embedding, time_weight, preferred_element_type=jnp.float32)
    shifts = jnp.repeat(modulation[:, :width], each, axis=0)
    scales = jnp.repeat(1.0 + modulation[:, width:], each, axis=0)
    gain = norm_gain.reshape(1, width)

    target = (labels[:, None] == jnp.arange(classes, dtype=jnp.int32)[None]).astype(jnp.float32)
    spread = jnp.asarray(
        np.repeat(np.eye(showers), each, axis=0).astype(np.float32)
    )
    spread_counts = jnp.broadcast_to(shower_counts[:, None], (showers, classes))
    heads_in = (spread_counts, class_bias.reshape(1, classes), target, spread)
    fixed = (perm, gain, scales, shifts)
    late = (row_counts, class_weight)
    def gather(x):
        found = {0: x}
        bit = team // 2
        while bit:
            found.update({m ^ bit: swap(piece, bit) for m, piece in found.items()})
            bit //= 2
        return [found[m] for m in range(team)]

    class_map = jnp.dot(down_weight, class_weight, preferred_element_type=jnp.float32)
    up_weight, class_map, fixed, late, heads_in, pool = lax.optimization_barrier(
        (up_weight, class_map, fixed, late, heads_in, pool)
    )
    class_map = gather(class_map)
    gates = gather(gate_weight)
    ups = gather(up_weight)
    sent, gates, ups, class_map = lax.optimization_barrier(
        ([pack(*tokens, *chunk, devices) for chunk in chunks[1:]], gates, ups, class_map)
    )
    received += [exchange(x) for x in sent]

    attention = None
    pooled = []
    for qkv, (first, count) in zip(received, chunks):
        head = HEAD if first + count == slabs else 0
        attention, part = attend(
            qkv, pool, first, count, 2 * slabs, devices, rows, head, attention
        )
        if pooled:
            part, pooled[-1] = lax.optimization_barrier((part, pooled[-1]))
        pooled.append(lax.all_to_all(part, "head", 0, 0, tiled=True))

    units = gate_weight.shape[1]

    inside = pl.BlockSpec(memory_space=pltpu.VMEM)
    outside = pl.BlockSpec(memory_space=pl.ANY)
    side = jax.ShapeDtypeStruct((team, total, units), jnp.float32)
    members = [x for member in zip(gates, ups, class_map) for x in member]
    operands = [*pooled, *fixed, *late, *members]

    def buffers(xs):
        return [pltpu.VMEM(x.shape, x.dtype) for x in xs]

    partial, gate_side, up_side, own_x = pl.pallas_call(
        functools.partial(forward_kernel, [count * LANES for _, count in chunks], team, rows),
        out_shape=(
            jax.ShapeDtypeStruct((devices, showers, classes), jnp.float32),
            side,
            side,
            jax.ShapeDtypeStruct((block, width), jnp.float32),
        ),
        in_specs=[pl.BlockSpec(memory_space=pltpu.SMEM)] + [outside] * len(operands),
        out_specs=(inside, outside, outside, inside),
        scratch_shapes=buffers(operands)
        + [
            pltpu.VMEM((total, width), jnp.float32),
            pltpu.VMEM((total, width), jnp.bfloat16),
            pltpu.VMEM((LANES, LANES), jnp.float32),
            pltpu.VMEM(side.shape, side.dtype),
            pltpu.VMEM(side.shape, side.dtype),
            pltpu.SemaphoreType.DMA((len(operands),)),
            pltpu.SemaphoreType.DMA((2 * team,)),
        ],
        compiler_params=pltpu.CompilerParams(vmem_limit_bytes=58 * MIB),
        name="classifier_forward",
    )(jnp.stack([placed, me % team]).astype(jnp.int32), *operands)

    parts = lax.all_to_all(partial, "head", 0, 0, tiled=True)
    grads, miss = pl.pallas_call(
        functools.partial(backward_kernel, team),
        out_shape=(
            jax.ShapeDtypeStruct((outer, block, width), jnp.bfloat16),
            jax.ShapeDtypeStruct((showers, classes), jnp.float32),
        ),
        in_specs=[inside] * (1 + len(heads_in)) + [outside] * (len(members) + 2),
        scratch_shapes=buffers(members)
        + [
            pltpu.VMEM(side.shape, side.dtype),
            pltpu.VMEM(side.shape, side.dtype),
            pltpu.VMEM((total, width), jnp.float32),
            pltpu.SemaphoreType.DMA((5 * team,)),
        ],
        compiler_params=pltpu.CompilerParams(vmem_limit_bytes=58 * MIB),
        name="classifier_backward",
    )(parts, *heads_in, *members, gate_side, up_side)

    lines = [[o * team + m for o in range(outer)] for m in range(team)]
    grads = lax.all_to_all(grads, "head", 0, 0, axis_index_groups=lines, tiled=True)
    feature_grad = mm(miss, class_weight.astype(jnp.float32), NT, HIGH)
    here = here.reshape(showers, each, LANES)[:, :, :1] / shower_counts[:, None, None]
    own_row_grads = (here * feature_grad[:, None, :]).reshape(block, width)
    guidance = pl.pallas_call(
        functools.partial(final_kernel, float(windows)),
        out_shape=jax.ShapeDtypeStruct((showers, each, width), jnp.float32),
        compiler_params=pltpu.CompilerParams(vmem_limit_bytes=58 * MIB),
        name="norm_backward",
    )(grads, own_x, gain, scales, own_row_grads)
    return (attention.transpose(0, 2, 1), guidance)


def solution(mesh):
    in_specs = (
        P("parts", "head", None),
        P("parts", "head", None),
        P("parts", "head", None),
        P("parts", "head"),
        P("parts"),
        P("parts"),
        P("parts"),
        P(),
        P(),
        P(None, "head"),
        P(None, "head"),
        P("head", None),
        P(),
        P(),
    )
    out_specs = (P(("parts", "head"), None, None), P("parts", "head", None))
    return jax.shard_map(body, mesh=mesh, in_specs=in_specs, out_specs=out_specs, check_vma=False)
```

time: 291 us -> 278 us (0.955)
  blocking collectives: 25.6 us -> 11.5 us
  waiting for transfers between devices: 127 us -> 141 us
  other arithmetic: 14.2 us -> 3.25 us
  Pallas kernels: 78.7 us -> 84.6 us
  starting transfers between devices: 33.4 us -> 28.8 us
  local copies, waits for them, and re-layouts: 7.94 us -> 5 us
    all_to_all x1 -> x0, blocking collectives: 14.1 us -> none  [body(): pooled.append(lax.all_to_all(part, 'head', 0, 0, tiled=True))]
    all_to_all x1 -> x2, waiting for transfers between devices: 6.97 us -> 19.1 us  [body(): pooled.append(lax.all_to_all(part, 'head', 0, 0, tiled=True))]
    concatenate x5 -> x0, other arithmetic: 9.62 us -> none  [the longest x2 6.63 us: body(): jnp.concatenate(x, axis=0)]
    ppermute x9, starting transfers between devices: 10.8 us -> 2.81 us  [swap(): return lax.ppermute(x, 'head', [(d, d ^ bit) for d in range(devices)])]
    pallas_call x4 -> x5, Pallas kernels: 67.7 us -> 72.4 us  [the longest x2 50 us: attend(): pl.pallas_call(functools.partial(attend_kernel, min(512, length), head),...]
    all_to_all x1, waiting for transfers between devices: 20.4 us -> 24.7 us  [body(): lax.all_to_all(grads, 'head', 0, 0, axis_index_groups=lines, tiled=True)]
    ppermute x9, waiting for transfers between devices: 99.9 us -> 95.9 us  [swap(): return lax.ppermute(x, 'head', [(d, d ^ bit) for d in range(devices)])]
    all_to_all x1 -> x2, starting transfers between devices: 6.1 us -> 8.56 us  [body(): pooled.append(lax.all_to_all(part, 'head', 0, 0, tiled=True))]
  transfers between devices with their start and end apart: 13 -> 14, of which waited for: 7 -> 8; matrix products, arithmetic and copies ran while one was open for 8% -> 3% of each run, Pallas kernels for 17% -> 20%
where the time goes in v3:
time: 278 us; the launch traced here: 277 us
  waiting for transfers between devices  141 us (51%)
  Pallas kernels  84.6 us (30%)
  starting transfers between devices  28.8 us (10%)
  blocking collectives  11.5 us (4%)
  local copies, waits for them, and re-layouts  5 us (2%)
  other arithmetic  3.25 us (1%)
    ppermute x9, waiting for transfers between devices, swap(): return lax.ppermute(x, 'head', [(d, d ^ bit) for d in range(devices)])  95.9 us
    pallas_call x2, Pallas kernels, attend(): pl.pallas_call(functools.partial(attend_kernel, min(512, length), head),...  50 us
    all_to_all x1, waiting for transfers between devices, body(): lax.all_to_all(grads, 'head', 0, 0, axis_index_groups=lines, tiled=True)  24.7 us
    all_to_all x2, waiting for transfers between devices, body(): pooled.append(lax.all_to_all(part, 'head', 0, 0, tiled=True))  19.1 us
    pallas_call x2, Pallas kernels, pack(): pl.pallas_call(functools.partial(pack_kernel, first, count), grid=(shower...  14.1 us
    all_to_all x2, starting transfers between devices, exchange(): got = lax.all_to_all(x, 'head', 0, 0, tiled=True)  13 us
    all_to_all x1, blocking collectives, body(): parts = lax.all_to_all(partial, 'head', 0, 0, tiled=True)  11.5 us
    pallas_call x1, Pallas kernels, body(): pl.pallas_call(functools.partial(forward_kernel, [count * LANES for _, co...  9.67 us
  transfers between devices with their start and end apart: 14, of which 8 were waited for; matrix products, arithmetic and copies ran while one was open for 3% of the time, Pallas kernels for 20%

profile of v3, /device:TPU:0, one launch (start us, length us, event | category | flops | bytes accessed | tf_op | source)
XLA Modules:
  0.0 277.5 jit_solution(6533672589363036640)
XLA Ops:
  0.6 7.5 %pack.3 = bf16[32,64,1152]{2,1,0:T(8,128)(2,1)} custom-call(s32[8,64]{1,0:T(8,128)} %slot_ref.3, s32[8]{0:T(128)} %count_ref.3, bf16[8,64,2048]{2,1,0:T(8,128)(2,1)} %q_ref.3, bf16[8,64,2048]{2,1,0:T(8,128)(2,1)} %k_ref.3, bf16[8,64,2048]{2,1,0:T(8,128)(2,1)} %v_ref.3), custom_call_target="tpu_custom_call" | custom-call | tf_op jit(solution)/shard_map/pack/pallas_call | solution.py:62
  8.1 7.4 %all-to-all-start.1 = ((bf16[32,64,1152]{2,1,0:T(8,128)(2,1)}), bf16[32,64,1152]{2,1,0:T(8,128)(2,1)}, u32[]{:S(2)}, u32[]{:S(2)}) async-start(bf16[32,64,1152]{2,1,0:T(8,128)(2,1)} %pack.3), calls=%async_computation.1 | async-start | bytes 9437184 | tf_op jit(solution)/shard_map/all_to_all | solution.py:353
  16.2 0.8 reshape.104.refs_4_.scale_ref
  17.1 0.8 reshape.105.refs_5_
  18.1 0.7 fusion.10.target_ref
  18.8 0.7 fusion.refs_2_
  19.5 1.6 fusion.13.refs_10_.refs_2_
  21.4 0.7 broadcast_in_dim.16.refs_6_
  22.1 0.7 broadcast_in_dim.17.counts_ref
  22.8 1.7 collective-permute-start.4
  25.3 60.4 %collective-permute-done.4.refs_15_.refs_7_ = bf16[2048,256]{1,0:T(8,128)(2,1)} collective-permute-done((bf16[2048,256]{1,0:T(8,128)(2,1)S(1)}, bf16[2048,256]{1,0:T(8,128)(2,1)}, u32[]{:S(2)}, u32[]{:S(2)}) %collective-permute-start.4) | collective-permute-done | bytes 1048608 | tf_op jit(solution)/shard_map/ppermute | solution.py:341
  85.8 28.3 %collective-permute-done.1.refs_14_.refs_6_ = bf16[2048,256]{1,0:T(8,128)(2,1)} collective-permute-done((bf16[2048,256]{1,0:T(8,128)(2,1)S(1)}, bf16[2048,256]{1,0:T(8,128)(2,1)}, u32[]{:S(2)}, u32[]{:S(2)}) %collective-permute-start.1) | collective-permute-done | bytes 1048608 | tf_op jit(solution)/shard_map/ppermute | solution.py:341
  114.2 5.8 %collective-permute-done.7.refs_16_.refs_8_ = f32[256,128]{1,0:T(8,128)S(1)} collective-permute-done((f32[256,128]{1,0:T(8,128)S(1)}, f32[256,128]{1,0:T(8,128)S(1)}, u32[]{:S(2)}, u32[]{:S(2)}) %collective-permute-start.7) | collective-permute-done | bytes 131104 | tf_op jit(solution)/shard_map/ppermute | solution.py:341
  120.0 1.3 collective-permute-done.6.refs_13_.refs_5_
  121.5 6.6 %pack.2 = bf16[32,64,384]{2,1,0:T(8,128)(2,1)} custom-call(s32[8,64]{1,0:T(8,128)} %slot_ref.3, s32[8]{0:T(128)} %count_ref.3, bf16[8,64,2048]{2,1,0:T(8,128)(2,1)} %q_ref.3, bf16[8,64,2048]{2,1,0:T(8,128)(2,1)} %k_ref.3, bf16[8,64,2048]{2,1,0:T(8,128)(2,1)} %v_ref.3), custom_call_target="tpu_custom_call" | custom-call | tf_op jit(solution)/shard_map/pack/pallas_call | solution.py:62
  128.1 0.6 copy-done.10
  128.8 5.6 %all-to-all-start = ((bf16[32,64,384]{2,1,0:T(8,128)(2,1)}), bf16[32,64,384]{2,1,0:T(8,128)(2,1)}, u32[]{:S(2)}, u32[]{:S(2)}) async-start(bf16[32,64,384]{2,1,0:T(8,128)(2,1)} %pack.2), calls=%async_computation | async-start | bytes 3145728 | tf_op jit(solution)/shard_map/all_to_all | solution.py:353
  134.4 36.4 %attend.2 = (bf16[8,64,2048]{2,1,0:T(8,128)(2,1)}, bf16[32,32,384]{2,1,0:T(8,128)(2,1)}) custom-call(bf16[2048,1152]{1,0:T(8,128)(2,1)} %bitcast.3.q_ref.k_ref.v_ref, bf16[2048,1152]{1,0:T(8,128)(2,1)} %bitcast.3.q_ref.k_ref.v_ref, bf16[2048,1152]{1,0:T(8,128)(2,1)} %bitcast.3.q_ref.k_ref.v_ref, bf16[128,2048]{1,0:T(8,128)(2,1)S(1)} %compare_convert_fusion.pool_ref), custom_call_target="tpu_custom_call" | custom-call | flops 6442450944 | bytes 6291456 | tf_op jit(solution)/shard_map/attend/pallas_call | solution.py:146
  170.8 1.1 all-to-all-done
  172.0 4.7 %all-to-all-start.2 = ((bf16[32,32,384]{2,1,0:T(8,128)(2,1)}), bf16[32,32,384]{2,1,0:T(8,128)(2,1)S(1)}, u32[]{:S(2)}, u32[]{:S(2)}) async-start(bf16[32,32,384]{2,1,0:T(8,128)(2,1)} %get-tuple-element.47), calls=%async_computation.2 | async-start | bytes 1572864 | tf_op jit(solution)/shard_map/all_to_all | solution.py:411
  176.7 13.6 %attend.3 = (bf16[8,64,2048]{2,1,0:T(8,128)(2,1)}, bf16[32,48,128]{2,1,0:T(8,128)(2,1)}) custom-call(bf16[2048,384]{1,0:T(8,128)(2,1)} %bitcast.2.q_ref.k_ref.v_ref, bf16[2048,384]{1,0:T(8,128)(2,1)} %bitcast.2.q_ref.k_ref.v_ref, bf16[2048,384]{1,0:T(8,128)(2,1)} %bitcast.2.q_ref.k_ref.v_ref, ...), custom_call_target="tpu_custom_call", output_to_operand_aliasing={{0}: (4, {})} | custom-call | flops 2147483648 | bytes 2097152 | tf_op jit(solution)/shard_map/attend/pallas_call | solution.py:146
  190.3 6.8 %all-to-all-done.2.refs_0_ = bf16[32,32,384]{2,1,0:T(8,128)(2,1)S(1)} async-done(((bf16[32,32,384]{2,1,0:T(8,128)(2,1)}), bf16[32,32,384]{2,1,0:T(8,128)(2,1)S(1)}, u32[]{:S(2)}, u32[]{:S(2)}) %all-to-all-start.2) | async-done | bytes 786464 | tf_op jit(solution)/shard_map/all_to_all | solution.py:411
  197.1 3.9 %all-to-all-start.3 = ((bf16[32,48,128]{2,1,0:T(8,128)(2,1)}), bf16[32,48,128]{2,1,0:T(8,128)(2,1)S(1)}, u32[]{:S(2)}, u32[]{:S(2)}) async-start(bf16[32,48,128]{2,1,0:T(8,128)(2,1)} %get-tuple-element.49), calls=%async_computation.3 | async-start | bytes 786432 | tf_op jit(solution)/shard_map/all_to_all | solution.py:411
  201.6 12.3 %all-to-all-done.3.refs_1_ = bf16[32,48,128]{2,1,0:T(8,128)(2,1)S(1)} async-done(((bf16[32,48,128]{2,1,0:T(8,128)(2,1)}), bf16[32,48,128]{2,1,0:T(8,128)(2,1)S(1)}, u32[]{:S(2)}, u32[]{:S(2)}) %all-to-all-start.3) | async-done | bytes 393248 | tf_op jit(solution)/shard_map/all_to_all | solution.py:411
  213.9 0.7 copy-done.6
  214.6 9.7 %classifier_forward.1 = (f32[32,8,128]{2,1,0:T(8,128)}, f32[4,256,256]{2,1,0:T(8,128)}, f32[4,256,256]{2,1,0:T(8,128)}, f32[32,2048]{1,0:T(8,128)}) custom-call(s32[2]{0:T(128)} %pad_add_fusion.place_ref, bf16[32,32,384]{2,1,0:T(8,128)(2,1)} %copy-done.5, bf16[32,48,128]{2,1,0:T(8,128)(2,1)} %copy-done.6, bf16[256,256]{1,0:T(8,128)(2,1)} %fusion.refs_2_, ...), custom_call_target="tpu_custom_call" | custom-call | tf_op jit(solution)/shard_map/classifier_forward/pallas_call | solution.py:424
  224.3 11.5 %all_to_all.30.parts_ref = f32[32,8,128]{2,1,0:T(8,128)} all-to-all(f32[32,8,128]{2,1,0:T(8,128)} %get-tuple-element.68), channel_id=1, replica_groups=mesh['parts'=1,'head'=32] {'head'}, dimensions={0} | all-to-all | bytes 262144 | tf_op jit(solution)/shard_map/all_to_all | solution.py:448
  235.8 8.3 %classifier_backward.1 = (bf16[8,32,2048]{2,1,0:T(8,128)(2,1)}, f32[8,128]{1,0:T(8,128)}) custom-call(f32[32,8,128]{2,1,0:T(8,128)} %all_to_all.30.parts_ref, f32[8,128]{1,0:T(8,128)} %broadcast_in_dim.17.counts_ref, f32[1,128]{1,0:T(1,128)} %bitcast.14, f32[8,128]{1,0:T(8,128)} %fusion.10.target_ref, f32[32,8]{1,0:T(8,128)} %constant.61.clone.spread_ref, ...), custom_call_target="tpu_custom_call" | custom-call | tf_op jit(solution)/shard_map/classifier_backward/pallas_call | solution.py:449
  244.2 4.4 %all-to-all-start.5 = ((bf16[8,32,2048]{2,1,0:T(8,128)(2,1)}), bf16[8,32,2048]{2,1,0:T(8,128)(2,1)}, u32[]{:S(2)}, u32[]{:S(2)}) async-start(bf16[8,32,2048]{2,1,0:T(8,128)(2,1)} %get-tuple-element.75), calls=%async_computation.5 | async-start | bytes 2097152 | tf_op jit(solution)/shard_map/all_to_all | solution.py:468
  249.6 0.8 broadcast_multiply_fusion.dy_ref
  250.3 24.7 %all-to-all-done.5.dn_ref = bf16[8,32,2048]{2,1,0:T(8,128)(2,1)} async-done(((bf16[8,32,2048]{2,1,0:T(8,128)(2,1)}), bf16[8,32,2048]{2,1,0:T(8,128)(2,1)}, u32[]{:S(2)}, u32[]{:S(2)}) %all-to-all-start.5) | async-done | bytes 1048608 | tf_op jit(solution)/shard_map/all_to_all | solution.py:468
  275.0 2.4 norm_backward.1
  (72 shorter events, 3.7 us)
Async XLA Ops:
  0.6 15.1 %copy-start = (bf16[256,4096]{1,0:T(8,128)(2,1)S(1)}, bf16[256,4096]{1,0:T(8,128)(2,1)}, u32[]{:S(2)}) copy-start(bf16[256,4096]{1,0:T(8,128)(2,1)} %param.24) | copy-start | bytes 6291460
  8.1 7.4 %copy-start.12 = (s32[8]{0:T(128)S(1)}, s32[8]{0:T(128)}, u32[]{:S(2)}) copy-start(s32[8]{0:T(128)} %count_ref.3) | copy-start | bytes 100
  8.1 7.4 %copy-start.18 = (s32[8]{0:T(128)S(1)}, s32[8]{0:T(128)}, u32[]{:S(2)}) copy-start(s32[8]{0:T(128)} %param.22) | copy-start | bytes 100
  8.1 120.6 %all-to-all-start.1 = ((bf16[32,64,1152]{2,1,0:T(8,128)(2,1)}), bf16[32,64,1152]{2,1,0:T(8,128)(2,1)}, u32[]{:S(2)}, u32[]{:S(2)}) async-start(bf16[32,64,1152]{2,1,0:T(8,128)(2,1)} %pack.3), calls=%async_computation.1 | async-start | bytes 9437184 | tf_op jit(solution)/shard_map/all_to_all | solution.py:353
  15.7 2.4 copy-start.17
  15.8 3.0 %copy-start.15 = (s32[256]{0:T(256)S(1)}, s32[256]{0:T(256)}, u32[]{:S(2)}) copy-start(s32[256]{0:T(256)} %constant.60.clone) | copy-start | bytes 3076
  15.8 3.8 %copy-start.1 = (bf16[2048,128]{1,0:T(8,128)(2,1)S(1)}, bf16[2048,128]{1,0:T(8,128)(2,1)}, u32[]{:S(2)}) copy-start(bf16[2048,128]{1,0:T(8,128)(2,1)} %refs_7_) | copy-start | bytes 1572868
  16.2 5.0 %copy-start.16 = (s32[128]{0:T(128)S(1)}, s32[128]{0:T(128)}, u32[]{:S(2)}) copy-start(s32[128]{0:T(128)} %constant.59.clone) | copy-start | bytes 1540
  18.1 4.7 %copy-start.4 = (bf16[2048,256]{1,0:T(8,128)(2,1)S(1)}, bf16[2048,256]{1,0:T(8,128)(2,1)}, u32[]{:S(2)}) copy-start(bf16[2048,256]{1,0:T(8,128)(2,1)} %refs_1_) | copy-start | bytes 3145732
  18.1 6.4 %copy-start.3 = (bf16[2048,256]{1,0:T(8,128)(2,1)S(1)}, bf16[2048,256]{1,0:T(8,128)(2,1)}, u32[]{:S(2)}) copy-start(bf16[2048,256]{1,0:T(8,128)(2,1)} %refs_0_) | copy-start | bytes 3145732
  21.2 106.9 %copy-start.7 = (f32[256,128]{1,0:T(8,128)}, f32[256,128]{1,0:T(8,128)S(1)}, u32[]{:S(2)}) copy-start(f32[256,128]{1,0:T(8,128)S(1)} %fusion.13.refs_10_.refs_2_) | copy-start | bytes 393220
  22.8 63.0 %collective-permute-start.4 = (bf16[2048,256]{1,0:T(8,128)(2,1)S(1)}, bf16[2048,256]{1,0:T(8,128)(2,1)}, u32[]{:S(2)}, u32[]{:S(2)}) collective-permute-start(bf16[2048,256]{1,0:T(8,128)(2,1)S(1)} %copy-done.4), channel_id=1, source_target_pairs={{0,2},{1,3},{2,0},{3,1},{4,6},{5,7},{6,4},{7,5},{8,10},{9,11},{10,... | collective-permute-start | bytes 3145736 | tf_op jit(solution)/shard_map/ppermute | solution.py:341
  24.5 89.6 %collective-permute-start.1 = (bf16[2048,256]{1,0:T(8,128)(2,1)S(1)}, bf16[2048,256]{1,0:T(8,128)(2,1)}, u32[]{:S(2)}, u32[]{:S(2)}) collective-permute-start(bf16[2048,256]{1,0:T(8,128)(2,1)S(1)} %copy-done.3), channel_id=1, source_target_pairs={{0,2},{1,3},{2,0},{3,1},{4,6},{5,7},{6,4},{7,5},{8,10},{9,11},{10,... | collective-permute-start | bytes 3145736 | tf_op jit(solution)/shard_map/ppermute | solution.py:341
  24.8 103.3 %collective-permute-start.3 = (bf16[2048,256]{1,0:T(8,128)(2,1)S(1)}, bf16[2048,256]{1,0:T(8,128)(2,1)}, u32[]{:S(2)}, u32[]{:S(2)}) collective-permute-start(bf16[2048,256]{1,0:T(8,128)(2,1)S(1)} %copy-done.4), channel_id=1, source_target_pairs={{0,1},{1,0},{2,3},{3,2},{4,5},{5,4},{6,7},{7,6},{8,9},{9,8},{10,11... | collective-permute-start | bytes 3145736 | tf_op jit(solution)/shard_map/ppermute | solution.py:341
  24.8 103.3 %collective-permute-start = (bf16[2048,256]{1,0:T(8,128)(2,1)S(1)}, bf16[2048,256]{1,0:T(8,128)(2,1)}, u32[]{:S(2)}, u32[]{:S(2)}) collective-permute-start(bf16[2048,256]{1,0:T(8,128)(2,1)S(1)} %copy-done.3), channel_id=1, source_target_pairs={{0,1},{1,0},{2,3},{3,2},{4,5},{5,4},{6,7},{7,6},{8,9},{9,8},{10,11... | collective-permute-start | bytes 3145736 | tf_op jit(solution)/shard_map/ppermute | solution.py:341
  85.8 43.0 %collective-permute-start.5 = (bf16[2048,256]{1,0:T(8,128)(2,1)}, bf16[2048,256]{1,0:T(8,128)(2,1)}, u32[]{:S(2)}, u32[]{:S(2)}) collective-permute-start(bf16[2048,256]{1,0:T(8,128)(2,1)} %collective-permute-done.4.refs_15_.refs_7_), channel_id=1, source_target_pairs={{0,1},{1,0},{2,3},{3,2},{4,5},{5,4},{6,7},{7,6},{8,9},{9,8},{10,11... | collective-permute-start | bytes 3145736 | tf_op jit(solution)/shard_map/ppermute | solution.py:341
  114.1 14.7 %collective-permute-start.2 = (bf16[2048,256]{1,0:T(8,128)(2,1)}, bf16[2048,256]{1,0:T(8,128)(2,1)}, u32[]{:S(2)}, u32[]{:S(2)}) collective-permute-start(bf16[2048,256]{1,0:T(8,128)(2,1)} %collective-permute-done.1.refs_14_.refs_6_), channel_id=1, source_target_pairs={{0,1},{1,0},{2,3},{3,2},{4,5},{5,4},{6,7},{7,6},{8,9},{9,8},{10,11... | collective-permute-start | bytes 3145736 | tf_op jit(solution)/shard_map/ppermute | solution.py:341
  114.1 5.9 %collective-permute-start.7 = (f32[256,128]{1,0:T(8,128)S(1)}, f32[256,128]{1,0:T(8,128)S(1)}, u32[]{:S(2)}, u32[]{:S(2)}) collective-permute-start(f32[256,128]{1,0:T(8,128)S(1)} %fusion.13.refs_10_.refs_2_), channel_id=1, source_target_pairs={{0,2},{1,3},{2,0},{3,1},{4,6},{5,7},{6,4},{7,5},{8,10},{9,11},{10,... | collective-permute-start | bytes 393224 | tf_op jit(solution)/shard_map/ppermute | solution.py:341
  120.0 8.1 %copy-start.8 = (f32[256,128]{1,0:T(8,128)}, f32[256,128]{1,0:T(8,128)S(1)}, u32[]{:S(2)}) copy-start(f32[256,128]{1,0:T(8,128)S(1)} %collective-permute-done.7.refs_16_.refs_8_) | copy-start | bytes 393220
  120.0 1.3 collective-permute-start.6
  121.3 6.7 %copy-start.9 = (f32[256,128]{1,0:T(8,128)}, f32[256,128]{1,0:T(8,128)S(1)}, u32[]{:S(2)}) copy-start(f32[256,128]{1,0:T(8,128)S(1)} %collective-permute-done.6.refs_13_.refs_5_) | copy-start | bytes 393220
  121.3 6.8 %collective-permute-start.8 = (f32[256,128]{1,0:T(8,128)S(1)}, f32[256,128]{1,0:T(8,128)S(1)}, u32[]{:S(2)}, u32[]{:S(2)}) collective-permute-start(f32[256,128]{1,0:T(8,128)S(1)} %collective-permute-done.7.refs_16_.refs_8_), channel_id=1, source_target_pairs={{0,1},{1,0},{2,3},{3,2},{4,5},{5,4},{6,7},{7,6},{8,9},{9,8},{10,11... | collective-permute-start | bytes 393224 | tf_op jit(solution)/shard_map/ppermute | solution.py:341
  128.8 43.2 %all-to-all-start = ((bf16[32,64,384]{2,1,0:T(8,128)(2,1)}), bf16[32,64,384]{2,1,0:T(8,128)(2,1)}, u32[]{:S(2)}, u32[]{:S(2)}) async-start(bf16[32,64,384]{2,1,0:T(8,128)(2,1)} %pack.2), calls=%async_computation | async-start | bytes 3145728 | tf_op jit(solution)/shard_map/all_to_all | solution.py:353
  172.0 25.1 %all-to-all-start.2 = ((bf16[32,32,384]{2,1,0:T(8,128)(2,1)}), bf16[32,32,384]{2,1,0:T(8,128)(2,1)S(1)}, u32[]{:S(2)}, u32[]{:S(2)}) async-start(bf16[32,32,384]{2,1,0:T(8,128)(2,1)} %get-tuple-element.47), calls=%async_computation.2 | async-start | bytes 1572864 | tf_op jit(solution)/shard_map/all_to_all | solution.py:411
  197.1 16.8 %copy-start.5 = (bf16[32,32,384]{2,1,0:T(8,128)(2,1)}, bf16[32,32,384]{2,1,0:T(8,128)(2,1)S(1)}, u32[]{:S(2)}) copy-start(bf16[32,32,384]{2,1,0:T(8,128)(2,1)S(1)} %all-to-all-done.2.refs_0_) | copy-start | bytes 2359300
  197.1 16.8 %all-to-all-start.3 = ((bf16[32,48,128]{2,1,0:T(8,128)(2,1)}), bf16[32,48,128]{2,1,0:T(8,128)(2,1)S(1)}, u32[]{:S(2)}, u32[]{:S(2)}) async-start(bf16[32,48,128]{2,1,0:T(8,128)(2,1)} %get-tuple-element.49), calls=%async_computation.3 | async-start | bytes 786432 | tf_op jit(solution)/shard_map/all_to_all | solution.py:411
  213.9 0.7 copy-start.6
  244.1 4.4 %copy-start.11 = (s32[8,64]{1,0:T(8,128)S(1)}, s32[8,64]{1,0:T(8,128)}, u32[]{:S(2)}) copy-start(s32[8,64]{1,0:T(8,128)} %slot_ref.3) | copy-start | bytes 6148
  244.2 4.4 %copy-start.13 = (s32[8]{0:T(128)S(1)}, s32[8]{0:T(128)}, u32[]{:S(2)}) copy-start(s32[8]{0:T(128)} %count_ref.3) | copy-start | bytes 100
  244.2 4.7 %copy-start.2 = (bf16[2048,128]{1,0:T(8,128)(2,1)S(1)}, bf16[2048,128]{1,0:T(8,128)(2,1)}, u32[]{:S(2)}) copy-start(bf16[2048,128]{1,0:T(8,128)(2,1)} %refs_7_) | copy-start | bytes 1572868
  244.2 4.7 %copy-start.14 = (f32[8,128]{1,0:T(8,128)S(1)}, f32[8,128]{1,0:T(8,128)}, u32[]{:S(2)}) copy-start(f32[8,128]{1,0:T(8,128)} %get-tuple-element.77) | copy-start | bytes 12292
  244.2 30.8 %all-to-all-start.5 = ((bf16[8,32,2048]{2,1,0:T(8,128)(2,1)}), bf16[8,32,2048]{2,1,0:T(8,128)(2,1)}, u32[]{:S(2)}, u32[]{:S(2)}) async-start(bf16[8,32,2048]{2,1,0:T(8,128)(2,1)} %get-tuple-element.75), calls=%async_computation.5 | async-start | bytes 2097152 | tf_op jit(solution)/shard_map/all_to_all | solution.py:468
  (1 other events, 0.7 us)

commit v4 on v3

--- a/solution.py
+++ b/solution.py
@@ -35,43 +35,67 @@
     return jnp.concatenate([jnp.cos(angles), jnp.sin(angles)], axis=1)
 
 
-def pack_kernel(first, count, slot_ref, count_ref, q_ref, k_ref, v_ref, out):
-    shower = pl.program_id(0)
-    group = out.shape[0]
-    local = q_ref.shape[1]
+def pack_kernel(first, count, slot_ref, count_ref, q_ref, k_ref, v_ref, out_ref, packed, sems, out_sems):
+    showers, group, local, _ = packed.shape
     features = q_ref.shape[2] // group
     size = count * LANES
-    valid = (slot_ref[pl.ds(shower, 1), :] < count_ref[shower]).astype(jnp.float32)
+    arriving = []
+    for m in range(group):
+        at = m * features + first * LANES
+        for t, ref in enumerate((q_ref, k_ref, v_ref)):
+            place = packed.at[:, m, :, t * size : (t + 1) * size]
+            copy = pltpu.make_async_copy(ref.at[:, :, at : at + size], place, sems.at[3 * m + t])
+            copy.start()
+            arriving.append(copy)
     square = (local, local)
     diagonal = lax.broadcasted_iota(jnp.int32, square, 0) == lax.broadcasted_iota(
         jnp.int32, square, 1
     )
-    column = jnp.sum(jnp.where(diagonal, valid, 0.0), axis=1, keepdims=True) > 0.5
+    columns = []
+    for s in range(showers):
+        valid = (slot_ref[s : s + 1, :] < count_ref[s]).astype(jnp.float32)
+        columns.append(jnp.sum(jnp.where(diagonal, valid, 0.0), axis=1, keepdims=True) > 0.5)
+    leaving = []
     for m in range(group):
-        at = m * features + first * LANES
-        for t, ref in enumerate((q_ref, k_ref, v_ref)):
-            part = ref[0, :, at : at + size]
-            if t == 1:
-                part = jnp.where(column, part, jnp.asarray(ABSENT, part.dtype))
-            out[m, :, t * size : (t + 1) * size] = part
+        for copy in arriving[3 * m : 3 * m + 3]:
+            copy.wait()
+        for s in range(showers):
+            part = packed[s, m, :, size : 2 * size]
+            packed[s, m, :, size : 2 * size] = jnp.where(
+                columns[s], part, jnp.asarray(ABSENT, part.dtype)
+            )
+        copy = pltpu.make_async_copy(packed.at[:, m], out_ref.at[:, m], out_sems.at[m])
+        copy.start()
+        leaving.append(copy)
+    for copy in leaving:
+        copy.wait()
 
 
 def pack(slot_positions, counts, queries, keys, values, first, count, devices):
     showers, local, width = queries.shape
     group = devices // showers
-    return pl.pallas_call(
+    shape = (showers, group, local, 3 * count * LANES)
+    outside = pl.BlockSpec(memory_space=pl.ANY)
+    packed = pl.pallas_call(
         functools.partial(pack_kernel, first, count),
-        grid=(showers,),
-        out_shape=jax.ShapeDtypeStruct((devices, local, 3 * count * LANES), jnp.bfloat16),
+        out_shape=jax.ShapeDtypeStruct(shape, jnp.bfloat16),
         in_specs=[
-            pl.BlockSpec((showers, local), lambda s: (0, 0)),
+            pl.BlockSpec(memory_space=pltpu.VMEM),
             pl.BlockSpec(memory_space=pltpu.SMEM),
-        ]
-        + [pl.BlockSpec((1, local, width), lambda s: (s, 0, 0))] * 3,
-        out_specs=pl.BlockSpec((group, local, 3 * count * LANES), lambda s: (s, 0, 0)),
+            outside,
+            outside,
+            outside,
+        ],
+        out_specs=outside,
+        scratch_shapes=[
+            pltpu.VMEM(shape, jnp.bfloat16),
+            pltpu.SemaphoreType.DMA((3 * group,)),
+            pltpu.SemaphoreType.DMA((group,)),
+        ],
         compiler_params=pltpu.CompilerParams(vmem_limit_bytes=58 * MIB),
         name="pack",
     )(slot_positions, counts, queries, keys, values)
+    return packed.reshape((devices,) + shape[2:])
 
 
 def attend_kernel(block, head, q_ref, k_ref, v_ref, pool_ref, *rest):
@@ -176,12 +200,18 @@
         pltpu.make_async_copy(source, buffer, sems.at[i])
         for i, (source, buffer) in enumerate(zip(sources, buffers))
     ]
-    for copy in arriving:
+    first = n + 6
+    for copy in arriving[: first + 3]:
         copy.start()
 
     def get(i):
         arriving[i].wait()
         return buffers[i]
+
+    def start_member(i):
+        if i < team:
+            for copy in arriving[first + 3 * i : first + 3 * i + 3]:
+                copy.start()
 
     showers = copies_ref.shape[1]
     group = buffers[0].shape[0] // showers
@@ -189,6 +219,7 @@
     block = own_x_ref.shape[0]
     total = rows * showers
     x_refs = [get(i) for i in range(n)]
+    start_member(1)
     for s in range(showers):
         for m in range(group):
             at = m * (width // group)
@@ -227,15 +258,16 @@
     coef = cnt / counts_ref[...][:, :1]
     leaving = []
     for i in range(team):
-        gate_ref, up_ref, map_ref = [get(n + 6 + 3 * i + j) for j in range(3)]
+        gate_ref, up_ref, map_ref = [get(first + 3 * i + j) for j in range(3)]
+        start_member(i + 2)
         gate = mm(normed[...], gate_ref[...])
         up = mm(normed[...], up_ref[...])
         sigma = jax.nn.sigmoid(gate)
         activated = gate * sigma
         hidden = (activated * up).astype(jnp.bfloat16)
         logits = logits + mm(mm(cnt_of, hidden, TN)[:showers], map_ref[...], precision=HIGH)
-        ga_ref[i] = coef * (up * sigma * (1.0 + gate * (1.0 - sigma)))
-        aa_ref[i] = coef * activated
+        ga_ref[i] = (coef * (up * sigma * (1.0 + gate * (1.0 - sigma)))).astype(jnp.bfloat16)
+        aa_ref[i] = (coef * activated).astype(jnp.bfloat16)
         for j, (kept, out) in enumerate(((ga_ref, ga_out), (aa_ref, aa_out))):
             copy = pltpu.make_async_copy(kept.at[i], out.at[i], out_sems.at[2 * i + j])
             copy.start()
@@ -262,8 +294,14 @@
                 for j, (source, buffer) in enumerate(pairs)
             ]
         )
-        for copy in arriving[-1]:
-            copy.start()
+
+    def start_member(i):
+        if i < team:
+            for copy in arriving[i]:
+                copy.start()
+
+    start_member(0)
+    start_member(1)
     blocks, block, _ = dn_ref.shape
     logits = jnp.sum(parts_ref[...], axis=0) / counts_ref[...] + bias_ref[...]
     exponent = jnp.exp(logits - jnp.max(logits, axis=1, keepdims=True))
@@ -274,10 +312,11 @@
         gate_ref, up_ref, map_ref = buffers[3 * i : 3 * i + 3]
         for copy in arriving[i]:
             copy.wait()
+        start_member(i + 2)
         wide = mm(spread, map_ref[...], NT, HIGH)
         wide = jnp.concatenate([wide] * blocks, axis=0)
-        gate_grad = (wide * ga_ref[i]).astype(jnp.bfloat16)
-        up_grad = (wide * aa_ref[i]).astype(jnp.bfloat16)
+        gate_grad = (wide * ga_ref[i].astype(jnp.float32)).astype(jnp.bfloat16)
+        up_grad = (wide * aa_ref[i].astype(jnp.float32)).astype(jnp.bfloat16)
         term = mm(gate_grad, gate_ref[...], NT) + mm(up_grad, up_ref[...], NT)
         if i == 0:
             total[...] = term
@@ -388,14 +427,15 @@
         return [found[m] for m in range(team)]
 
     class_map = jnp.dot(down_weight, class_weight, preferred_element_type=jnp.float32)
-    up_weight, class_map, fixed, late, heads_in, pool = lax.optimization_barrier(
-        (up_weight, class_map, fixed, late, heads_in, pool)
+    sent = [pack(*tokens, *chunk, devices) for chunk in chunks[1:]]
+    sent, up_weight, class_map, fixed, late, heads_in, pool = lax.optimization_barrier(
+        (sent, up_weight, class_map, fixed, late, heads_in, pool)
     )
     class_map = gather(class_map)
     gates = gather(gate_weight)
     ups = gather(up_weight)
     sent, gates, ups, class_map = lax.optimization_barrier(
-        ([pack(*tokens, *chunk, devices) for chunk in chunks[1:]], gates, ups, class_map)
+        (sent, gates, ups, class_map)
     )
     received += [exchange(x) for x in sent]
 
@@ -414,7 +454,7 @@
 
     inside = pl.BlockSpec(memory_space=pltpu.VMEM)
     outside = pl.BlockSpec(memory_space=pl.ANY)
-    side = jax.ShapeDtypeStruct((team, total, units), jnp.float32)
+    side = jax.ShapeDtypeStruct((team, total, units), jnp.bfloat16)
     members = [x for member in zip(gates, ups, class_map) for x in member]
     operands = [*pooled, *fixed, *late, *members]
 

time: 278 us -> 272 us (0.978)
  Pallas kernels: 84.6 us -> 78.5 us
    pallas_call x2, Pallas kernels: 14.1 us -> 8.01 us  [pack(): pl.pallas_call(functools.partial(pack_kernel, first, count), out_shape=ja...]
  transfers between devices with their start and end apart: 14 -> 14, of which waited for: 8 -> 9; matrix products, arithmetic and copies ran while one was open for 3% -> 3% of each run, Pallas kernels for 20% -> 20%
where the time goes in v4:
time: 272 us; the launch traced here: 271 us
  waiting for transfers between devices  139 us (51%)
  Pallas kernels  78.5 us (29%)
  starting transfers between devices  28.8 us (11%)
  blocking collectives  11.5 us (4%)
  local copies, waits for them, and re-layouts  6.87 us (3%)
  other arithmetic  3.31 us (1%)
    ppermute x9, waiting for transfers between devices, swap(): return lax.ppermute(x, 'head', [(d, d ^ bit) for d in range(devices)])  93.7 us
    pallas_call x2, Pallas kernels, attend(): pl.pallas_call(functools.partial(attend_kernel, min(512, length), head),...  50.1 us
    all_to_all x1, waiting for transfers between devices, body(): lax.all_to_all(grads, 'head', 0, 0, axis_index_groups=lines, tiled=True)  24.6 us
    all_to_all x2, waiting for transfers between devices, body(): pooled.append(lax.all_to_all(part, 'head', 0, 0, tiled=True))  19.1 us
    all_to_all x2, starting transfers between devices, exchange(): got = lax.all_to_all(x, 'head', 0, 0, tiled=True)  13 us
    all_to_all x1, blocking collectives, body(): parts = lax.all_to_all(partial, 'head', 0, 0, tiled=True)  11.5 us
    pallas_call x1, Pallas kernels, body(): pl.pallas_call(functools.partial(forward_kernel, [count * LANES for _, co...  9.63 us
    all_to_all x2, starting transfers between devices, body(): pooled.append(lax.all_to_all(part, 'head', 0, 0, tiled=True))  8.62 us
  transfers between devices with their start and end apart: 14, of which 9 were waited for; matrix products, arithmetic and copies ran while one was open for 3% of the time, Pallas kernels for 20%

profile of v4, /device:TPU:0, one launch (start us, length us, event | category | flops | bytes accessed | tf_op | source)
XLA Modules:
  0.0 271.1 jit_solution(4492027876043267968)
XLA Ops:
  0.6 4.8 %pack.3 = bf16[8,4,64,1152]{3,2,1,0:T(8,128)(2,1)} custom-call(s32[8,64]{1,0:T(8,128)} %slot_ref.3, s32[8]{0:T(128)} %count_ref.3, bf16[8,64,2048]{2,1,0:T(8,128)(2,1)} %q_ref.3, bf16[8,64,2048]{2,1,0:T(8,128)(2,1)} %k_ref.3, bf16[8,64,2048]{2,1,0:T(8,128)(2,1)} %v_ref.3), custom_call_target="tpu_custom_call" | custom-call | tf_op jit(solution)/shard_map/pack/pallas_call | solution.py:79
  5.4 7.4 %all-to-all-start.1 = ((bf16[32,64,1152]{2,1,0:T(8,128)(2,1)}), bf16[32,64,1152]{2,1,0:T(8,128)(2,1)}, u32[]{:S(2)}, u32[]{:S(2)}) async-start(bf16[32,64,1152]{2,1,0:T(8,128)(2,1)} %bitcast.14), calls=%async_computation.1 | async-start | bytes 9437184 | tf_op jit(solution)/shard_map/all_to_all | solution.py:392
  12.9 3.2 %pack.2 = bf16[8,4,64,384]{3,2,1,0:T(8,128)(2,1)} custom-call(s32[8,64]{1,0:T(8,128)} %slot_ref.3, s32[8]{0:T(128)} %count_ref.3, bf16[8,64,2048]{2,1,0:T(8,128)(2,1)} %q_ref.3, bf16[8,64,2048]{2,1,0:T(8,128)(2,1)} %k_ref.3, bf16[8,64,2048]{2,1,0:T(8,128)(2,1)} %v_ref.3), custom_call_target="tpu_custom_call" | custom-call | tf_op jit(solution)/shard_map/pack/pallas_call | solution.py:79
  16.8 0.8 reshape.111.refs_4_.scale_ref
  17.7 0.8 reshape.112.refs_5_
  19.4 0.8 fusion.refs_2_
  20.1 1.6 fusion.13.refs_10_.refs_2_
  22.0 0.8 broadcast_in_dim.16.refs_6_
  23.4 1.7 collective-permute-start.4
  25.9 57.0 %collective-permute-done.4.refs_15_.refs_7_ = bf16[2048,256]{1,0:T(8,128)(2,1)S(1)} collective-permute-done((bf16[2048,256]{1,0:T(8,128)(2,1)S(1)}, bf16[2048,256]{1,0:T(8,128)(2,1)S(1)}, u32[]{:S(2)}, u32[]{:S(2)}) %collective-permute-start.4) | collective-permute-done | bytes 1048608 | tf_op jit(solution)/shard_map/ppermute | solution.py:380
  83.0 28.3 %collective-permute-done.1.refs_14_.refs_6_ = bf16[2048,256]{1,0:T(8,128)(2,1)S(1)} collective-permute-done((bf16[2048,256]{1,0:T(8,128)(2,1)S(1)}, bf16[2048,256]{1,0:T(8,128)(2,1)S(1)}, u32[]{:S(2)}, u32[]{:S(2)}) %collective-permute-start.1) | collective-permute-done | bytes 1048608 | tf_op jit(solution)/shard_map/ppermute | solution.py:380
  111.4 5.8 %collective-permute-done.7.refs_16_.refs_8_ = f32[256,128]{1,0:T(8,128)S(1)} collective-permute-done((f32[256,128]{1,0:T(8,128)S(1)}, f32[256,128]{1,0:T(8,128)S(1)}, u32[]{:S(2)}, u32[]{:S(2)}) %collective-permute-start.7) | collective-permute-done | bytes 131104 | tf_op jit(solution)/shard_map/ppermute | solution.py:380
  117.2 1.3 collective-permute-done.6.refs_13_.refs_5_
  118.7 1.2 collective-permute-done.8.refs_19_.refs_11_
  119.9 1.0 copy-done.7
  121.4 1.0 copy-done.9
  122.4 5.6 %all-to-all-start = ((bf16[32,64,384]{2,1,0:T(8,128)(2,1)}), bf16[32,64,384]{2,1,0:T(8,128)(2,1)}, u32[]{:S(2)}, u32[]{:S(2)}) async-start(bf16[32,64,384]{2,1,0:T(8,128)(2,1)} %bitcast.15), calls=%async_computation | async-start | bytes 3145728 | tf_op jit(solution)/shard_map/all_to_all | solution.py:392
  128.0 36.5 %attend.2 = (bf16[8,64,2048]{2,1,0:T(8,128)(2,1)}, bf16[32,32,384]{2,1,0:T(8,128)(2,1)}) custom-call(bf16[2048,1152]{1,0:T(8,128)(2,1)} %bitcast.5.q_ref.k_ref.v_ref, bf16[2048,1152]{1,0:T(8,128)(2,1)} %bitcast.5.q_ref.k_ref.v_ref, bf16[2048,1152]{1,0:T(8,128)(2,1)} %bitcast.5.q_ref.k_ref.v_ref, bf16[128,2048]{1,0:T(8,128)(2,1)S(1)} %compare_convert_fusion.pool_ref), custom_call_target="tpu_custom_call" | custom-call | flops 6442450944 | bytes 6291456 | tf_op jit(solution)/shard_map/attend/pallas_call | solution.py:170
  164.5 1.1 all-to-all-done
  165.6 4.7 %all-to-all-start.2 = ((bf16[32,32,384]{2,1,0:T(8,128)(2,1)}), bf16[32,32,384]{2,1,0:T(8,128)(2,1)S(1)}, u32[]{:S(2)}, u32[]{:S(2)}) async-start(bf16[32,32,384]{2,1,0:T(8,128)(2,1)} %get-tuple-element.49), calls=%async_computation.2 | async-start | bytes 1572864 | tf_op jit(solution)/shard_map/all_to_all | solution.py:451
  170.3 13.6 %attend.3 = (bf16[8,64,2048]{2,1,0:T(8,128)(2,1)}, bf16[32,48,128]{2,1,0:T(8,128)(2,1)}) custom-call(bf16[2048,384]{1,0:T(8,128)(2,1)} %bitcast.3.q_ref.k_ref.v_ref, bf16[2048,384]{1,0:T(8,128)(2,1)} %bitcast.3.q_ref.k_ref.v_ref, bf16[2048,384]{1,0:T(8,128)(2,1)} %bitcast.3.q_ref.k_ref.v_ref, ...), custom_call_target="tpu_custom_call", output_to_operand_aliasing={{0}: (4, {})} | custom-call | flops 2147483648 | bytes 2097152 | tf_op jit(solution)/shard_map/attend/pallas_call | solution.py:170
  183.9 6.8 %all-to-all-done.2.refs_0_ = bf16[32,32,384]{2,1,0:T(8,128)(2,1)S(1)} async-done(((bf16[32,32,384]{2,1,0:T(8,128)(2,1)}), bf16[32,32,384]{2,1,0:T(8,128)(2,1)S(1)}, u32[]{:S(2)}, u32[]{:S(2)}) %all-to-all-start.2) | async-done | bytes 786464 | tf_op jit(solution)/shard_map/all_to_all | solution.py:451
  190.7 3.9 %all-to-all-start.3 = ((bf16[32,48,128]{2,1,0:T(8,128)(2,1)}), bf16[32,48,128]{2,1,0:T(8,128)(2,1)S(1)}, u32[]{:S(2)}, u32[]{:S(2)}) async-start(bf16[32,48,128]{2,1,0:T(8,128)(2,1)} %get-tuple-element.51), calls=%async_computation.3 | async-start | bytes 786432 | tf_op jit(solution)/shard_map/all_to_all | solution.py:451
  195.2 12.3 %all-to-all-done.3.refs_1_ = bf16[32,48,128]{2,1,0:T(8,128)(2,1)S(1)} async-done(((bf16[32,48,128]{2,1,0:T(8,128)(2,1)}), bf16[32,48,128]{2,1,0:T(8,128)(2,1)S(1)}, u32[]{:S(2)}, u32[]{:S(2)}) %all-to-all-start.3) | async-done | bytes 393248 | tf_op jit(solution)/shard_map/all_to_all | solution.py:451
  207.5 0.8 copy-done.11
  208.3 9.6 %classifier_forward.1 = (f32[32,8,128]{2,1,0:T(8,128)}, bf16[4,256,256]{2,1,0:T(8,128)(2,1)}, bf16[4,256,256]{2,1,0:T(8,128)(2,1)}, f32[32,2048]{1,0:T(8,128)}) custom-call(s32[2]{0:T(128)} %pad_add_fusion.place_ref, bf16[32,32,384]{2,1,0:T(8,128)(2,1)} %copy-done.10, bf16[32,48,128]{2,1,0:T(8,128)(2,1)} %copy-done.11, bf16[256,256]{1,0:T(8,128)(2,1)} %fusion.refs_2_, ...), custom_call_target="tpu_custom_call" | custom-call | tf_op jit(solution)/shard_map/classifier_forward/pallas_call | solution.py:464
  217.9 11.5 %all_to_all.30.parts_ref = f32[32,8,128]{2,1,0:T(8,128)} all-to-all(f32[32,8,128]{2,1,0:T(8,128)} %get-tuple-element.70), channel_id=1, replica_groups=mesh['parts'=1,'head'=32] {'head'}, dimensions={0} | all-to-all | bytes 262144 | tf_op jit(solution)/shard_map/all_to_all | solution.py:488
  229.5 8.4 %classifier_backward.1 = (bf16[8,32,2048]{2,1,0:T(8,128)(2,1)}, f32[8,128]{1,0:T(8,128)}) custom-call(f32[32,8,128]{2,1,0:T(8,128)} %all_to_all.30.parts_ref, f32[8,128]{1,0:T(8,128)} %broadcast_in_dim.17.counts_ref, f32[1,128]{1,0:T(1,128)} %bitcast.18, f32[8,128]{1,0:T(8,128)} %fusion.10.target_ref, f32[32,8]{1,0:T(8,128)} %constant.61.clone.spread_ref, ...), custom_call_target="tpu_custom_call" | custom-call | tf_op jit(solution)/shard_map/classifier_backward/pallas_call | solution.py:489
  237.9 4.4 %all-to-all-start.5 = ((bf16[8,32,2048]{2,1,0:T(8,128)(2,1)}), bf16[8,32,2048]{2,1,0:T(8,128)(2,1)}, u32[]{:S(2)}, u32[]{:S(2)}) async-start(bf16[8,32,2048]{2,1,0:T(8,128)(2,1)} %get-tuple-element.77), calls=%async_computation.5 | async-start | bytes 2097152 | tf_op jit(solution)/shard_map/all_to_all | solution.py:508
  243.2 0.8 broadcast_multiply_fusion.dy_ref
  244.0 24.6 %all-to-all-done.5.dn_ref = bf16[8,32,2048]{2,1,0:T(8,128)(2,1)} async-done(((bf16[8,32,2048]{2,1,0:T(8,128)(2,1)}), bf16[8,32,2048]{2,1,0:T(8,128)(2,1)}, u32[]{:S(2)}, u32[]{:S(2)}) %all-to-all-start.5) | async-done | bytes 1048608 | tf_op jit(solution)/shard_map/all_to_all | solution.py:508
  268.7 2.4 norm_backward.1
  (82 shorter events, 5.5 us)
Async XLA Ops:
  0.6 15.7 %copy-start = (bf16[256,4096]{1,0:T(8,128)(2,1)S(1)}, bf16[256,4096]{1,0:T(8,128)(2,1)}, u32[]{:S(2)}) copy-start(bf16[256,4096]{1,0:T(8,128)(2,1)} %param.24) | copy-start | bytes 6291460
  5.4 7.4 %copy-start.17 = (s32[8]{0:T(128)S(1)}, s32[8]{0:T(128)}, u32[]{:S(2)}) copy-start(s32[8]{0:T(128)} %count_ref.3) | copy-start | bytes 100
  5.4 116.9 %all-to-all-start.1 = ((bf16[32,64,1152]{2,1,0:T(8,128)(2,1)}), bf16[32,64,1152]{2,1,0:T(8,128)(2,1)}, u32[]{:S(2)}, u32[]{:S(2)}) async-start(bf16[32,64,1152]{2,1,0:T(8,128)(2,1)} %bitcast.14), calls=%async_computation.1 | async-start | bytes 9437184 | tf_op jit(solution)/shard_map/all_to_all | solution.py:392
  12.9 3.3 %copy-start.23 = (s32[8]{0:T(128)S(1)}, s32[8]{0:T(128)}, u32[]{:S(2)}) copy-start(s32[8]{0:T(128)} %param.22) | copy-start | bytes 100
  16.3 3.8 %copy-start.1 = (bf16[2048,128]{1,0:T(8,128)(2,1)S(1)}, bf16[2048,128]{1,0:T(8,128)(2,1)}, u32[]{:S(2)}) copy-start(bf16[2048,128]{1,0:T(8,128)(2,1)} %refs_7_) | copy-start | bytes 1572868
  16.7 5.1 %copy-start.21 = (s32[128]{0:T(128)S(1)}, s32[128]{0:T(128)}, u32[]{:S(2)}) copy-start(s32[128]{0:T(128)} %constant.59.clone) | copy-start | bytes 1540
  18.7 4.7 %copy-start.4 = (bf16[2048,256]{1,0:T(8,128)(2,1)S(1)}, bf16[2048,256]{1,0:T(8,128)(2,1)}, u32[]{:S(2)}) copy-start(bf16[2048,256]{1,0:T(8,128)(2,1)} %refs_1_) | copy-start | bytes 3145732
  18.7 6.4 %copy-start.3 = (bf16[2048,256]{1,0:T(8,128)(2,1)S(1)}, bf16[2048,256]{1,0:T(8,128)(2,1)}, u32[]{:S(2)}) copy-start(bf16[2048,256]{1,0:T(8,128)(2,1)} %refs_0_) | copy-start | bytes 3145732
  21.8 142.7 %copy-start.12 = (f32[256,128]{1,0:T(8,128)}, f32[256,128]{1,0:T(8,128)S(1)}, u32[]{:S(2)}) copy-start(f32[256,128]{1,0:T(8,128)S(1)} %fusion.13.refs_10_.refs_2_) | copy-start | bytes 393220
  23.4 59.6 %collective-permute-start.4 = (bf16[2048,256]{1,0:T(8,128)(2,1)S(1)}, bf16[2048,256]{1,0:T(8,128)(2,1)S(1)}, u32[]{:S(2)}, u32[]{:S(2)}) collective-permute-start(bf16[2048,256]{1,0:T(8,128)(2,1)S(1)} %copy-done.4), channel_id=1, source_target_pairs={{0,2},{1,3},{2,0},{3,1},{4,6},{5,7},{6,4},{7,5},{8,10},{9,11},{10,... | collective-permute-start | bytes 3145736 | tf_op jit(solution)/shard_map/ppermute | solution.py:380
  25.1 86.2 %collective-permute-start.1 = (bf16[2048,256]{1,0:T(8,128)(2,1)S(1)}, bf16[2048,256]{1,0:T(8,128)(2,1)S(1)}, u32[]{:S(2)}, u32[]{:S(2)}) collective-permute-start(bf16[2048,256]{1,0:T(8,128)(2,1)S(1)} %copy-done.3), channel_id=1, source_target_pairs={{0,2},{1,3},{2,0},{3,1},{4,6},{5,7},{6,4},{7,5},{8,10},{9,11},{10,... | collective-permute-start | bytes 3145736 | tf_op jit(solution)/shard_map/ppermute | solution.py:380
  25.4 94.5 %collective-permute-start.3 = (bf16[2048,256]{1,0:T(8,128)(2,1)S(1)}, bf16[2048,256]{1,0:T(8,128)(2,1)S(1)}, u32[]{:S(2)}, u32[]{:S(2)}) collective-permute-start(bf16[2048,256]{1,0:T(8,128)(2,1)S(1)} %copy-done.4), channel_id=1, source_target_pairs={{0,1},{1,0},{2,3},{3,2},{4,5},{5,4},{6,7},{7,6},{8,9},{9,8},{10,11... | collective-permute-start | bytes 3145736 | tf_op jit(solution)/shard_map/ppermute | solution.py:380
  25.4 94.5 %collective-permute-start = (bf16[2048,256]{1,0:T(8,128)(2,1)S(1)}, bf16[2048,256]{1,0:T(8,128)(2,1)S(1)}, u32[]{:S(2)}, u32[]{:S(2)}) collective-permute-start(bf16[2048,256]{1,0:T(8,128)(2,1)S(1)} %copy-done.3), channel_id=1, source_target_pairs={{0,1},{1,0},{2,3},{3,2},{4,5},{5,4},{6,7},{7,6},{8,9},{9,8},{10,11... | collective-permute-start | bytes 3145736 | tf_op jit(solution)/shard_map/ppermute | solution.py:380
  83.0 36.9 %copy-start.5 = (bf16[2048,256]{1,0:T(8,128)(2,1)}, bf16[2048,256]{1,0:T(8,128)(2,1)S(1)}, u32[]{:S(2)}) copy-start(bf16[2048,256]{1,0:T(8,128)(2,1)S(1)} %collective-permute-done.4.refs_15_.refs_7_) | copy-start | bytes 3145732
  83.0 37.0 %collective-permute-start.5 = (bf16[2048,256]{1,0:T(8,128)(2,1)S(1)}, bf16[2048,256]{1,0:T(8,128)(2,1)S(1)}, u32[]{:S(2)}, u32[]{:S(2)}) collective-permute-start(bf16[2048,256]{1,0:T(8,128)(2,1)S(1)} %collective-permute-done.4.refs_15_.refs_7_), channel_id=1, source_target_pairs={{0,1},{1,0},{2,3},{3,2},{4,5},{5,4},{6,7},{7,6},{8,9},{9,8},{10,11... | collective-permute-start | bytes 3145736 | tf_op jit(solution)/shard_map/ppermute | solution.py:380
  111.3 8.7 %copy-start.6 = (bf16[2048,256]{1,0:T(8,128)(2,1)}, bf16[2048,256]{1,0:T(8,128)(2,1)S(1)}, u32[]{:S(2)}) copy-start(bf16[2048,256]{1,0:T(8,128)(2,1)S(1)} %collective-permute-done.1.refs_14_.refs_6_) | copy-start | bytes 3145732
  111.3 11.1 %collective-permute-start.2 = (bf16[2048,256]{1,0:T(8,128)(2,1)S(1)}, bf16[2048,256]{1,0:T(8,128)(2,1)}, u32[]{:S(2)}, u32[]{:S(2)}) collective-permute-start(bf16[2048,256]{1,0:T(8,128)(2,1)S(1)} %collective-permute-done.1.refs_14_.refs_6_), channel_id=1, source_target_pairs={{0,1},{1,0},{2,3},{3,2},{4,5},{5,4},{6,7},{7,6},{8,9},{9,8},{10,11... | collective-permute-start | bytes 3145736 | tf_op jit(solution)/shard_map/ppermute | solution.py:380
  111.3 5.9 %collective-permute-start.7 = (f32[256,128]{1,0:T(8,128)S(1)}, f32[256,128]{1,0:T(8,128)S(1)}, u32[]{:S(2)}, u32[]{:S(2)}) collective-permute-start(f32[256,128]{1,0:T(8,128)S(1)} %fusion.13.refs_10_.refs_2_), channel_id=1, source_target_pairs={{0,2},{1,3},{2,0},{3,1},{4,6},{5,7},{6,4},{7,5},{8,10},{9,11},{10,... | collective-permute-start | bytes 393224 | tf_op jit(solution)/shard_map/ppermute | solution.py:380
  117.2 47.3 %copy-start.13 = (f32[256,128]{1,0:T(8,128)}, f32[256,128]{1,0:T(8,128)S(1)}, u32[]{:S(2)}) copy-start(f32[256,128]{1,0:T(8,128)S(1)} %collective-permute-done.7.refs_16_.refs_8_) | copy-start | bytes 393220
  117.2 1.3 collective-permute-start.6
  118.5 45.9 %copy-start.14 = (f32[256,128]{1,0:T(8,128)}, f32[256,128]{1,0:T(8,128)S(1)}, u32[]{:S(2)}) copy-start(f32[256,128]{1,0:T(8,128)S(1)} %collective-permute-done.6.refs_13_.refs_5_) | copy-start | bytes 393220
  118.5 1.3 collective-permute-start.8
  119.9 44.6 %copy-start.15 = (f32[256,128]{1,0:T(8,128)}, f32[256,128]{1,0:T(8,128)S(1)}, u32[]{:S(2)}) copy-start(f32[256,128]{1,0:T(8,128)S(1)} %collective-permute-done.8.refs_19_.refs_11_) | copy-start | bytes 393220
  122.4 43.2 %all-to-all-start = ((bf16[32,64,384]{2,1,0:T(8,128)(2,1)}), bf16[32,64,384]{2,1,0:T(8,128)(2,1)}, u32[]{:S(2)}, u32[]{:S(2)}) async-start(bf16[32,64,384]{2,1,0:T(8,128)(2,1)} %bitcast.15), calls=%async_computation | async-start | bytes 3145728 | tf_op jit(solution)/shard_map/all_to_all | solution.py:392
  165.6 25.1 %all-to-all-start.2 = ((bf16[32,32,384]{2,1,0:T(8,128)(2,1)}), bf16[32,32,384]{2,1,0:T(8,128)(2,1)S(1)}, u32[]{:S(2)}, u32[]{:S(2)}) async-start(bf16[32,32,384]{2,1,0:T(8,128)(2,1)} %get-tuple-element.49), calls=%async_computation.2 | async-start | bytes 1572864 | tf_op jit(solution)/shard_map/all_to_all | solution.py:451
  190.7 16.8 %copy-start.10 = (bf16[32,32,384]{2,1,0:T(8,128)(2,1)}, bf16[32,32,384]{2,1,0:T(8,128)(2,1)S(1)}, u32[]{:S(2)}) copy-start(bf16[32,32,384]{2,1,0:T(8,128)(2,1)S(1)} %all-to-all-done.2.refs_0_) | copy-start | bytes 2359300
  190.7 16.8 %all-to-all-start.3 = ((bf16[32,48,128]{2,1,0:T(8,128)(2,1)}), bf16[32,48,128]{2,1,0:T(8,128)(2,1)S(1)}, u32[]{:S(2)}, u32[]{:S(2)}) async-start(bf16[32,48,128]{2,1,0:T(8,128)(2,1)} %get-tuple-element.51), calls=%async_computation.3 | async-start | bytes 786432 | tf_op jit(solution)/shard_map/all_to_all | solution.py:451
  237.8 4.4 %copy-start.16 = (s32[8,64]{1,0:T(8,128)S(1)}, s32[8,64]{1,0:T(8,128)}, u32[]{:S(2)}) copy-start(s32[8,64]{1,0:T(8,128)} %slot_ref.3) | copy-start | bytes 6148
  237.8 4.4 %copy-start.18 = (s32[8]{0:T(128)S(1)}, s32[8]{0:T(128)}, u32[]{:S(2)}) copy-start(s32[8]{0:T(128)} %count_ref.3) | copy-start | bytes 100
  237.8 4.7 %copy-start.2 = (bf16[2048,128]{1,0:T(8,128)(2,1)S(1)}, bf16[2048,128]{1,0:T(8,128)(2,1)}, u32[]{:S(2)}) copy-start(bf16[2048,128]{1,0:T(8,128)(2,1)} %refs_7_) | copy-start | bytes 1572868
  237.9 4.7 %copy-start.19 = (f32[8,128]{1,0:T(8,128)S(1)}, f32[8,128]{1,0:T(8,128)}, u32[]{:S(2)}) copy-start(f32[8,128]{1,0:T(8,128)} %get-tuple-element.79) | copy-start | bytes 12292
  237.9 30.8 %all-to-all-start.5 = ((bf16[8,32,2048]{2,1,0:T(8,128)(2,1)}), bf16[8,32,2048]{2,1,0:T(8,128)(2,1)}, u32[]{:S(2)}, u32[]{:S(2)}) async-start(bf16[8,32,2048]{2,1,0:T(8,128)(2,1)} %get-tuple-element.77), calls=%async_computation.5 | async-start | bytes 2097152 | tf_op jit(solution)/shard_map/all_to_all | solution.py:508
  (6 other events, 9.8 us)

commit v5 on v4

--- a/solution.py
+++ b/solution.py
@@ -14,7 +14,7 @@
 LANES = 128
 MASKED = -1e30
 HEAD = 16
-TEAMS = 8
+TEAM = 8
 ABSENT = 64.0
 epsilon = 1e-06
 HIGH = lax.Precision.HIGHEST
@@ -190,9 +190,14 @@
     )(*operands)
 
 
+def split(x):
+    coarse = x.astype(jnp.bfloat16)
+    return coarse, (x - coarse.astype(jnp.float32)).astype(jnp.bfloat16)
+
+
 def forward_kernel(lanes, team, rows, place_ref, *refs):
     n = len(lanes)
-    inputs = n + 6 + 3 * team
+    inputs = n + 6 + 2 * team
     sources, (copies_ref, ga_out, aa_out, own_x_ref) = refs[:inputs], refs[inputs : inputs + 4]
     buffers = refs[inputs + 4 : 2 * inputs + 4]
     gathered, normed, counted, ga_ref, aa_ref, sems, out_sems = refs[2 * inputs + 4 :]
@@ -201,7 +206,7 @@
         for i, (source, buffer) in enumerate(zip(sources, buffers))
     ]
     first = n + 6
-    for copy in arriving[: first + 3]:
+    for copy in arriving[: first + 2]:
         copy.start()
 
     def get(i):
@@ -210,10 +215,10 @@
 
     def start_member(i):
         if i < team:
-            for copy in arriving[first + 3 * i : first + 3 * i + 3]:
+            for copy in arriving[first + 2 * i : first + 2 * i + 2]:
                 copy.start()
 
-    showers = copies_ref.shape[1]
+    showers, classes = copies_ref.shape[1:]
     group = buffers[0].shape[0] // showers
     width = gathered.shape[1]
     block = own_x_ref.shape[0]
@@ -258,14 +263,17 @@
     coef = cnt / counts_ref[...][:, :1]
     leaving = []
     for i in range(team):
-        gate_ref, up_ref, map_ref = [get(first + 3 * i + j) for j in range(3)]
+        gate_ref, up_ref = [get(first + 2 * i + j) for j in range(2)]
         start_member(i + 2)
         gate = mm(normed[...], gate_ref[...])
-        up = mm(normed[...], up_ref[...])
+        up = mm(normed[...], up_ref[:width])
         sigma = jax.nn.sigmoid(gate)
         activated = gate * sigma
         hidden = (activated * up).astype(jnp.bfloat16)
-        logits = logits + mm(mm(cnt_of, hidden, TN)[:showers], map_ref[...], precision=HIGH)
+        coarse, fine = split(mm(cnt_of, hidden, TN)[:showers])
+        both = mm(coarse, up_ref[width:], NT)
+        logits = logits + both[:, :classes] + both[:, classes:]
+        logits = logits + mm(fine, up_ref[width : width + classes], NT)
         ga_ref[i] = (coef * (up * sigma * (1.0 + gate * (1.0 - sigma)))).astype(jnp.bfloat16)
         aa_ref[i] = (coef * activated).astype(jnp.bfloat16)
         for j, (kept, out) in enumerate(((ga_ref, ga_out), (aa_ref, aa_out))):
@@ -279,18 +287,17 @@
 
 
 def backward_kernel(team, parts_ref, counts_ref, bias_ref, target_ref, spread_ref, *refs):
-    sources = refs[: 3 * team]
-    ga_in, aa_in, dn_ref, miss_ref = refs[3 * team : 3 * team + 4]
-    buffers = refs[3 * team + 4 : 6 * team + 4]
-    ga_ref, aa_ref, total, sems = refs[6 * team + 4 :]
+    sources = refs[: 2 * team]
+    ga_in, aa_in, dn_ref, miss_ref = refs[2 * team : 2 * team + 4]
+    buffers = refs[2 * team + 4 : 4 * team + 4]
+    ga_ref, aa_ref, total, sems = refs[4 * team + 4 :]
     arriving = []
     for i in range(team):
-        pairs = [(sources[3 * i + 2], buffers[3 * i + 2]), (ga_in.at[i], ga_ref.at[i])]
-        pairs += [(aa_in.at[i], aa_ref.at[i])]
-        pairs += [(sources[3 * i + j], buffers[3 * i + j]) for j in range(2)]
+        pairs = [(ga_in.at[i], ga_ref.at[i]), (aa_in.at[i], aa_ref.at[i])]
+        pairs += [(sources[2 * i + j], buffers[2 * i + j]) for j in range(2)]
         arriving.append(
             [
-                pltpu.make_async_copy(source, buffer, sems.at[5 * i + j])
+                pltpu.make_async_copy(source, buffer, sems.at[4 * i + j])
                 for j, (source, buffer) in enumerate(pairs)
             ]
         )
@@ -307,17 +314,20 @@
     exponent = jnp.exp(logits - jnp.max(logits, axis=1, keepdims=True))
     miss = target_ref[...] - exponent / jnp.sum(exponent, axis=1, keepdims=True)
     miss_ref[...] = miss
-    spread = mm(spread_ref[...], miss, precision=HIGH)
+    coarse, fine = split(mm(spread_ref[...], miss, precision=HIGH))
+    coarse = jnp.concatenate([coarse, coarse], axis=1)
+    classes = miss.shape[1]
+    width = dn_ref.shape[2]
     for i in range(team):
-        gate_ref, up_ref, map_ref = buffers[3 * i : 3 * i + 3]
+        gate_ref, up_ref = buffers[2 * i : 2 * i + 2]
         for copy in arriving[i]:
             copy.wait()
         start_member(i + 2)
-        wide = mm(spread, map_ref[...], NT, HIGH)
+        wide = mm(coarse, up_ref[width:]) + mm(fine, up_ref[width : width + classes])
         wide = jnp.concatenate([wide] * blocks, axis=0)
         gate_grad = (wide * ga_ref[i].astype(jnp.float32)).astype(jnp.bfloat16)
         up_grad = (wide * aa_ref[i].astype(jnp.float32)).astype(jnp.bfloat16)
-        term = mm(gate_grad, gate_ref[...], NT) + mm(up_grad, up_ref[...], NT)
+        term = mm(gate_grad, gate_ref[...], NT) + mm(up_grad, up_ref[:width], NT)
         if i == 0:
             total[...] = term
         elif i < team - 1:
@@ -364,8 +374,8 @@
     showers, local, width = queries.shape
     length = local * devices
     group = devices // showers
-    team = devices // TEAMS
-    outer = TEAMS
+    team = TEAM
+    outer = devices // team
     features = width // group
     slabs = features // LANES
     each = local // POOL
@@ -418,26 +428,35 @@
     heads_in = (spread_counts, class_bias.reshape(1, classes), target, spread)
     fixed = (perm, gain, scales, shifts)
     late = (row_counts, class_weight)
-    def gather(x):
+    def spread_out(x, bits):
         found = {0: x}
-        bit = team // 2
-        while bit:
+        for bit in bits:
             found.update({m ^ bit: swap(piece, bit) for m, piece in found.items()})
-            bit //= 2
+        return found
+
+    high, middle = team // 2, team // 4
+    rest = [1 << b for b in range(team.bit_length() - 3)][::-1]
+    class_map = mm(class_weight, down_weight, (((0,), (1,)), ((), ())))
+    coarse = lax.reduce_precision(class_map, exponent_bits=8, mantissa_bits=7)
+    parts = [x.astype(jnp.bfloat16) for x in (coarse, class_map - coarse)]
+    up_weight = jnp.concatenate([up_weight, *parts], axis=0)
+    sent = [pack(*tokens, *chunk, devices) for chunk in chunks[1:]]
+    sent, up_weight, fixed, late, heads_in, pool = lax.optimization_barrier(
+        (sent, up_weight, fixed, late, heads_in, pool)
+    )
+    gates = spread_out(gate_weight, [high, middle, *rest[:-1]])
+    ups = spread_out(up_weight, [middle, high, *rest[:-1]])
+    direct = [0, high, middle]
+    sent, near_gates, near_ups = lax.optimization_barrier(
+        (sent, [gates[m] for m in direct], [ups[m] for m in direct])
+    )
+    gates.update(zip(direct, near_gates))
+    ups.update(zip(direct, near_ups))
+    received += [exchange(x) for x in sent]
+
+    def spread_out_again(found):
+        found = {**found, **{m ^ 1: swap(piece, 1) for m, piece in found.items()}}
         return [found[m] for m in range(team)]
-
-    class_map = jnp.dot(down_weight, class_weight, preferred_element_type=jnp.float32)
-    sent = [pack(*tokens, *chunk, devices) for chunk in chunks[1:]]
-    sent, up_weight, class_map, fixed, late, heads_in, pool = lax.optimization_barrier(
-        (sent, up_weight, class_map, fixed, late, heads_in, pool)
-    )
-    class_map = gather(class_map)
-    gates = gather(gate_weight)
-    ups = gather(up_weight)
-    sent, gates, ups, class_map = lax.optimization_barrier(
-        (sent, gates, ups, class_map)
-    )
-    received += [exchange(x) for x in sent]
 
     attention = None
     pooled = []
@@ -448,6 +467,9 @@
         )
         if pooled:
             part, pooled[-1] = lax.optimization_barrier((part, pooled[-1]))
+        else:
+            part, gates, ups = lax.optimization_barrier((part, gates, ups))
+            gates, ups = spread_out_again(gates), spread_out_again(ups)
         pooled.append(lax.all_to_all(part, "head", 0, 0, tiled=True))
 
     units = gate_weight.shape[1]
@@ -455,7 +477,7 @@
     inside = pl.BlockSpec(memory_space=pltpu.VMEM)
     outside = pl.BlockSpec(memory_space=pl.ANY)
     side = jax.ShapeDtypeStruct((team, total, units), jnp.bfloat16)
-    members = [x for member in zip(gates, ups, class_map) for x in member]
+    members = [x for member in zip(gates, ups) for x in member]
     operands = [*pooled, *fixed, *late, *members]
 
     def buffers(xs):
@@ -498,7 +520,7 @@
             pltpu.VMEM(side.shape, side.dtype),
             pltpu.VMEM(side.shape, side.dtype),
             pltpu.VMEM((total, width), jnp.float32),
-            pltpu.SemaphoreType.DMA((5 * team,)),
+            pltpu.SemaphoreType.DMA((4 * team,)),
         ],
         compiler_params=pltpu.CompilerParams(vmem_limit_bytes=58 * MIB),
         name="classifier_backward",

time: 272 us -> 265 us (0.974); the launches traced: 271 us -> 261 us
  waiting for transfers between devices: 139 us -> 118 us
  starting transfers between devices: 28.8 us -> 34.6 us
  Pallas kernels: 78.5 us -> 82.9 us
    all_to_all x1, waiting for transfers between devices: 24.6 us -> 12.6 us  [body(): lax.all_to_all(grads, 'head', 0, 0, axis_index_groups=lines, tiled=True)]
    all_to_all x2, waiting for transfers between devices: 19.1 us -> 9.95 us  [body(): pooled.append(lax.all_to_all(part, 'head', 0, 0, tiled=True))]
    ppermute x9 -> x14, starting transfers between devices: 2.81 us -> 9.43 us  [swap(): return lax.ppermute(x, 'head', [(d, d ^ bit) for d in range(devices)])]
    ppermute x9 -> x14, waiting for transfers between devices: 93.7 us -> 91.8 us  [swap(): return lax.ppermute(x, 'head', [(d, d ^ bit) for d in range(devices)])]
  transfers between devices with their start and end apart: 14 -> 19, of which waited for: 9 -> 7; matrix products, arithmetic and copies ran while one was open for 3% -> 4% of each run, Pallas kernels for 20% -> 20%
where the time goes in v5:
time: 265 us; the launch traced here: 261 us
  waiting for transfers between devices  118 us (45%)
  Pallas kernels  82.9 us (31%)
  starting transfers between devices  34.6 us (13%)
  blocking collectives  11.5 us (4%)
  local copies, waits for them, and re-layouts  6.34 us (2%)
  other arithmetic  3.34 us (1%)
  matrix products  3.28 us (1%)
    ppermute x14, waiting for transfers between devices, swap(): return lax.ppermute(x, 'head', [(d, d ^ bit) for d in range(devices)])  91.8 us
    pallas_call x2, Pallas kernels, attend(): pl.pallas_call(functools.partial(attend_kernel, min(512, length), head),...  49.9 us
    all_to_all x1, waiting for transfers between devices, body(): lax.all_to_all(grads, 'head', 0, 0, axis_index_groups=lines, tiled=True)  12.6 us
    pallas_call x1, Pallas kernels, body(): pl.pallas_call(functools.partial(forward_kernel, [count * LANES for _, co...  11.8 us
    all_to_all x1, blocking collectives, body(): parts = lax.all_to_all(partial, 'head', 0, 0, tiled=True)  11.5 us
    all_to_all x2, starting transfers between devices, exchange(): got = lax.all_to_all(x, 'head', 0, 0, tiled=True)  11.1 us
    pallas_call x1, Pallas kernels, body(): pl.pallas_call(functools.partial(backward_kernel, team), out_shape=(jax.S...  10.9 us
    all_to_all x2, starting transfers between devices, body(): pooled.append(lax.all_to_all(part, 'head', 0, 0, tiled=True))  10.6 us
  transfers between devices with their start and end apart: 19, of which 7 were waited for; matrix products, arithmetic and copies ran while one was open for 4% of the time, Pallas kernels for 20%

profile of v5, /device:TPU:0, one launch (start us, length us, event | category | flops | bytes accessed | tf_op | source)
XLA Modules:
  0.0 261.1 jit_solution(3983412854578916930)
XLA Ops:
  0.6 4.8 %pack.3 = bf16[8,4,64,1152]{3,2,1,0:T(8,128)(2,1)} custom-call(s32[8,64]{1,0:T(8,128)} %slot_ref.3, s32[8]{0:T(128)} %count_ref.3, bf16[8,64,2048]{2,1,0:T(8,128)(2,1)} %q_ref.3, bf16[8,64,2048]{2,1,0:T(8,128)(2,1)} %k_ref.3, bf16[8,64,2048]{2,1,0:T(8,128)(2,1)} %v_ref.3), custom_call_target="tpu_custom_call" | custom-call | tf_op jit(solution)/shard_map/pack/pallas_call | solution.py:79
  5.4 7.4 %all-to-all-start.1 = ((bf16[32,64,1152]{2,1,0:T(8,128)(2,1)}), bf16[32,64,1152]{2,1,0:T(8,128)(2,1)}, u32[]{:S(2)}, u32[]{:S(2)}) async-start(bf16[32,64,1152]{2,1,0:T(8,128)(2,1)} %bitcast.14), calls=%async_computation.1 | async-start | bytes 9437184 | tf_op jit(solution)/shard_map/all_to_all | solution.py:402
  12.9 3.3 %pack.2 = bf16[8,4,64,384]{3,2,1,0:T(8,128)(2,1)} custom-call(s32[8,64]{1,0:T(8,128)} %slot_ref.3, s32[8]{0:T(128)} %count_ref.3, bf16[8,64,2048]{2,1,0:T(8,128)(2,1)} %q_ref.3, bf16[8,64,2048]{2,1,0:T(8,128)(2,1)} %k_ref.3, bf16[8,64,2048]{2,1,0:T(8,128)(2,1)} %v_ref.3), custom_call_target="tpu_custom_call" | custom-call | tf_op jit(solution)/shard_map/pack/pallas_call | solution.py:79
  17.1 0.8 reshape.112.refs_5_
  17.9 0.8 reshape.111.refs_4_.scale_ref
  20.1 1.7 reduce-precision_convert_fusion
  22.1 0.8 broadcast_in_dim.17.counts_ref
  23.0 0.7 broadcast_in_dim.16.refs_6_
  23.7 1.7 collective-permute-start.3
  25.4 1.5 collective-permute-start.2
  27.7 86.3 %collective-permute-done.refs_16_.refs_8_ = bf16[2048,256]{1,0:T(8,128)(2,1)} collective-permute-done((bf16[2048,256]{1,0:T(8,128)(2,1)}, bf16[2048,256]{1,0:T(8,128)(2,1)}, u32[]{:S(2)}, u32[]{:S(2)}) %collective-permute-start) | collective-permute-done | bytes 1048608 | tf_op jit(solution)/shard_map/ppermute | solution.py:390
  114.2 1.1 copy-done.2
  115.3 3.3 %all-to-all-done.1 = bf16[32,64,1152]{2,1,0:T(8,128)(2,1)} async-done(((bf16[32,64,1152]{2,1,0:T(8,128)(2,1)}), bf16[32,64,1152]{2,1,0:T(8,128)(2,1)}, u32[]{:S(2)}, u32[]{:S(2)}) %all-to-all-start.1) | async-done | bytes 4718624 | tf_op jit(solution)/shard_map/all_to_all | solution.py:402
  118.6 3.7 %all-to-all-start = ((bf16[32,64,384]{2,1,0:T(8,128)(2,1)}), bf16[32,64,384]{2,1,0:T(8,128)(2,1)}, u32[]{:S(2)}, u32[]{:S(2)}) async-start(bf16[32,64,384]{2,1,0:T(8,128)(2,1)} %bitcast.15), calls=%async_computation | async-start | bytes 3145728 | tf_op jit(solution)/shard_map/all_to_all | solution.py:402
  122.3 1.9 collective-permute-start.5
  124.3 1.5 collective-permute-start.4
  125.7 36.4 %attend.2 = (bf16[8,64,2048]{2,1,0:T(8,128)(2,1)}, bf16[32,16,384]{2,1,0:T(8,128)(2,1)}) custom-call(bf16[2048,1152]{1,0:T(8,128)(2,1)} %bitcast.5.q_ref.k_ref.v_ref, bf16[2048,1152]{1,0:T(8,128)(2,1)} %bitcast.5.q_ref.k_ref.v_ref, bf16[2048,1152]{1,0:T(8,128)(2,1)} %bitcast.5.q_ref.k_ref.v_ref, bf16[128,2048]{1,0:T(8,128)(2,1)S(1)} %compare_convert_fusion.pool_ref), custom_call_target="tpu_custom_call" | custom-call | flops 6442450944 | bytes 6291456 | tf_op jit(solution)/shard_map/attend/pallas_call | solution.py:170
  162.1 2.4 collective-permute-done.4.refs_20_.refs_12_
  164.5 2.9 %collective-permute-done.5.refs_21_.refs_13_ = bf16[2304,256]{1,0:T(8,128)(2,1)} collective-permute-done((bf16[2304,256]{1,0:T(8,128)(2,1)}, bf16[2304,256]{1,0:T(8,128)(2,1)}, u32[]{:S(2)}, u32[]{:S(2)}) %collective-permute-start.5) | collective-permute-done | bytes 1179680 | tf_op jit(solution)/shard_map/ppermute | solution.py:390
  167.9 4.8 %all-to-all-start.2 = ((bf16[32,16,384]{2,1,0:T(8,128)(2,1)}), bf16[32,16,384]{2,1,0:T(8,128)(2,1)S(1)}, u32[]{:S(2)}, u32[]{:S(2)}) async-start(bf16[32,16,384]{2,1,0:T(8,128)(2,1)} %get-tuple-element.57), calls=%async_computation.2 | async-start | bytes 786432 | tf_op jit(solution)/shard_map/all_to_all | solution.py:473
  174.2 13.6 %attend.3 = (bf16[8,64,2048]{2,1,0:T(8,128)(2,1)}, bf16[32,32,128]{2,1,0:T(8,128)(2,1)}) custom-call(bf16[2048,384]{1,0:T(8,128)(2,1)} %bitcast.3.q_ref.k_ref.v_ref, bf16[2048,384]{1,0:T(8,128)(2,1)} %bitcast.3.q_ref.k_ref.v_ref, bf16[2048,384]{1,0:T(8,128)(2,1)} %bitcast.3.q_ref.k_ref.v_ref, ...), custom_call_target="tpu_custom_call", output_to_operand_aliasing={{0}: (4, {})} | custom-call | flops 2147483648 | bytes 2097152 | tf_op jit(solution)/shard_map/attend/pallas_call | solution.py:170
  187.7 5.8 %all-to-all-start.3 = ((bf16[32,32,128]{2,1,0:T(8,128)(2,1)}), bf16[32,32,128]{2,1,0:T(8,128)(2,1)S(1)}, u32[]{:S(2)}, u32[]{:S(2)}) async-start(bf16[32,32,128]{2,1,0:T(8,128)(2,1)} %get-tuple-element.59), calls=%async_computation.3 | async-start | bytes 524288 | tf_op jit(solution)/shard_map/all_to_all | solution.py:473
  194.1 9.9 %all-to-all-done.3.refs_1_ = bf16[32,32,128]{2,1,0:T(8,128)(2,1)S(1)} async-done(((bf16[32,32,128]{2,1,0:T(8,128)(2,1)}), bf16[32,32,128]{2,1,0:T(8,128)(2,1)S(1)}, u32[]{:S(2)}, u32[]{:S(2)}) %all-to-all-start.3) | async-done | bytes 262176 | tf_op jit(solution)/shard_map/all_to_all | solution.py:473
  204.8 11.8 %classifier_forward.1 = (f32[32,8,128]{2,1,0:T(8,128)}, bf16[8,128,256]{2,1,0:T(8,128)(2,1)}, bf16[8,128,256]{2,1,0:T(8,128)(2,1)}, f32[32,2048]{1,0:T(8,128)}) custom-call(s32[2]{0:T(128)} %pad_add_fusion.place_ref, bf16[32,16,384]{2,1,0:T(8,128)(2,1)} %copy-done.6, bf16[32,32,128]{2,1,0:T(8,128)(2,1)} %copy-done.8, bf16[128,128]{1,0:T(8,128)(2,1)} %fusion.1.refs_2_, ...), custom_call_target="tpu_custom_call" | custom-call | tf_op jit(solution)/shard_map/classifier_forward/pallas_call | solution.py:486
  216.6 11.5 %all_to_all.30.parts_ref = f32[32,8,128]{2,1,0:T(8,128)} all-to-all(f32[32,8,128]{2,1,0:T(8,128)} %get-tuple-element.74), channel_id=1, replica_groups=mesh['parts'=1,'head'=32] {'head'}, dimensions={0} | all-to-all | bytes 262144 | tf_op jit(solution)/shard_map/all_to_all | solution.py:510
  228.1 10.9 %classifier_backward.1 = (bf16[4,32,2048]{2,1,0:T(8,128)(2,1)}, f32[8,128]{1,0:T(8,128)}) custom-call(f32[32,8,128]{2,1,0:T(8,128)} %all_to_all.30.parts_ref, f32[8,128]{1,0:T(8,128)} %broadcast_in_dim.17.counts_ref, f32[1,128]{1,0:T(1,128)} %bitcast.18, f32[8,128]{1,0:T(8,128)} %fusion.11.target_ref, f32[32,8]{1,0:T(8,128)} %constant.62.clone.spread_ref, ...), custom_call_target="tpu_custom_call" | custom-call | tf_op jit(solution)/shard_map/classifier_backward/pallas_call | solution.py:511
  239.0 3.5 %all-to-all-start.5 = ((bf16[4,32,2048]{2,1,0:T(8,128)(2,1)}), bf16[4,32,2048]{2,1,0:T(8,128)(2,1)S(1)}, u32[]{:S(2)}, u32[]{:S(2)}) async-start(bf16[4,32,2048]{2,1,0:T(8,128)(2,1)} %get-tuple-element.81), calls=%async_computation.5 | async-start | bytes 1048576 | tf_op jit(solution)/shard_map/all_to_all | solution.py:530
  242.8 1.2 fusion.14
  244.1 0.8 broadcast_multiply_fusion.dy_ref
  244.9 12.6 %all-to-all-done.5.dn_ref = bf16[4,32,2048]{2,1,0:T(8,128)(2,1)S(1)} async-done(((bf16[4,32,2048]{2,1,0:T(8,128)(2,1)}), bf16[4,32,2048]{2,1,0:T(8,128)(2,1)S(1)}, u32[]{:S(2)}, u32[]{:S(2)}) %all-to-all-start.5) | async-done | bytes 524320 | tf_op jit(solution)/shard_map/all_to_all | solution.py:530
  257.6 0.8 copy-done.5
  258.4 2.2 norm_backward.1
  (77 shorter events, 7.3 us)
Async XLA Ops:
  0.6 16.0 %copy-start = (bf16[256,4096]{1,0:T(8,128)(2,1)S(1)}, bf16[256,4096]{1,0:T(8,128)(2,1)}, u32[]{:S(2)}) copy-start(bf16[256,4096]{1,0:T(8,128)(2,1)} %param.24) | copy-start | bytes 6291460
  5.4 7.4 %copy-start.10 = (s32[8]{0:T(128)S(1)}, s32[8]{0:T(128)}, u32[]{:S(2)}) copy-start(s32[8]{0:T(128)} %count_ref.3) | copy-start | bytes 100
  5.4 113.1 %all-to-all-start.1 = ((bf16[32,64,1152]{2,1,0:T(8,128)(2,1)}), bf16[32,64,1152]{2,1,0:T(8,128)(2,1)}, u32[]{:S(2)}, u32[]{:S(2)}) async-start(bf16[32,64,1152]{2,1,0:T(8,128)(2,1)} %bitcast.14), calls=%async_computation.1 | async-start | bytes 9437184 | tf_op jit(solution)/shard_map/all_to_all | solution.py:402
  12.9 3.3 %copy-start.15 = (s32[8]{0:T(128)S(1)}, s32[8]{0:T(128)}, u32[]{:S(2)}) copy-start(s32[8]{0:T(128)} %param.22) | copy-start | bytes 100
  16.6 2.2 copy-start.14
  16.6 2.8 %copy-start.12 = (s32[128]{0:T(128)S(1)}, s32[128]{0:T(128)}, u32[]{:S(2)}) copy-start(s32[128]{0:T(128)} %constant.61.clone) | copy-start | bytes 1540
  16.6 3.5 %copy-start.3 = (bf16[2048,128]{1,0:T(8,128)(2,1)S(1)}, bf16[2048,128]{1,0:T(8,128)(2,1)}, u32[]{:S(2)}) copy-start(bf16[2048,128]{1,0:T(8,128)(2,1)} %refs_7_) | copy-start | bytes 1572868
  18.8 3.1 %copy-start.7 = (bf16[2048,256]{1,0:T(8,128)(2,1)S(1)}, bf16[2048,256]{1,0:T(8,128)(2,1)}, u32[]{:S(2)}) copy-start(bf16[2048,256]{1,0:T(8,128)(2,1)} %param.27) | copy-start | bytes 3145732
  18.8 3.2 %copy-start.13 = (s32[128]{0:T(128)S(1)}, s32[128]{0:T(128)}, u32[]{:S(2)}) copy-start(s32[128]{0:T(128)} %constant.60.clone) | copy-start | bytes 1540
  22.0 3.4 %copy-start.1 = (bf16[2304,256]{1,0:T(8,128)(2,1)}, bf16[2304,256]{1,0:T(8,128)(2,1)S(1)}, u32[]{:S(2)}) copy-start(bf16[2304,256]{1,0:T(8,128)(2,1)S(1)} %pad_maximum_fusion.refs_9_.refs_1_) | copy-start | bytes 3538948
  23.7 90.5 %collective-permute-start.3 = (bf16[2304,256]{1,0:T(8,128)(2,1)S(1)}, bf16[2304,256]{1,0:T(8,128)(2,1)S(1)}, u32[]{:S(2)}, u32[]{:S(2)}) collective-permute-start(bf16[2304,256]{1,0:T(8,128)(2,1)S(1)} %pad_maximum_fusion.refs_9_.refs_1_), channel_id=1, source_target_pairs={{0,2},{1,3},{2,0},{3,1},{4,6},{5,7},{6,4},{7,5},{8,10},{9,11},{10,... | collective-permute-start | bytes 3538952 | tf_op jit(solution)/shard_map/ppermute | solution.py:390
  25.4 89.9 %collective-permute-start.2 = (bf16[2304,256]{1,0:T(8,128)(2,1)S(1)}, bf16[2304,256]{1,0:T(8,128)(2,1)}, u32[]{:S(2)}, u32[]{:S(2)}) collective-permute-start(bf16[2304,256]{1,0:T(8,128)(2,1)S(1)} %pad_maximum_fusion.refs_9_.refs_1_), channel_id=1, source_target_pairs={{0,4},{1,5},{2,6},{3,7},{4,0},{5,1},{6,2},{7,3},{8,12},{9,13},{10,... | collective-permute-start | bytes 3538952 | tf_op jit(solution)/shard_map/ppermute | solution.py:390
  26.8 87.2 %collective-permute-start = (bf16[2048,256]{1,0:T(8,128)(2,1)}, bf16[2048,256]{1,0:T(8,128)(2,1)}, u32[]{:S(2)}, u32[]{:S(2)}) collective-permute-start(bf16[2048,256]{1,0:T(8,128)(2,1)} %refs_0_), channel_id=1, source_target_pairs={{0,4},{1,5},{2,6},{3,7},{4,0},{5,1},{6,2},{7,3},{8,12},{9,13},{10,... | collective-permute-start | bytes 3145736 | tf_op jit(solution)/shard_map/ppermute | solution.py:390
  27.4 86.8 %collective-permute-start.1 = (bf16[2048,256]{1,0:T(8,128)(2,1)}, bf16[2048,256]{1,0:T(8,128)(2,1)}, u32[]{:S(2)}, u32[]{:S(2)}) collective-permute-start(bf16[2048,256]{1,0:T(8,128)(2,1)} %refs_0_), channel_id=1, source_target_pairs={{0,2},{1,3},{2,0},{3,1},{4,6},{5,7},{6,4},{7,5},{8,10},{9,11},{10,... | collective-permute-start | bytes 3145736 | tf_op jit(solution)/shard_map/ppermute | solution.py:390
  118.6 49.3 %all-to-all-start = ((bf16[32,64,384]{2,1,0:T(8,128)(2,1)}), bf16[32,64,384]{2,1,0:T(8,128)(2,1)}, u32[]{:S(2)}, u32[]{:S(2)}) async-start(bf16[32,64,384]{2,1,0:T(8,128)(2,1)} %bitcast.15), calls=%async_computation | async-start | bytes 3145728 | tf_op jit(solution)/shard_map/all_to_all | solution.py:402
  122.3 45.1 %collective-permute-start.5 = (bf16[2304,256]{1,0:T(8,128)(2,1)}, bf16[2304,256]{1,0:T(8,128)(2,1)}, u32[]{:S(2)}, u32[]{:S(2)}) collective-permute-start(bf16[2304,256]{1,0:T(8,128)(2,1)} %copy-done.2), channel_id=1, source_target_pairs={{0,4},{1,5},{2,6},{3,7},{4,0},{5,1},{6,2},{7,3},{8,12},{9,13},{10,... | collective-permute-start | bytes 3538952 | tf_op jit(solution)/shard_map/ppermute | solution.py:390
  124.3 40.2 %collective-permute-start.4 = (bf16[2048,256]{1,0:T(8,128)(2,1)}, bf16[2048,256]{1,0:T(8,128)(2,1)}, u32[]{:S(2)}, u32[]{:S(2)}) collective-permute-start(bf16[2048,256]{1,0:T(8,128)(2,1)} %collective-permute-done.refs_16_.refs_8_), channel_id=1, source_target_pairs={{0,2},{1,3},{2,0},{3,1},{4,6},{5,7},{6,4},{7,5},{8,10},{9,11},{10,... | collective-permute-start | bytes 3145736 | tf_op jit(solution)/shard_map/ppermute | solution.py:390
  167.4 5.9 %collective-permute-start.6 = (bf16[2048,256]{1,0:T(8,128)(2,1)}, bf16[2048,256]{1,0:T(8,128)(2,1)}, u32[]{:S(2)}, u32[]{:S(2)}) collective-permute-start(bf16[2048,256]{1,0:T(8,128)(2,1)} %refs_0_), channel_id=1, source_target_pairs={{0,1},{1,0},{2,3},{3,2},{4,5},{5,4},{6,7},{7,6},{8,9},{9,8},{10,11... | collective-permute-start | bytes 3145736 | tf_op jit(solution)/shard_map/ppermute | solution.py:390
  167.4 6.3 %collective-permute-start.8 = (bf16[2048,256]{1,0:T(8,128)(2,1)}, bf16[2048,256]{1,0:T(8,128)(2,1)}, u32[]{:S(2)}, u32[]{:S(2)}) collective-permute-start(bf16[2048,256]{1,0:T(8,128)(2,1)} %collective-permute-done.1.refs_12_.refs_4_), channel_id=1, source_target_pairs={{0,1},{1,0},{2,3},{3,2},{4,5},{5,4},{6,7},{7,6},{8,9},{9,8},{10,11... | collective-permute-start | bytes 3145736 | tf_op jit(solution)/shard_map/ppermute | solution.py:390
  167.9 5.9 %collective-permute-start.10 = (bf16[2048,256]{1,0:T(8,128)(2,1)}, bf16[2048,256]{1,0:T(8,128)(2,1)}, u32[]{:S(2)}, u32[]{:S(2)}) collective-permute-start(bf16[2048,256]{1,0:T(8,128)(2,1)} %collective-permute-done.refs_16_.refs_8_), channel_id=1, source_target_pairs={{0,1},{1,0},{2,3},{3,2},{4,5},{5,4},{6,7},{7,6},{8,9},{9,8},{10,11... | collective-permute-start | bytes 3145736 | tf_op jit(solution)/shard_map/ppermute | solution.py:390
  167.9 19.8 %all-to-all-start.2 = ((bf16[32,16,384]{2,1,0:T(8,128)(2,1)}), bf16[32,16,384]{2,1,0:T(8,128)(2,1)S(1)}, u32[]{:S(2)}, u32[]{:S(2)}) async-start(bf16[32,16,384]{2,1,0:T(8,128)(2,1)} %get-tuple-element.57), calls=%async_computation.2 | async-start | bytes 786432 | tf_op jit(solution)/shard_map/all_to_all | solution.py:473
  172.7 21.4 %collective-permute-start.7 = (bf16[2304,256]{1,0:T(8,128)(2,1)}, bf16[2304,256]{1,0:T(8,128)(2,1)}, u32[]{:S(2)}, u32[]{:S(2)}) collective-permute-start(bf16[2304,256]{1,0:T(8,128)(2,1)} %copy-done.1), channel_id=1, source_target_pairs={{0,1},{1,0},{2,3},{3,2},{4,5},{5,4},{6,7},{7,6},{8,9},{9,8},{10,11... | collective-permute-start | bytes 3538952 | tf_op jit(solution)/shard_map/ppermute | solution.py:390
  173.1 21.0 %collective-permute-start.9 = (bf16[2304,256]{1,0:T(8,128)(2,1)}, bf16[2304,256]{1,0:T(8,128)(2,1)}, u32[]{:S(2)}, u32[]{:S(2)}) collective-permute-start(bf16[2304,256]{1,0:T(8,128)(2,1)} %copy-done.2), channel_id=1, source_target_pairs={{0,1},{1,0},{2,3},{3,2},{4,5},{5,4},{6,7},{7,6},{8,9},{9,8},{10,11... | collective-permute-start | bytes 3538952 | tf_op jit(solution)/shard_map/ppermute | solution.py:390
  173.3 20.8 %collective-permute-start.11 = (bf16[2304,256]{1,0:T(8,128)(2,1)}, bf16[2304,256]{1,0:T(8,128)(2,1)}, u32[]{:S(2)}, u32[]{:S(2)}) collective-permute-start(bf16[2304,256]{1,0:T(8,128)(2,1)} %collective-permute-done.2.refs_17_.refs_9_), channel_id=1, source_target_pairs={{0,1},{1,0},{2,3},{3,2},{4,5},{5,4},{6,7},{7,6},{8,9},{9,8},{10,11... | collective-permute-start | bytes 3538952 | tf_op jit(solution)/shard_map/ppermute | solution.py:390
  173.7 20.5 %collective-permute-start.13 = (bf16[2304,256]{1,0:T(8,128)(2,1)}, bf16[2304,256]{1,0:T(8,128)(2,1)}, u32[]{:S(2)}, u32[]{:S(2)}) collective-permute-start(bf16[2304,256]{1,0:T(8,128)(2,1)} %collective-permute-done.5.refs_21_.refs_13_), channel_id=1, source_target_pairs={{0,1},{1,0},{2,3},{3,2},{4,5},{5,4},{6,7},{7,6},{8,9},{9,8},{10,11... | collective-permute-start | bytes 3538952 | tf_op jit(solution)/shard_map/ppermute | solution.py:390
  173.8 20.3 %collective-permute-start.12 = (bf16[2048,256]{1,0:T(8,128)(2,1)}, bf16[2048,256]{1,0:T(8,128)(2,1)}, u32[]{:S(2)}, u32[]{:S(2)}) collective-permute-start(bf16[2048,256]{1,0:T(8,128)(2,1)} %collective-permute-done.4.refs_20_.refs_12_), channel_id=1, source_target_pairs={{0,1},{1,0},{2,3},{3,2},{4,5},{5,4},{6,7},{7,6},{8,9},{9,8},{10,11... | collective-permute-start | bytes 3145736 | tf_op jit(solution)/shard_map/ppermute | solution.py:390
  187.7 16.4 %copy-start.6 = (bf16[32,16,384]{2,1,0:T(8,128)(2,1)}, bf16[32,16,384]{2,1,0:T(8,128)(2,1)S(1)}, u32[]{:S(2)}) copy-start(bf16[32,16,384]{2,1,0:T(8,128)(2,1)S(1)} %all-to-all-done.2.refs_0_) | copy-start | bytes 1179652
  187.7 16.4 %all-to-all-start.3 = ((bf16[32,32,128]{2,1,0:T(8,128)(2,1)}), bf16[32,32,128]{2,1,0:T(8,128)(2,1)S(1)}, u32[]{:S(2)}, u32[]{:S(2)}) async-start(bf16[32,32,128]{2,1,0:T(8,128)(2,1)} %get-tuple-element.59), calls=%async_computation.3 | async-start | bytes 524288 | tf_op jit(solution)/shard_map/all_to_all | solution.py:473
  228.1 14.4 %copy-start.9 = (s32[8,64]{1,0:T(8,128)S(1)}, s32[8,64]{1,0:T(8,128)}, u32[]{:S(2)}) copy-start(s32[8,64]{1,0:T(8,128)} %slot_ref.3) | copy-start | bytes 6148
  228.1 14.4 %copy-start.11 = (s32[8]{0:T(128)S(1)}, s32[8]{0:T(128)}, u32[]{:S(2)}) copy-start(s32[8]{0:T(128)} %count_ref.3) | copy-start | bytes 100
  228.1 14.6 %copy-start.4 = (bf16[2048,128]{1,0:T(8,128)(2,1)S(1)}, bf16[2048,128]{1,0:T(8,128)(2,1)}, u32[]{:S(2)}) copy-start(bf16[2048,128]{1,0:T(8,128)(2,1)} %refs_7_) | copy-start | bytes 1572868
  239.0 18.6 %all-to-all-start.5 = ((bf16[4,32,2048]{2,1,0:T(8,128)(2,1)}), bf16[4,32,2048]{2,1,0:T(8,128)(2,1)S(1)}, u32[]{:S(2)}, u32[]{:S(2)}) async-start(bf16[4,32,2048]{2,1,0:T(8,128)(2,1)} %get-tuple-element.81), calls=%async_computation.5 | async-start | bytes 1048576 | tf_op jit(solution)/shard_map/all_to_all | solution.py:530
  (3 other events, 2.6 us)

commit v6 on v5

--- a/solution.py
+++ b/solution.py
@@ -107,20 +107,26 @@
     keys = k_ref[...]
     rows = v_ref[...]
     one = jnp.ones_like(rows)
-    present = jnp.where(keys.astype(jnp.float32) < 0.5 * ABSENT, 1.0, 0.0).astype(jnp.bfloat16)
+    wide_keys = keys.astype(jnp.float32)
+    present = jnp.where(wide_keys < 0.5 * ABSENT, 1.0, 0.0).astype(jnp.bfloat16)
     pick = jnp.broadcast_to(jnp.where(lane == 0, 1.0, 0.0).astype(jnp.bfloat16), (8, LANES))
     valid = mm(pick, present, NT)[:1]
-    bias = jnp.where(valid > 0.5, 0.0, MASKED)
+    marked = jnp.where(wide_keys < 0.5 * ABSENT, 0.0, MASKED)
+    marked_keys = (
+        jnp.where(low, wide_keys, jnp.where(lane == half, marked, 0.0)).astype(jnp.bfloat16),
+        jnp.where(low, jnp.where(lane == 0, marked, 0.0), wide_keys).astype(jnp.bfloat16),
+    )
+    marks = [jnp.where(lane == at, 1.0, 0.0).astype(jnp.bfloat16) for at in (half, 0)]
     values = (jnp.where(low, rows, one), jnp.where(low, one, rows))
 
     for i in range(length // block):
         at = slice(i * block, (i + 1) * block)
         query = q_ref[at, :] * jnp.asarray(0.125, jnp.bfloat16)
-        zero = jnp.zeros_like(query)
         outs = []
         for h in range(2):
-            own = jnp.where(low, query, zero) if h == 0 else jnp.where(low, zero, query)
-            scores = mm(own, keys, NT) + bias
+            mark = jnp.broadcast_to(marks[h], query.shape)
+            own = jnp.where(low, query, mark) if h == 0 else jnp.where(low, mark, query)
+            scores = mm(own, marked_keys[h], NT)
             peak = jnp.max(scores, axis=1, keepdims=True)
             weights = jnp.exp(scores - peak).astype(jnp.bfloat16)
             outs.append(mm(weights, values[h]))
@@ -262,24 +268,33 @@
     logits = mm(sums, class_ref[...].astype(jnp.float32), precision=HIGH)
     coef = cnt / counts_ref[...][:, :1]
     leaving = []
-    for i in range(team):
-        gate_ref, up_ref = [get(first + 2 * i + j) for j in range(2)]
-        start_member(i + 2)
-        gate = mm(normed[...], gate_ref[...])
-        up = mm(normed[...], up_ref[:width])
+
+    def finish(i, gate, up, logits):
+        up_ref = buffers[first + 2 * i + 1]
         sigma = jax.nn.sigmoid(gate)
         activated = gate * sigma
         hidden = (activated * up).astype(jnp.bfloat16)
-        coarse, fine = split(mm(cnt_of, hidden, TN)[:showers])
-        both = mm(coarse, up_ref[width:], NT)
-        logits = logits + both[:, :classes] + both[:, classes:]
-        logits = logits + mm(fine, up_ref[width : width + classes], NT)
         ga_ref[i] = (coef * (up * sigma * (1.0 + gate * (1.0 - sigma)))).astype(jnp.bfloat16)
         aa_ref[i] = (coef * activated).astype(jnp.bfloat16)
         for j, (kept, out) in enumerate(((ga_ref, ga_out), (aa_ref, aa_out))):
             copy = pltpu.make_async_copy(kept.at[i], out.at[i], out_sems.at[2 * i + j])
             copy.start()
             leaving.append(copy)
+        coarse, fine = split(mm(cnt_of, hidden, TN)[:showers])
+        both = mm(coarse, up_ref[width:], NT)
+        logits = logits + both[:, :classes] + both[:, classes:]
+        return logits + mm(fine, up_ref[width : width + classes], NT)
+
+    before = None
+    for i in range(team):
+        gate_ref, up_ref = [get(first + 2 * i + j) for j in range(2)]
+        start_member(i + 2)
+        gate = mm(normed[...], gate_ref[...])
+        up = mm(normed[...], up_ref[:width])
+        if before is not None:
+            logits = finish(i - 1, *before, logits)
+        before = (gate, up)
+    logits = finish(team - 1, *before, logits)
     for d in range(copies_ref.shape[0]):
         copies_ref[d] = logits
     for copy in leaving:
@@ -454,10 +469,10 @@
     ups.update(zip(direct, near_ups))
     received += [exchange(x) for x in sent]
 
-    def spread_out_again(found):
-        found = {**found, **{m ^ 1: swap(piece, 1) for m, piece in found.items()}}
-        return [found[m] for m in range(team)]
-
+    def cross(found, members):
+        found.update({m ^ 1: swap(found[m], 1) for m in members})
+
+    far = [m for m in gates if m not in direct]
     attention = None
     pooled = []
     for qkv, (first, count) in zip(received, chunks):
@@ -467,9 +482,22 @@
         )
         if pooled:
             part, pooled[-1] = lax.optimization_barrier((part, pooled[-1]))
-        else:
-            part, gates, ups = lax.optimization_barrier((part, gates, ups))
-            gates, ups = spread_out_again(gates), spread_out_again(ups)
+        if not pooled:
+            _, near_gates, near_ups = lax.optimization_barrier(
+                (part, [gates[m] for m in direct], [ups[m] for m in direct])
+            )
+            gates.update(zip(direct, near_gates))
+            ups.update(zip(direct, near_ups))
+            cross(gates, direct)
+            cross(ups, direct)
+        if first + count == slabs:
+            _, far_gates, far_ups = lax.optimization_barrier(
+                (part, [gates[m] for m in far], [ups[m] for m in far])
+            )
+            gates.update(zip(far, far_gates))
+            ups.update(zip(far, far_ups))
+            cross(gates, far)
+            cross(ups, far)
         pooled.append(lax.all_to_all(part, "head", 0, 0, tiled=True))
 
     units = gate_weight.shape[1]
@@ -477,7 +505,7 @@
     inside = pl.BlockSpec(memory_space=pltpu.VMEM)
     outside = pl.BlockSpec(memory_space=pl.ANY)
     side = jax.ShapeDtypeStruct((team, total, units), jnp.bfloat16)
-    members = [x for member in zip(gates, ups) for x in member]
+    members = [x for m in range(team) for x in (gates[m], ups[m])]
     operands = [*pooled, *fixed, *late, *members]
 
     def buffers(xs):

time: 265 us -> 252 us (0.951); the launches traced: 261 us -> 251 us
  waiting for transfers between devices: 118 us -> 112 us
  Pallas kernels: 82.9 us -> 79.5 us
    ppermute x14, waiting for transfers between devices: 91.8 us -> 86.6 us  [swap(): return lax.ppermute(x, 'head', [(d, d ^ bit) for d in range(devices)])]
    pallas_call x2, Pallas kernels: 49.9 us -> 47.1 us  [attend(): pl.pallas_call(functools.partial(attend_kernel, min(512, length), head),...]
  transfers between devices with their start and end apart: 19 -> 19, of which waited for: 7 -> 5; matrix products, arithmetic and copies ran while one was open for 4% -> 4% of each run, Pallas kernels for 20% -> 20%
where the time goes in v6:
time: 252 us; the launch traced here: 251 us
  waiting for transfers between devices  112 us (44%)
  Pallas kernels  79.5 us (32%)
  starting transfers between devices  33.3 us (13%)
  blocking collectives  11.5 us (5%)
  local copies, waits for them, and re-layouts  7.05 us (3%)
  other arithmetic  3.37 us (1%)
  matrix products  3.28 us (1%)
    ppermute x14, waiting for transfers between devices, swap(): return lax.ppermute(x, 'head', [(d, d ^ bit) for d in range(devices)])  86.6 us
    pallas_call x2, Pallas kernels, attend(): pl.pallas_call(functools.partial(attend_kernel, min(512, length), head),...  47.1 us
    all_to_all x1, waiting for transfers between devices, body(): lax.all_to_all(grads, 'head', 0, 0, axis_index_groups=lines, tiled=True)  12.6 us
    all_to_all x1, blocking collectives, body(): parts = lax.all_to_all(partial, 'head', 0, 0, tiled=True)  11.5 us
    pallas_call x1, Pallas kernels, body(): pl.pallas_call(functools.partial(forward_kernel, [count * LANES for _, co...  11.3 us
    all_to_all x2, starting transfers between devices, exchange(): got = lax.all_to_all(x, 'head', 0, 0, tiled=True)  11.2 us
    pallas_call x1, Pallas kernels, body(): pl.pallas_call(functools.partial(backward_kernel, team), out_shape=(jax.S...  10.8 us
    all_to_all x2, starting transfers between devices, body(): pooled.append(lax.all_to_all(part, 'head', 0, 0, tiled=True))  9.97 us
  transfers between devices with their start and end apart: 19, of which 5 were waited for; matrix products, arithmetic and copies ran while one was open for 4% of the time, Pallas kernels for 20%

profile of v6, /device:TPU:0, one launch (start us, length us, event | category | flops | bytes accessed | tf_op | source)
XLA Modules:
  0.0 251.3 jit_solution(6680094888807385050)
XLA Ops:
  0.6 4.8 %pack.3 = bf16[8,4,64,1152]{3,2,1,0:T(8,128)(2,1)} custom-call(s32[8,64]{1,0:T(8,128)} %slot_ref.3, s32[8]{0:T(128)} %count_ref.3, bf16[8,64,2048]{2,1,0:T(8,128)(2,1)} %q_ref.3, bf16[8,64,2048]{2,1,0:T(8,128)(2,1)} %k_ref.3, bf16[8,64,2048]{2,1,0:T(8,128)(2,1)} %v_ref.3), custom_call_target="tpu_custom_call" | custom-call | tf_op jit(solution)/shard_map/pack/pallas_call | solution.py:79
  5.5 7.4 %all-to-all-start.1 = ((bf16[32,64,1152]{2,1,0:T(8,128)(2,1)}), bf16[32,64,1152]{2,1,0:T(8,128)(2,1)}, u32[]{:S(2)}, u32[]{:S(2)}) async-start(bf16[32,64,1152]{2,1,0:T(8,128)(2,1)} %bitcast.14), calls=%async_computation.1 | async-start | bytes 9437184 | tf_op jit(solution)/shard_map/all_to_all | solution.py:417
  12.9 3.3 %pack.2 = bf16[8,4,64,384]{3,2,1,0:T(8,128)(2,1)} custom-call(s32[8,64]{1,0:T(8,128)} %slot_ref.3, s32[8]{0:T(128)} %count_ref.3, bf16[8,64,2048]{2,1,0:T(8,128)(2,1)} %q_ref.3, bf16[8,64,2048]{2,1,0:T(8,128)(2,1)} %k_ref.3, bf16[8,64,2048]{2,1,0:T(8,128)(2,1)} %v_ref.3), custom_call_target="tpu_custom_call" | custom-call | tf_op jit(solution)/shard_map/pack/pallas_call | solution.py:79
  17.1 0.8 reshape.112.refs_5_
  17.9 0.8 reshape.111.refs_4_.scale_ref
  19.4 0.7 fusion.1.refs_2_
  20.1 1.7 reduce-precision_convert_fusion
  22.1 0.8 broadcast_in_dim.17.counts_ref
  22.9 0.7 broadcast_in_dim.16.refs_6_
  23.6 1.7 collective-permute-start.3
  25.3 1.5 collective-permute-start.2
  27.7 86.4 %collective-permute-done.refs_16_.refs_8_ = bf16[2048,256]{1,0:T(8,128)(2,1)} collective-permute-done((bf16[2048,256]{1,0:T(8,128)(2,1)}, bf16[2048,256]{1,0:T(8,128)(2,1)}, u32[]{:S(2)}, u32[]{:S(2)}) %collective-permute-start) | collective-permute-done | bytes 1048608 | tf_op jit(solution)/shard_map/ppermute | solution.py:405
  114.2 1.1 copy-done.2
  115.3 3.3 %all-to-all-done.1 = bf16[32,64,1152]{2,1,0:T(8,128)(2,1)} async-done(((bf16[32,64,1152]{2,1,0:T(8,128)(2,1)}), bf16[32,64,1152]{2,1,0:T(8,128)(2,1)}, u32[]{:S(2)}, u32[]{:S(2)}) %all-to-all-start.1) | async-done | bytes 4718624 | tf_op jit(solution)/shard_map/all_to_all | solution.py:417
  118.6 3.7 %all-to-all-start = ((bf16[32,64,384]{2,1,0:T(8,128)(2,1)}), bf16[32,64,384]{2,1,0:T(8,128)(2,1)}, u32[]{:S(2)}, u32[]{:S(2)}) async-start(bf16[32,64,384]{2,1,0:T(8,128)(2,1)} %bitcast.15), calls=%async_computation | async-start | bytes 3145728 | tf_op jit(solution)/shard_map/all_to_all | solution.py:417
  122.3 1.6 collective-permute-start.10
  123.9 1.5 collective-permute-start.11
  125.4 34.2 %attend.2 = (bf16[8,64,2048]{2,1,0:T(8,128)(2,1)}, bf16[32,16,384]{2,1,0:T(8,128)(2,1)}) custom-call(bf16[2048,1152]{1,0:T(8,128)(2,1)} %bitcast.5.q_ref.k_ref.v_ref, bf16[2048,1152]{1,0:T(8,128)(2,1)} %bitcast.5.q_ref.k_ref.v_ref, bf16[2048,1152]{1,0:T(8,128)(2,1)} %bitcast.5.q_ref.k_ref.v_ref, bf16[128,2048]{1,0:T(8,128)(2,1)S(1)} %compare_convert_fusion.pool_ref), custom_call_target="tpu_custom_call" | custom-call | flops 6442450944 | bytes 6291456 | tf_op jit(solution)/shard_map/attend/pallas_call | solution.py:176
  160.2 4.0 %all-to-all-start.2 = ((bf16[32,16,384]{2,1,0:T(8,128)(2,1)}), bf16[32,16,384]{2,1,0:T(8,128)(2,1)S(1)}, u32[]{:S(2)}, u32[]{:S(2)}) async-start(bf16[32,16,384]{2,1,0:T(8,128)(2,1)} %get-tuple-element.49), calls=%async_computation.2 | async-start | bytes 786432 | tf_op jit(solution)/shard_map/all_to_all | solution.py:501
  164.2 12.9 %attend.3 = (bf16[8,64,2048]{2,1,0:T(8,128)(2,1)}, bf16[32,32,128]{2,1,0:T(8,128)(2,1)}) custom-call(bf16[2048,384]{1,0:T(8,128)(2,1)} %bitcast.3.q_ref.k_ref.v_ref, bf16[2048,384]{1,0:T(8,128)(2,1)} %bitcast.3.q_ref.k_ref.v_ref, bf16[2048,384]{1,0:T(8,128)(2,1)} %bitcast.3.q_ref.k_ref.v_ref, ...), custom_call_target="tpu_custom_call", output_to_operand_aliasing={{0}: (4, {})} | custom-call | flops 2147483648 | bytes 2097152 | tf_op jit(solution)/shard_map/attend/pallas_call | solution.py:176
  177.2 0.7 copy-done.7
  179.0 5.9 %all-to-all-start.3 = ((bf16[32,32,128]{2,1,0:T(8,128)(2,1)}), bf16[32,32,128]{2,1,0:T(8,128)(2,1)S(1)}, u32[]{:S(2)}, u32[]{:S(2)}) async-start(bf16[32,32,128]{2,1,0:T(8,128)(2,1)} %get-tuple-element.51), calls=%async_computation.3 | async-start | bytes 524288 | tf_op jit(solution)/shard_map/all_to_all | solution.py:501
  185.7 9.6 %all-to-all-done.3.refs_1_ = bf16[32,32,128]{2,1,0:T(8,128)(2,1)S(1)} async-done(((bf16[32,32,128]{2,1,0:T(8,128)(2,1)}), bf16[32,32,128]{2,1,0:T(8,128)(2,1)S(1)}, u32[]{:S(2)}, u32[]{:S(2)}) %all-to-all-start.3) | async-done | bytes 262176 | tf_op jit(solution)/shard_map/all_to_all | solution.py:501
  196.0 11.3 %classifier_forward.1 = (f32[32,8,128]{2,1,0:T(8,128)}, bf16[8,128,256]{2,1,0:T(8,128)(2,1)}, bf16[8,128,256]{2,1,0:T(8,128)(2,1)}, f32[32,2048]{1,0:T(8,128)}) custom-call(s32[2]{0:T(128)} %pad_add_fusion.place_ref, bf16[32,16,384]{2,1,0:T(8,128)(2,1)} %copy-done.7, bf16[32,32,128]{2,1,0:T(8,128)(2,1)} %copy-done.9, bf16[128,128]{1,0:T(8,128)(2,1)} %fusion.1.refs_2_, ...), custom_call_target="tpu_custom_call" | custom-call | tf_op jit(solution)/shard_map/classifier_forward/pallas_call | solution.py:514
  207.3 11.5 %all_to_all.30.parts_ref = f32[32,8,128]{2,1,0:T(8,128)} all-to-all(f32[32,8,128]{2,1,0:T(8,128)} %get-tuple-element.72), channel_id=1, replica_groups=mesh['parts'=1,'head'=32] {'head'}, dimensions={0} | all-to-all | bytes 262144 | tf_op jit(solution)/shard_map/all_to_all | solution.py:538
  218.8 10.8 %classifier_backward.1 = (bf16[4,32,2048]{2,1,0:T(8,128)(2,1)}, f32[8,128]{1,0:T(8,128)}) custom-call(f32[32,8,128]{2,1,0:T(8,128)} %all_to_all.30.parts_ref, f32[8,128]{1,0:T(8,128)} %broadcast_in_dim.17.counts_ref, f32[1,128]{1,0:T(1,128)} %bitcast.18, f32[8,128]{1,0:T(8,128)} %fusion.11.target_ref, f32[32,8]{1,0:T(8,128)} %constant.62.clone.spread_ref, ...), custom_call_target="tpu_custom_call" | custom-call | tf_op jit(solution)/shard_map/classifier_backward/pallas_call | solution.py:539
  229.6 3.5 %all-to-all-start.5 = ((bf16[4,32,2048]{2,1,0:T(8,128)(2,1)}), bf16[4,32,2048]{2,1,0:T(8,128)(2,1)S(1)}, u32[]{:S(2)}, u32[]{:S(2)}) async-start(bf16[4,32,2048]{2,1,0:T(8,128)(2,1)} %get-tuple-element.79), calls=%async_computation.5 | async-start | bytes 1048576 | tf_op jit(solution)/shard_map/all_to_all | solution.py:558
  233.4 1.2 fusion.14
  234.8 0.8 broadcast_multiply_fusion.dy_ref
  235.6 12.6 %all-to-all-done.5.dn_ref = bf16[4,32,2048]{2,1,0:T(8,128)(2,1)S(1)} async-done(((bf16[4,32,2048]{2,1,0:T(8,128)(2,1)}), bf16[4,32,2048]{2,1,0:T(8,128)(2,1)S(1)}, u32[]{:S(2)}, u32[]{:S(2)}) %all-to-all-start.5) | async-done | bytes 524320 | tf_op jit(solution)/shard_map/all_to_all | solution.py:558
  248.2 0.8 copy-done.6
  249.0 2.2 norm_backward.1
  (79 shorter events, 6.3 us)
Async XLA Ops:
  0.6 16.0 %copy-start = (bf16[256,4096]{1,0:T(8,128)(2,1)S(1)}, bf16[256,4096]{1,0:T(8,128)(2,1)}, u32[]{:S(2)}) copy-start(bf16[256,4096]{1,0:T(8,128)(2,1)} %param.24) | copy-start | bytes 6291460
  5.5 7.4 %copy-start.11 = (s32[8]{0:T(128)S(1)}, s32[8]{0:T(128)}, u32[]{:S(2)}) copy-start(s32[8]{0:T(128)} %count_ref.3) | copy-start | bytes 100
  5.5 113.1 %all-to-all-start.1 = ((bf16[32,64,1152]{2,1,0:T(8,128)(2,1)}), bf16[32,64,1152]{2,1,0:T(8,128)(2,1)}, u32[]{:S(2)}, u32[]{:S(2)}) async-start(bf16[32,64,1152]{2,1,0:T(8,128)(2,1)} %bitcast.14), calls=%async_computation.1 | async-start | bytes 9437184 | tf_op jit(solution)/shard_map/all_to_all | solution.py:417
  12.9 3.3 %copy-start.16 = (s32[8]{0:T(128)S(1)}, s32[8]{0:T(128)}, u32[]{:S(2)}) copy-start(s32[8]{0:T(128)} %param.22) | copy-start | bytes 100
  16.6 2.2 copy-start.15
  16.6 2.8 %copy-start.13 = (s32[128]{0:T(128)S(1)}, s32[128]{0:T(128)}, u32[]{:S(2)}) copy-start(s32[128]{0:T(128)} %constant.61.clone) | copy-start | bytes 1540
  16.6 3.5 %copy-start.4 = (bf16[2048,128]{1,0:T(8,128)(2,1)S(1)}, bf16[2048,128]{1,0:T(8,128)(2,1)}, u32[]{:S(2)}) copy-start(bf16[2048,128]{1,0:T(8,128)(2,1)} %refs_7_) | copy-start | bytes 1572868
  18.7 3.1 %copy-start.8 = (bf16[2048,256]{1,0:T(8,128)(2,1)S(1)}, bf16[2048,256]{1,0:T(8,128)(2,1)}, u32[]{:S(2)}) copy-start(bf16[2048,256]{1,0:T(8,128)(2,1)} %param.27) | copy-start | bytes 3145732
  18.7 3.2 %copy-start.14 = (s32[128]{0:T(128)S(1)}, s32[128]{0:T(128)}, u32[]{:S(2)}) copy-start(s32[128]{0:T(128)} %constant.60.clone) | copy-start | bytes 1540
  21.9 3.4 %copy-start.1 = (bf16[2304,256]{1,0:T(8,128)(2,1)}, bf16[2304,256]{1,0:T(8,128)(2,1)S(1)}, u32[]{:S(2)}) copy-start(bf16[2304,256]{1,0:T(8,128)(2,1)S(1)} %pad_maximum_fusion.refs_9_.refs_1_) | copy-start | bytes 3538948
  23.6 90.6 %collective-permute-start.3 = (bf16[2304,256]{1,0:T(8,128)(2,1)S(1)}, bf16[2304,256]{1,0:T(8,128)(2,1)S(1)}, u32[]{:S(2)}, u32[]{:S(2)}) collective-permute-start(bf16[2304,256]{1,0:T(8,128)(2,1)S(1)} %pad_maximum_fusion.refs_9_.refs_1_), channel_id=1, source_target_pairs={{0,2},{1,3},{2,0},{3,1},{4,6},{5,7},{6,4},{7,5},{8,10},{9,11},{10,... | collective-permute-start | bytes 3538952 | tf_op jit(solution)/shard_map/ppermute | solution.py:405
  25.3 90.0 %collective-permute-start.2 = (bf16[2304,256]{1,0:T(8,128)(2,1)S(1)}, bf16[2304,256]{1,0:T(8,128)(2,1)}, u32[]{:S(2)}, u32[]{:S(2)}) collective-permute-start(bf16[2304,256]{1,0:T(8,128)(2,1)S(1)} %pad_maximum_fusion.refs_9_.refs_1_), channel_id=1, source_target_pairs={{0,4},{1,5},{2,6},{3,7},{4,0},{5,1},{6,2},{7,3},{8,12},{9,13},{10,... | collective-permute-start | bytes 3538952 | tf_op jit(solution)/shard_map/ppermute | solution.py:405
  26.8 87.3 %collective-permute-start = (bf16[2048,256]{1,0:T(8,128)(2,1)}, bf16[2048,256]{1,0:T(8,128)(2,1)}, u32[]{:S(2)}, u32[]{:S(2)}) collective-permute-start(bf16[2048,256]{1,0:T(8,128)(2,1)} %refs_0_), channel_id=1, source_target_pairs={{0,4},{1,5},{2,6},{3,7},{4,0},{5,1},{6,2},{7,3},{8,12},{9,13},{10,... | collective-permute-start | bytes 3145736 | tf_op jit(solution)/shard_map/ppermute | solution.py:405
  27.4 86.9 %collective-permute-start.1 = (bf16[2048,256]{1,0:T(8,128)(2,1)}, bf16[2048,256]{1,0:T(8,128)(2,1)}, u32[]{:S(2)}, u32[]{:S(2)}) collective-permute-start(bf16[2048,256]{1,0:T(8,128)(2,1)} %refs_0_), channel_id=1, source_target_pairs={{0,2},{1,3},{2,0},{3,1},{4,6},{5,7},{6,4},{7,5},{8,10},{9,11},{10,... | collective-permute-start | bytes 3145736 | tf_op jit(solution)/shard_map/ppermute | solution.py:405
  118.6 41.6 %all-to-all-start = ((bf16[32,64,384]{2,1,0:T(8,128)(2,1)}), bf16[32,64,384]{2,1,0:T(8,128)(2,1)}, u32[]{:S(2)}, u32[]{:S(2)}) async-start(bf16[32,64,384]{2,1,0:T(8,128)(2,1)} %bitcast.15), calls=%async_computation | async-start | bytes 3145728 | tf_op jit(solution)/shard_map/all_to_all | solution.py:417
  122.3 55.6 %collective-permute-start.10 = (bf16[2048,256]{1,0:T(8,128)(2,1)}, bf16[2048,256]{1,0:T(8,128)(2,1)}, u32[]{:S(2)}, u32[]{:S(2)}) collective-permute-start(bf16[2048,256]{1,0:T(8,128)(2,1)} %collective-permute-done.refs_16_.refs_8_), channel_id=1, source_target_pairs={{0,2},{1,3},{2,0},{3,1},{4,6},{5,7},{6,4},{7,5},{8,10},{9,11},{10,... | collective-permute-start | bytes 3145736 | tf_op jit(solution)/shard_map/ppermute | solution.py:405
  123.9 54.0 %collective-permute-start.11 = (bf16[2304,256]{1,0:T(8,128)(2,1)}, bf16[2304,256]{1,0:T(8,128)(2,1)}, u32[]{:S(2)}, u32[]{:S(2)}) collective-permute-start(bf16[2304,256]{1,0:T(8,128)(2,1)} %copy-done.2), channel_id=1, source_target_pairs={{0,4},{1,5},{2,6},{3,7},{4,0},{5,1},{6,2},{7,3},{8,12},{9,13},{10,... | collective-permute-start | bytes 3538952 | tf_op jit(solution)/shard_map/ppermute | solution.py:405
  159.6 18.8 %collective-permute-start.4 = (bf16[2048,256]{1,0:T(8,128)(2,1)}, bf16[2048,256]{1,0:T(8,128)(2,1)}, u32[]{:S(2)}, u32[]{:S(2)}) collective-permute-start(bf16[2048,256]{1,0:T(8,128)(2,1)} %refs_0_), channel_id=1, source_target_pairs={{0,1},{1,0},{2,3},{3,2},{4,5},{5,4},{6,7},{7,6},{8,9},{9,8},{10,11... | collective-permute-start | bytes 3145736 | tf_op jit(solution)/shard_map/ppermute | solution.py:405
  159.6 18.9 %collective-permute-start.6 = (bf16[2048,256]{1,0:T(8,128)(2,1)}, bf16[2048,256]{1,0:T(8,128)(2,1)}, u32[]{:S(2)}, u32[]{:S(2)}) collective-permute-start(bf16[2048,256]{1,0:T(8,128)(2,1)} %collective-permute-done.1.refs_12_.refs_4_), channel_id=1, source_target_pairs={{0,1},{1,0},{2,3},{3,2},{4,5},{5,4},{6,7},{7,6},{8,9},{9,8},{10,11... | collective-permute-start | bytes 3145736 | tf_op jit(solution)/shard_map/ppermute | solution.py:405
  160.1 18.8 %collective-permute-start.8 = (bf16[2048,256]{1,0:T(8,128)(2,1)}, bf16[2048,256]{1,0:T(8,128)(2,1)}, u32[]{:S(2)}, u32[]{:S(2)}) collective-permute-start(bf16[2048,256]{1,0:T(8,128)(2,1)} %collective-permute-done.refs_16_.refs_8_), channel_id=1, source_target_pairs={{0,1},{1,0},{2,3},{3,2},{4,5},{5,4},{6,7},{7,6},{8,9},{9,8},{10,11... | collective-permute-start | bytes 3145736 | tf_op jit(solution)/shard_map/ppermute | solution.py:405
  160.2 17.0 %all-to-all-start.2 = ((bf16[32,16,384]{2,1,0:T(8,128)(2,1)}), bf16[32,16,384]{2,1,0:T(8,128)(2,1)S(1)}, u32[]{:S(2)}, u32[]{:S(2)}) async-start(bf16[32,16,384]{2,1,0:T(8,128)(2,1)} %get-tuple-element.49), calls=%async_computation.2 | async-start | bytes 786432 | tf_op jit(solution)/shard_map/all_to_all | solution.py:501
  177.9 7.7 %collective-permute-start.5 = (bf16[2304,256]{1,0:T(8,128)(2,1)}, bf16[2304,256]{1,0:T(8,128)(2,1)S(1)}, u32[]{:S(2)}, u32[]{:S(2)}) collective-permute-start(bf16[2304,256]{1,0:T(8,128)(2,1)} %copy-done.1), channel_id=1, source_target_pairs={{0,1},{1,0},{2,3},{3,2},{4,5},{5,4},{6,7},{7,6},{8,9},{9,8},{10,11... | collective-permute-start | bytes 3538952 | tf_op jit(solution)/shard_map/ppermute | solution.py:405
  177.9 7.7 %collective-permute-start.7 = (bf16[2304,256]{1,0:T(8,128)(2,1)}, bf16[2304,256]{1,0:T(8,128)(2,1)}, u32[]{:S(2)}, u32[]{:S(2)}) collective-permute-start(bf16[2304,256]{1,0:T(8,128)(2,1)} %copy-done.2), channel_id=1, source_target_pairs={{0,1},{1,0},{2,3},{3,2},{4,5},{5,4},{6,7},{7,6},{8,9},{9,8},{10,11... | collective-permute-start | bytes 3538952 | tf_op jit(solution)/shard_map/ppermute | solution.py:405
  178.4 7.2 %collective-permute-start.9 = (bf16[2304,256]{1,0:T(8,128)(2,1)}, bf16[2304,256]{1,0:T(8,128)(2,1)}, u32[]{:S(2)}, u32[]{:S(2)}) collective-permute-start(bf16[2304,256]{1,0:T(8,128)(2,1)} %collective-permute-done.2.refs_17_.refs_9_), channel_id=1, source_target_pairs={{0,1},{1,0},{2,3},{3,2},{4,5},{5,4},{6,7},{7,6},{8,9},{9,8},{10,11... | collective-permute-start | bytes 3538952 | tf_op jit(solution)/shard_map/ppermute | solution.py:405
  178.5 16.8 %collective-permute-start.13 = (bf16[2304,256]{1,0:T(8,128)(2,1)}, bf16[2304,256]{1,0:T(8,128)(2,1)}, u32[]{:S(2)}, u32[]{:S(2)}) collective-permute-start(bf16[2304,256]{1,0:T(8,128)(2,1)} %collective-permute-done.11.refs_21_.refs_13_), channel_id=1, source_target_pairs={{0,1},{1,0},{2,3},{3,2},{4,5},{5,4},{6,7},{7,6},{8,9},{9,8},{10,11... | collective-permute-start | bytes 3538952 | tf_op jit(solution)/shard_map/ppermute | solution.py:405
  179.0 16.3 %collective-permute-start.12 = (bf16[2048,256]{1,0:T(8,128)(2,1)}, bf16[2048,256]{1,0:T(8,128)(2,1)}, u32[]{:S(2)}, u32[]{:S(2)}) collective-permute-start(bf16[2048,256]{1,0:T(8,128)(2,1)} %collective-permute-done.10.refs_20_.refs_12_), channel_id=1, source_target_pairs={{0,1},{1,0},{2,3},{3,2},{4,5},{5,4},{6,7},{7,6},{8,9},{9,8},{10,11... | collective-permute-start | bytes 3145736 | tf_op jit(solution)/shard_map/ppermute | solution.py:405
  179.0 16.3 %all-to-all-start.3 = ((bf16[32,32,128]{2,1,0:T(8,128)(2,1)}), bf16[32,32,128]{2,1,0:T(8,128)(2,1)S(1)}, u32[]{:S(2)}, u32[]{:S(2)}) async-start(bf16[32,32,128]{2,1,0:T(8,128)(2,1)} %get-tuple-element.51), calls=%async_computation.3 | async-start | bytes 524288 | tf_op jit(solution)/shard_map/all_to_all | solution.py:501
  185.6 9.7 %copy-start.3 = (bf16[2304,256]{1,0:T(8,128)(2,1)}, bf16[2304,256]{1,0:T(8,128)(2,1)S(1)}, u32[]{:S(2)}) copy-start(bf16[2304,256]{1,0:T(8,128)(2,1)S(1)} %collective-permute-done.5.refs_11_.refs_3_) | copy-start | bytes 3538948
  218.8 14.3 %copy-start.10 = (s32[8,64]{1,0:T(8,128)S(1)}, s32[8,64]{1,0:T(8,128)}, u32[]{:S(2)}) copy-start(s32[8,64]{1,0:T(8,128)} %slot_ref.3) | copy-start | bytes 6148
  218.8 14.4 %copy-start.12 = (s32[8]{0:T(128)S(1)}, s32[8]{0:T(128)}, u32[]{:S(2)}) copy-start(s32[8]{0:T(128)} %count_ref.3) | copy-start | bytes 100
  218.8 14.6 %copy-start.5 = (bf16[2048,128]{1,0:T(8,128)(2,1)S(1)}, bf16[2048,128]{1,0:T(8,128)(2,1)}, u32[]{:S(2)}) copy-start(bf16[2048,128]{1,0:T(8,128)(2,1)} %refs_7_) | copy-start | bytes 1572868
  229.6 18.6 %all-to-all-start.5 = ((bf16[4,32,2048]{2,1,0:T(8,128)(2,1)}), bf16[4,32,2048]{2,1,0:T(8,128)(2,1)S(1)}, u32[]{:S(2)}, u32[]{:S(2)}) async-start(bf16[4,32,2048]{2,1,0:T(8,128)(2,1)} %get-tuple-element.79), calls=%async_computation.5 | async-start | bytes 1048576 | tf_op jit(solution)/shard_map/all_to_all | solution.py:558
  (4 other events, 3.3 us)
